TPU v7x, 512 devices: a whole 4x8x8 slice. The times are simulated.
512 devices in a mesh: seq: 64 (over x, z, core), mp: 8 (over y).
Axes of the slice: x: 4, y: 8, z: 8, core: 2. Of those that a mesh axis runs over, the one named last changes fastest.
Arguments:
- queries: bfloat16 [32768, 2048], P('seq', 'mp'), may hold values from -30 to 30
- stretch_kv: bfloat16 [32768, 1792], P(('seq', 'mp')), may hold values from -5 to 5
- pool: bfloat16 [512, 64, 896], P('seq', 'mp'), may hold values from -20 to 20
- neighbour_owner: int32 [512, 2], replicated, may hold values from 0 to 63, all different within a row; in each aligned block of 8 rows (0 to 7, 8 to 15, ...) at most 2 rows name the same one
- neighbour_slot: int32 [512, 2], replicated, may hold values from 0 to 7
- enc_query_weight: bfloat16 [896, 896], P('mp'), may hold values from -0.1875 to 0.1875
- dec_kv_weight: bfloat16 [896, 2, 2048], P(None, None, 'mp'), may hold values from -0.1875 to 0.1875
- out_cotangent: bfloat16 [32768, 2048], P('seq', 'mp'), may hold values from -5 to 5
Outputs:
- attended: bfloat16 [32768, 2048], P('seq', 'mp')
- grad_queries: bfloat16 [32768, 2048], P('seq', 'mp')
- grad_pool: float32 [512, 64, 896], P('seq', 'mp')
Inputs may be any that keep to these rules, and one draw needn't show every extreme that they name: `neighbour_owner`: the 8 stretches of one index of seq name one owner at most 2 times, a bound that some block reaches; the 2 neighbours of a stretch have different owners.
All inputs are finite; a program needn't handle non-finite values.
Results may differ from a plain program's by a relative error of at most 0.034.
Values may be sent and summed in bfloat16 or wider, within the bound.
No kernel may reach another device: no remote copies, remote signals or barrier semaphores. Data moves between devices by JAX's collectives and lax.ppermute only.
A program may use at most 64 MiB of HBM per device.

v0:
```python
import jax
import jax.numpy as jnp
from jax import lax
from jax.sharding import PartitionSpec as P

STRETCH_DEV = 8
STRETCH_LEN = 64
NEIGHBOURS = 2
CAP = 2
HEAD_DIM = 128


def encoder_parts(rows, context, weight):
    count, pair, span, width = rows.shape
    heads = width // HEAD_DIM
    query = jnp.dot(rows.reshape(-1, width), weight, preferred_element_type=jnp.float32).astype(
        jnp.bfloat16
    )
    query = query.reshape(count, pair, span, heads, HEAD_DIM)
    keys = context[:, :, :width].reshape(count, -1, heads, HEAD_DIM)
    values = context[:, :, width:].reshape(count, -1, heads, HEAD_DIM)
    scores = jnp.einsum(
        "cnthd,cshd->cnhts", query, keys, preferred_element_type=jnp.float32
    ) * HEAD_DIM ** (-0.5)
    weights = jax.nn.softmax(scores, axis=-1)
    return (weights, keys, values)


def encode(rows, context, weight):
    weights, keys, values = encoder_parts(rows, context, weight)
    mixed = jnp.einsum(
        "cnhts,cshd->cnthd",
        weights.astype(jnp.bfloat16),
        values,
        preferred_element_type=jnp.float32,
    )
    return (rows.astype(jnp.float32) + mixed.reshape(rows.shape)).astype(jnp.bfloat16)


def encode_back(rows, context, weight, grad_out):
    weights, keys, values = encoder_parts(rows, context, weight)
    count, pair, span, width = rows.shape
    heads = width // HEAD_DIM
    grad_heads = grad_out.reshape(count, pair, span, heads, HEAD_DIM)
    grad_w = jnp.einsum("cnthd,cshd->cnhts", grad_heads, values, preferred_element_type=jnp.float32)
    grad_s = (weights * (grad_w - jnp.sum(grad_w * weights, axis=-1, keepdims=True))).astype(
        jnp.bfloat16
    )
    grad_q = (
        jnp.einsum("cnhts,cshd->cnthd", grad_s, keys, preferred_element_type=jnp.float32)
        * HEAD_DIM ** (-0.5)
    ).astype(jnp.bfloat16)
    back = lax.dot_general(
        grad_q.reshape(-1, width),
        weight,
        (((1,), (1,)), ((), ())),
        preferred_element_type=jnp.float32,
    )
    return (grad_out.astype(jnp.float32) + back.reshape(rows.shape)).astype(jnp.bfloat16)


def shards(
    queries,
    stretch_kv,
    pool,
    neighbour_owner,
    neighbour_slot,
    enc_query_weight,
    dec_kv_weight,
    out_cotangent,
):
    seq_count = lax.axis_size("seq")
    here = lax.axis_index("seq")
    whole_weight = lax.all_gather(enc_query_weight, "mp", axis=0, tiled=True)
    requests = STRETCH_DEV * NEIGHBOURS
    span = pool.shape[1]
    width = pool.shape[2]
    stored = pool.shape[0]
    owners = neighbour_owner.reshape(seq_count, requests)
    slots = neighbour_slot.reshape(seq_count, requests)
    order = jnp.arange(requests)
    earlier = order[None, :] < order[:, None]
    same = owners[:, :, None] == owners[:, None, :]
    rank = jnp.sum(same & earlier[None], axis=2)
    picks = []
    flags = []
    for place in range(CAP):
        chosen = (owners == here) & (rank == place)
        picks.append(jnp.sum(jnp.where(chosen, slots, 0), axis=1))
        flags.append(jnp.any(chosen, axis=1))
    selected = jnp.stack(picks, axis=1).reshape(-1)
    usable = jnp.stack(flags, axis=1).reshape(-1)
    outgoing = jnp.take(pool, selected, axis=0)
    outgoing = jnp.where(usable[:, None, None], outgoing, jnp.zeros_like(outgoing))
    outgoing = outgoing.reshape(seq_count, CAP, span, width)
    arrived = lax.all_to_all(outgoing, "seq", split_axis=0, concat_axis=0, tiled=True)
    mine_owner = lax.dynamic_index_in_dim(owners, here, 0, keepdims=False)
    mine_rank = lax.dynamic_index_in_dim(rank, here, 0, keepdims=False)
    position = mine_owner * CAP + mine_rank
    rows = jnp.take(arrived.reshape(seq_count * CAP, span, width), position, axis=0)
    rows = rows.reshape(STRETCH_DEV, NEIGHBOURS, span, width)
    every_kv = lax.all_gather(stretch_kv, "mp", axis=0, tiled=True).reshape(
        STRETCH_DEV, STRETCH_LEN, 2 * width
    )
    encoded = encode(rows, every_kv, whole_weight)
    projected = jnp.einsum(
        "cnte,ekf->cntkf",
        lax.all_gather(encoded, "mp", axis=2, tiled=True),
        dec_kv_weight,
        preferred_element_type=jnp.float32,
    ).astype(jnp.bfloat16)
    local_width = queries.shape[1]
    heads = local_width // HEAD_DIM
    scale = HEAD_DIM ** (-0.5)
    keys = projected[:, :, :, 0, :].reshape(STRETCH_DEV, -1, heads, HEAD_DIM)
    values = projected[:, :, :, 1, :].reshape(STRETCH_DEV, -1, heads, HEAD_DIM)
    query = queries.reshape(STRETCH_DEV, STRETCH_LEN, heads, HEAD_DIM)
    scores = jnp.einsum("cqhd,ckhd->chqk", query, keys, preferred_element_type=jnp.float32) * scale
    weights = jax.nn.softmax(scores, axis=-1)
    weights_low = weights.astype(jnp.bfloat16)
    attended = jnp.einsum(
        "chqk,ckhd->cqhd", weights_low, values, preferred_element_type=jnp.float32
    )
    attended = attended.astype(jnp.bfloat16).reshape(-1, local_width)
    cotangent = out_cotangent.reshape(STRETCH_DEV, STRETCH_LEN, heads, HEAD_DIM)
    grad_v = jnp.einsum(
        "chqk,cqhd->ckhd", weights_low, cotangent, preferred_element_type=jnp.float32
    ).astype(jnp.bfloat16)
    grad_w = jnp.einsum("cqhd,ckhd->chqk", cotangent, values, preferred_element_type=jnp.float32)
    grad_s = (weights * (grad_w - jnp.sum(grad_w * weights, axis=-1, keepdims=True))).astype(
        jnp.bfloat16
    )
    grad_queries = (
        jnp.einsum("chqk,ckhd->cqhd", grad_s, keys, preferred_element_type=jnp.float32) * scale
    ).astype(jnp.bfloat16)
    grad_queries = grad_queries.reshape(-1, local_width)
    grad_k = (
        jnp.einsum("chqk,cqhd->ckhd", grad_s, query, preferred_element_type=jnp.float32) * scale
    ).astype(jnp.bfloat16)
    grad_kv = jnp.stack(
        (
            grad_k.reshape(STRETCH_DEV, NEIGHBOURS, -1, local_width),
            grad_v.reshape(STRETCH_DEV, NEIGHBOURS, -1, local_width),
        ),
        axis=3,
    )
    summed = lax.psum_scatter(
        jnp.einsum(
            "cntkf,ekf->tcne", grad_kv, dec_kv_weight, preferred_element_type=jnp.float32
        ).astype(jnp.bfloat16),
        "mp",
        scatter_dimension=0,
        tiled=True,
    )
    grad_encoded = summed.transpose(1, 2, 0, 3)
    grad_in = encode_back(rows, every_kv, whole_weight, grad_encoded)
    flat_grad = grad_in.reshape(requests, span * width)
    placing = (position[None, :] == jnp.arange(seq_count * CAP)[:, None]).astype(jnp.bfloat16)
    leaving = jnp.dot(placing, flat_grad, preferred_element_type=jnp.float32).astype(jnp.bfloat16)
    leaving = leaving.reshape(seq_count, CAP, span, width)
    returned = lax.all_to_all(leaving, "seq", split_axis=0, concat_axis=0, tiled=True)
    owner_rows = ((selected[None, :] == jnp.arange(stored)[:, None]) & usable[None, :]).astype(
        jnp.bfloat16
    )
    grad_pool = jnp.dot(
        owner_rows,
        returned.reshape(seq_count * CAP, span * width),
        preferred_element_type=jnp.float32,
    )
    return (attended, grad_queries, grad_pool.reshape(stored, span, width))


def solution(mesh):
    in_specs = (
        P("seq", "mp"),
        P(("seq", "mp"), None),
        P("seq", "mp", None),
        P(),
        P(),
        P("mp", None),
        P(None, None, "mp"),
        P("seq", "mp"),
    )
    out_specs = (P("seq", "mp"), P("seq", "mp"), P("seq", "mp", None))
    return jax.shard_map(shards, mesh=mesh, in_specs=in_specs, out_specs=out_specs, check_vma=False)
```

profile of v0, /device:TPU:1, one launch (start us, length us, event | category | flops | bytes accessed | tf_op | source)
XLA Modules:
  0.0 287.2 jit_solution(14224206698591718803)
XLA Ops:
  13.7 1.5 select_select_fusion
  15.2 15.0 %all-to-all-start = ((bf16[64,2,8,896]{3,2,1,0:T(8,128)(2,1)}), bf16[64,2,8,896]{3,2,1,0:T(8,128)(2,1)}, u32[]{:S(2)}, u32[]{:S(2)}) async-start(bf16[64,2,8,896]{3,2,1,0:T(8,128)(2,1)} %select_select_fusion), calls=%async_computation | async-start | bytes 3670016 | tf_op jit(solution)/shard_map/all_to_all | solution.py:96
  31.8 22.7 %all-gather.6.cloned.1.call-done = bf16[512,1792]{1,0:T(8,128)(2,1)} async-done(((bf16[64,1792]{1,0:T(8,128)(2,1)}), bf16[512,1792]{1,0:T(8,128)(2,1)}) %all-gather.6.cloned.1.call-update) | async-done | bytes 1835024 | tf_op jit(solution)/shard_map/all_gather | solution.py:102
  54.5 2.6 fusion.69
  57.1 2.1 reshape.198
  59.3 2.0 reshape.199
  61.3 14.3 %all-to-all-done = bf16[64,2,8,896]{3,2,1,0:T(8,128)(2,1)} async-done(((bf16[64,2,8,896]{3,2,1,0:T(8,128)(2,1)}), bf16[64,2,8,896]{3,2,1,0:T(8,128)(2,1)}, u32[]{:S(2)}, u32[]{:S(2)}) %all-to-all-start) | async-done | bytes 1835040 | tf_op jit(solution)/shard_map/all_to_all | solution.py:96
  75.5 2.1 gather_fusion.1
  77.6 20.8 %all-gather.4.cloned.1.call-done = bf16[896,896]{1,0:T(8,128)(2,1)} async-done(((bf16[112,896]{1,0:T(8,128)(2,1)}), bf16[896,896]{1,0:T(8,128)(2,1)}) %all-gather.4.cloned.1.call-update) | async-done | bytes 1605648 | tf_op jit(solution)/shard_map/all_gather | solution.py:74
  98.4 1.9 convolution_convert_fusion.3
  104.7 42.3 %all-gather.8.cloned.1.call-done = bf16[8,2,64,896]{3,2,1,0:T(8,128)(2,1)} async-done(((bf16[8,2,8,896]{3,2,1,0:T(8,128)(2,1)}), bf16[8,2,64,896]{3,2,1,0:T(8,128)(2,1)}) %all-gather.8.cloned.1.call-update) | async-done | bytes 1835024 | tf_op jit(solution)/shard_map/all_gather | solution.py:108
  147.0 2.7 fusion.7
  150.5 2.8 fusion.72
  153.4 3.1 %fusion.14 = bf16[8,128,2,128]{3,1,2,0:T(8,128)(2,1)} fusion(bf16[8,64,2,128]{3,2,1,0:T(2,128)(2,1)S(1)} %reshape.203, f32[8,2,64]{2,1,0:T(2,128)S(1)} %get-tuple-element.31, f32[8,2,64,128]{3,2,1,0:T(8,128)S(1)} %fusion.16), kind=kOutput, calls=%fused_computation.19 | convolution fusion | flops 34210944 | bytes 1314816 | tf_op jit(solution)/shard_map/chqk,cqhd->ckhd/dot_general | solution.py:126
  161.8 1.9 copy.201
  163.7 2.4 reshape.236
  166.0 41.5 %reduce-scatter.4.cloned.1.call-done = bf16[8,14336]{1,0:T(8,128)(2,1)} async-done(((bf16[64,14336]{1,0:T(8,128)(2,1)}), bf16[8,14336]{1,0:T(8,128)(2,1)}) %reduce-scatter.4.cloned.1.call-update) | async-done | bytes 229392
  207.6 1.7 multiply_reduce_fusion.1
  212.0 1.6 copy.206
  213.6 15.5 %all-to-all-start.1 = ((bf16[64,2,8,896]{3,2,1,0:T(8,128)(2,1)}), bf16[64,2,8,896]{3,2,1,0:T(8,128)(2,1)S(1)}, u32[]{:S(2)}, u32[]{:S(2)}) async-start(bf16[64,2,8,896]{3,2,1,0:T(8,128)(2,1)} %bitcast.126), calls=%async_computation.1 | async-start | bytes 3670016 | tf_op jit(solution)/shard_map/all_to_all | solution.py:161
  231.2 3.2 %fusion.27 = bf16[8,64,2,128]{3,1,2,0:T(8,128)(2,1)S(1)} fusion(bf16[8,128,2,128]{3,2,1,0:T(2,128)(2,1)} %copy-done.8, f32[8,2,64]{2,1,0:T(2,128)S(1)} %get-tuple-element.31, f32[8,2,64,128]{3,2,1,0:T(8,128)} %copy-done.5), kind=kOutput, calls=%fused_computation.37 | convolution fusion | flops 34079872 | bytes 1314816 | tf_op jit(solution)/shard_map/chqk,ckhd->cqhd/dot_general | solution.py:121
  235.5 39.0 %all-to-all-done.1 = bf16[64,2,8,896]{3,2,1,0:T(8,128)(2,1)S(1)} async-done(((bf16[64,2,8,896]{3,2,1,0:T(8,128)(2,1)}), bf16[64,2,8,896]{3,2,1,0:T(8,128)(2,1)S(1)}, u32[]{:S(2)}, u32[]{:S(2)}) %all-to-all-start.1) | async-done | bytes 1835040 | tf_op jit(solution)/shard_map/all_to_all | solution.py:161
  274.5 1.6 copy.207
  276.1 3.3 %copy.178 = bf16[128,7168]{0,1:T(8,128)(2,1)S(1)} copy(bf16[128,7168]{1,0:T(8,128)(2,1)} %bitcast.129) | data formatting | bytes 3670016 | tf_op jit(solution)/shard_map/reshape | solution.py:167
  (118 shorter events, 25.4 us)
Async XLA Ops:
  7.2 139.8 %copy-start = (bf16[896,2,256]{2,1,0:T(2,128)(2,1)S(1)}, bf16[896,2,256]{2,1,0:T(2,128)(2,1)}, u32[]{:S(2)}) copy-start(bf16[896,2,256]{2,1,0:T(2,128)(2,1)} %param.14) | copy-start | bytes 2752516
  7.2 5.6 %copy-start.1 = (bf16[8,8,896]{2,1,0:T(8,128)(2,1)S(1)}, bf16[8,8,896]{2,1,0:T(8,128)(2,1)}, u32[]{:S(2)}) copy-start(bf16[8,8,896]{2,1,0:T(8,128)(2,1)} %param.10) | copy-start | bytes 344068
  7.2 47.4 %all-gather.6.cloned.1.call-start = ((), (), s32[]{:S(2)}) async-start(), calls=%async_computation.4 | async-start | bytes 2064384 | tf_op jit(solution)/shard_map/all_gather | solution.py:102
  15.2 60.4 %all-to-all-start = ((bf16[64,2,8,896]{3,2,1,0:T(8,128)(2,1)}), bf16[64,2,8,896]{3,2,1,0:T(8,128)(2,1)}, u32[]{:S(2)}, u32[]{:S(2)}) async-start(bf16[64,2,8,896]{3,2,1,0:T(8,128)(2,1)} %select_select_fusion), calls=%async_computation | async-start | bytes 3670016 | tf_op jit(solution)/shard_map/all_to_all | solution.py:96
  30.2 68.2 %all-gather.4.cloned.1.call-start = ((), (), s32[]{:S(2)}) async-start(), calls=%async_computation.3 | async-start | bytes 1806336 | tf_op jit(solution)/shard_map/all_gather | solution.py:74
  31.0 116.0 %all-gather.8.cloned.1.call-start = ((), (), s32[]{:S(2)}) async-start(), calls=%async_computation.5 | async-start | bytes 2064384 | tf_op jit(solution)/shard_map/all_gather | solution.py:108
  59.2 41.1 %copy-start.3 = (bf16[8,64,7,128]{3,2,1,0:T(8,128)(2,1)}, bf16[8,64,7,128]{3,2,1,0:T(8,128)(2,1)S(1)}, u32[]{:S(2)}) copy-start(bf16[8,64,7,128]{3,2,1,0:T(8,128)(2,1)S(1)} %reshape.198) | copy-start | bytes 2752516
  77.6 24.3 %copy-start.6 = (bf16[8,64,7,128]{3,2,1,0:T(8,128)(2,1)S(1)}, bf16[8,64,7,128]{3,2,1,0:T(8,128)(2,1)}, u32[]{:S(2)}) copy-start(bf16[8,64,7,128]{3,2,1,0:T(8,128)(2,1)} %reshape.199) | copy-start | bytes 2752516
  101.9 2.4 copy-start.16
  101.9 2.6 copy-start.14
  101.9 2.7 copy-start.15
  104.3 103.3 %reduce-scatter.4.cloned.1.call-start = ((), (), s32[]{:S(2)}) async-start(), calls=%async_computation.6 | async-start | bytes 2064384
  150.1 6.4 %copy-start.8 = (bf16[8,128,2,128]{3,2,1,0:T(2,128)(2,1)}, bf16[8,128,2,128]{3,2,1,0:T(2,128)(2,1)S(1)}, u32[]{:S(2)}) copy-start(bf16[8,128,2,128]{3,2,1,0:T(2,128)(2,1)S(1)} %reshape_squeeze.6) | copy-start | bytes 1572868
  150.5 6.5 %copy-start.5 = (f32[8,2,64,128]{3,2,1,0:T(8,128)}, f32[8,2,64,128]{3,2,1,0:T(8,128)S(1)}, u32[]{:S(2)}) copy-start(f32[8,2,64,128]{3,2,1,0:T(8,128)S(1)} %fusion.16) | copy-start | bytes 1572868
  157.4 2.1 copy-start.9
  166.0 41.5 %copy-start.7 = (bf16[8,64,7,128]{3,2,1,0:T(8,128)(2,1)S(1)}, bf16[8,64,7,128]{3,2,1,0:T(8,128)(2,1)}, u32[]{:S(2)}) copy-start(bf16[8,64,7,128]{3,2,1,0:T(8,128)(2,1)} %reshape.199) | copy-start | bytes 2752516
  166.0 41.5 %copy-start.11 = (f32[8,2,7,8,64]{4,3,1,2,0:T(8,128)S(1)}, f32[8,2,7,8,64]{4,3,1,2,0:T(8,128)}, u32[]{:S(2)}) copy-start(f32[8,2,7,8,64]{4,3,1,2,0:T(8,128)} %get-tuple-element.30) | copy-start | bytes 688132
  166.0 41.5 %copy-start.17 = (f32[8,2,7,8]{3,1,2,0:T(2,128)S(1)}, f32[8,2,7,8]{3,1,2,0:T(2,128)}, u32[]{:S(2)}) copy-start(f32[8,2,7,8]{3,1,2,0:T(2,128)} %copy-done.16) | copy-start | bytes 10756
  207.6 1.7 copy-start.4
  209.3 1.4 copy-start.2
  209.3 1.4 copy-start.12
  209.8 1.6 copy-start.19
  213.6 60.9 %all-to-all-start.1 = ((bf16[64,2,8,896]{3,2,1,0:T(8,128)(2,1)}), bf16[64,2,8,896]{3,2,1,0:T(8,128)(2,1)S(1)}, u32[]{:S(2)}, u32[]{:S(2)}) async-start(bf16[64,2,8,896]{3,2,1,0:T(8,128)(2,1)} %bitcast.126), calls=%async_computation.1 | async-start | bytes 3670016 | tf_op jit(solution)/shard_map/all_to_all | solution.py:161
  276.1 3.3 %copy-start.20 = (pred[128]{0:T(512)(128)(4,1)S(1)}, pred[128]{0:T(512)(128)(4,1)}, u32[]{:S(2)}) copy-start(pred[128]{0:T(512)(128)(4,1)} %and.54) | copy-start | bytes 388
  (3 other events, 2.3 us)
Sparse Core Ops, SparseCore 0:
  10.1 44.3 all-gather.5
  56.6 41.7 all-gather.3
  104.4 42.5 all-gather.7
  166.2 41.3 reduce-scatter.3
where the time goes:
time: 288 us; the launch traced here: 287 us
  waiting for transfers between devices  182 us (63%)
  local copies, waits for them, and re-layouts  32.5 us (11%)
  starting transfers between devices  30.8 us (11%)
  matrix products  20.7 us (7%)
  between operations  14.3 us (5%)
  other arithmetic  6.83 us (2%)
    unnamed x5, waiting for transfers between devices  42.9 us
    all_gather x1, waiting for transfers between devices, shards(): lax.all_gather(encoded, 'mp', axis=2, tiled=True)  42.3 us
    all_to_all x1, waiting for transfers between devices, shards(): lax.all_to_all(leaving, 'seq', split_axis=0, concat_axis=0, tiled=True)  39 us
    all_gather x1, waiting for transfers between devices, shards(): lax.all_gather(stretch_kv, 'mp', axis=0, tiled=True)  22.7 us
    all_gather x1, waiting for transfers between devices, shards(): whole_weight = lax.all_gather(enc_query_weight, 'mp', axis=0, tiled=True)  20.8 us
    all_to_all x1, starting transfers between devices, shards(): lax.all_to_all(leaving, 'seq', split_axis=0, concat_axis=0, tiled=True)  15.5 us
    all_to_all x1, starting transfers between devices, shards(): lax.all_to_all(outgoing, 'seq', split_axis=0, concat_axis=0, tiled=True)  15 us
    all_to_all x1, waiting for transfers between devices, shards(): lax.all_to_all(outgoing, 'seq', split_axis=0, concat_axis=0, tiled=True)  14.3 us
  transfers between devices with their start and end apart: 6, of which 6 were waited for; matrix products, arithmetic and copies ran while one was open for 8% of the time, Pallas kernels for 0%

commit v1 on v0

v1 whole, which is shorter than its diff:
```python
import jax
import jax.numpy as jnp
from jax import lax
from jax.experimental import pallas as pl
from jax.experimental.pallas import tpu as pltpu
from jax.sharding import Mesh
from jax.sharding import PartitionSpec as P

HEAD_DIM = 128
SCALE = HEAD_DIM ** (-0.5)
SEQ = ("x", "z", "core")
NX, NZ, NC, NM = 4, 8, 2, 8
REQ = 16
SLOTS = 8
STRETCH = 64
SPAN = 8
WIDTH = 896
ENC_HEADS = 7
KV = 2 * HEAD_DIM
ENC_ROWS = 112
PACK = WIDTH + 2 * ENC_ROWS


def dot(a, b, dims):
    return lax.dot_general(a, b, ((dims[0], dims[1]), ((), ())), preferred_element_type=jnp.float32)


def softmax(scores):
    top = jnp.max(scores, axis=-1, keepdims=True)
    e = jnp.exp(scores - top)
    return e / jnp.sum(e, axis=-1, keepdims=True)


def softmax_back(weights, grad):
    return weights * (grad - jnp.sum(grad * weights, axis=-1, keepdims=True))


def stretch_kernel(
    core_ref,
    rows_ref,
    kv_ref,
    qg_ref,
    mine_ref,
    other_ref,
    out_ref,
    grad_ref,
    enc_w,
    dec_w,
    encoded_ref,
    heads_ref,
    probs_ref,
    total_ref,
    enc_sem,
    dec_sem,
):
    core = core_ref[0]
    enc_copies = []
    for source in range(2):
        ref = mine_ref if source == 0 else other_ref
        for m in range(NM):
            for pair in range(2):
                enc_copies.append(
                    pltpu.make_async_copy(
                        ref.at[m, pl.ds(WIDTH + pair * ENC_ROWS, ENC_ROWS), :],
                        enc_w.at[source, pl.ds(m * ENC_ROWS, ENC_ROWS), pl.ds(pair * KV, KV)],
                        enc_sem.at[source, m, pair],
                    )
                )
    for copy in enc_copies:
        copy.start()
    dec_copies = []
    for m in range(NM):
        pair = []
        for source in range(2):
            ref = mine_ref if source == 0 else other_ref
            head = core if source == 0 else 1 - core
            pair.append(
                pltpu.make_async_copy(
                    ref.at[m, pl.ds(0, WIDTH), :], dec_w.at[m, head], dec_sem.at[m, source]
                )
            )
        dec_copies.append(pair)
        for copy in pair:
            copy.start()
    for copy in enc_copies:
        copy.wait()

    rows = rows_ref[...]
    low = enc_w[core]
    high = enc_w[1 - core]
    weight = jnp.concatenate([low, high[:, 128:]], axis=1)
    query = dot(rows, weight, ((1,), (0,))).astype(jnp.bfloat16)
    for h in range(ENC_HEADS):
        cols = slice(h * HEAD_DIM, (h + 1) * HEAD_DIM)
        keys = kv_ref[:, cols]
        values = kv_ref[:, WIDTH + h * HEAD_DIM : WIDTH + (h + 1) * HEAD_DIM]
        weights = softmax(dot(query[:, cols], keys, ((1,), (1,))) * SCALE)
        probs_ref[h] = weights
        mixed = dot(weights.astype(jnp.bfloat16), values, ((1,), (0,)))
        encoded_ref[:, cols] = (rows[:, cols].astype(jnp.float32) + mixed).astype(jnp.bfloat16)
    encoded = encoded_ref[...]

    for m in range(NM):
        for copy in dec_copies[m]:
            copy.wait()
        for h in range(2):
            cols = slice(h * HEAD_DIM, (h + 1) * HEAD_DIM)
            both = dot(encoded, dec_w[m, h], ((1,), (0,))).astype(jnp.bfloat16)
            keys, values = both[:, :HEAD_DIM], both[:, HEAD_DIM:]
            q = qg_ref[m, :STRETCH, cols]
            g = qg_ref[m, STRETCH:, cols]
            weights = softmax(dot(q, keys, ((1,), (1,))) * SCALE)
            low_w = weights.astype(jnp.bfloat16)
            out_ref[m, :STRETCH, cols] = dot(low_w, values, ((1,), (0,))).astype(jnp.bfloat16)
            grad_s = softmax_back(weights, dot(g, values, ((1,), (1,)))).astype(jnp.bfloat16)
            out_ref[m, STRETCH:, cols] = (dot(grad_s, keys, ((1,), (0,))) * SCALE).astype(
                jnp.bfloat16
            )
            grad_v = dot(low_w, g, ((0,), (0,))).astype(jnp.bfloat16)
            grad_k = (dot(grad_s, q, ((0,), (0,))) * SCALE).astype(jnp.bfloat16)
            term = dot(jnp.concatenate([grad_k, grad_v], axis=1), dec_w[m, h], ((1,), (1,)))
            if m == 0 and h == 0:
                total_ref[...] = term
            else:
                total_ref[...] += term

    grad_encoded = total_ref[...].astype(jnp.bfloat16)
    for h in range(ENC_HEADS):
        cols = slice(h * HEAD_DIM, (h + 1) * HEAD_DIM)
        keys = kv_ref[:, cols]
        values = kv_ref[:, WIDTH + h * HEAD_DIM : WIDTH + (h + 1) * HEAD_DIM]
        grad_w = dot(grad_encoded[:, cols], values, ((1,), (1,)))
        grad_s = softmax_back(probs_ref[h], grad_w).astype(jnp.bfloat16)
        heads_ref[:, cols] = (dot(grad_s, keys, ((1,), (0,))) * SCALE).astype(jnp.bfloat16)
    back = dot(heads_ref[...], weight, ((1,), (1,)))
    grad_ref[...] = (grad_encoded.astype(jnp.float32) + back).astype(jnp.bfloat16)


def stretch_call(core, rows, kv, qg, mine, other):
    vmem = pl.BlockSpec(memory_space=pltpu.VMEM)
    hbm = pl.BlockSpec(memory_space=pl.ANY)
    return pl.pallas_call(
        stretch_kernel,
        out_shape=(
            jax.ShapeDtypeStruct((NM, 2 * STRETCH, KV), jnp.bfloat16),
            jax.ShapeDtypeStruct((2 * STRETCH, WIDTH), jnp.bfloat16),
        ),
        in_specs=[pl.BlockSpec(memory_space=pltpu.SMEM), vmem, vmem, vmem, hbm, hbm],
        out_specs=(vmem, vmem),
        scratch_shapes=[
            pltpu.VMEM((2, WIDTH, 2 * KV), jnp.bfloat16),
            pltpu.VMEM((NM, 2, WIDTH, KV), jnp.bfloat16),
            pltpu.VMEM((2 * STRETCH, WIDTH), jnp.bfloat16),
            pltpu.VMEM((2 * STRETCH, WIDTH), jnp.bfloat16),
            pltpu.VMEM((ENC_HEADS, 2 * STRETCH, STRETCH), jnp.float32),
            pltpu.VMEM((2 * STRETCH, WIDTH), jnp.float32),
            pltpu.SemaphoreType.DMA((2, NM, 2)),
            pltpu.SemaphoreType.DMA((NM, 2)),
        ],
        compiler_params=pltpu.CompilerParams(vmem_limit_bytes=24 * 1024 * 1024),
        cost_estimate=pl.CostEstimate(
            flops=7_000_000_000, bytes_accessed=11_000_000, transcendentals=200_000
        ),
        name="stretch",
    )(core, rows, kv, qg, mine, other)


def place_kernel(place_ref, mine_ref, other_ref, out_ref, total_ref):
    total_ref[...] = jnp.zeros_like(total_ref)
    for source in range(2):
        ref = mine_ref if source == 0 else other_ref

        def add(i, carry, ref=ref, source=source):
            at = place_ref[source, i]
            total_ref[at] += ref[i].astype(jnp.float32)
            return carry

        lax.fori_loop(0, NX * REQ, add, 0, unroll=4)
    out_ref[...] = total_ref[: NZ * SLOTS].astype(jnp.bfloat16)


def place_call(place, mine, other):
    vmem = pl.BlockSpec(memory_space=pltpu.VMEM)
    return pl.pallas_call(
        place_kernel,
        out_shape=jax.ShapeDtypeStruct((NZ * SLOTS, SPAN, WIDTH), jnp.bfloat16),
        in_specs=[pl.BlockSpec(memory_space=pltpu.SMEM), vmem, vmem],
        out_specs=vmem,
        scratch_shapes=[pltpu.VMEM((NZ * SLOTS + 1, SPAN, WIDTH), jnp.float32)],
        compiler_params=pltpu.CompilerParams(vmem_limit_bytes=8 * 1024 * 1024),
        cost_estimate=pl.CostEstimate(
            flops=1_000_000, bytes_accessed=3_000_000, transcendentals=0
        ),
        name="place",
    )(place, mine, other)


def hops(k):
    index = [(z, core) for z in range(NZ) for core in range(NC)]
    return [
        (z * NC + core, (z + (k if core == 0 else -k)) % NZ * NC + core) for z, core in index
    ]


def shards(queries, stretch_kv, pool, owner, slot, enc_weight, dec_weight, cotangent):
    x, z, core = lax.axis_index("x"), lax.axis_index("z"), lax.axis_index("core")
    swap = [(0, 1), (1, 0)]

    own = lax.dynamic_slice_in_dim(dec_weight, core * HEAD_DIM, HEAD_DIM, axis=2)
    own = own.reshape(WIDTH, KV)
    enc_own = lax.dynamic_slice_in_dim(enc_weight, core * 384, 2 * KV, axis=1)
    packed = jnp.concatenate([own, enc_own[:, :KV], enc_own[:, KV:]], axis=0)
    mine = lax.all_gather(packed, "mp", axis=0, tiled=False)

    qg = jnp.concatenate(
        [queries.reshape(NM, STRETCH, KV), cotangent.reshape(NM, STRETCH, KV)], axis=1
    )

    owner = owner.reshape(NX, NZ, NC, REQ)
    slot = slot.reshape(NX, NZ, NC, REQ)
    owner_core = owner % NC
    owner_z = (owner // NC) % NZ
    owner_x = owner // (NC * NZ)
    row = owner_z * SLOTS + slot
    ahead = (owner_z - z) % NZ
    own_core = owner_core == core
    direct = jnp.where(core == 0, ahead > 4, ahead < 4)
    far = jnp.minimum(ahead, NZ - ahead)
    stored_row = slot + jnp.where(
        far == 0,
        jnp.where(own_core, 0, SLOTS),
        jnp.where(
            far == 4,
            jnp.where(own_core, 64, 120),
            far * 2 * SLOTS
            + jnp.where(direct, 0, 56)
            + jnp.where(own_core == direct, 0, SLOTS),
        ),
    )

    def of_column(values, which):
        return lax.dynamic_slice(values, (0, z, which, 0), (NX, 1, 1, REQ)).reshape(NX * REQ)

    beside = lax.ppermute(pool, "core", swap)
    chip = jnp.concatenate([pool, beside], axis=0)
    chip, qg = lax.optimization_barrier((chip, qg))
    qg = lax.all_to_all(qg, "mp", split_axis=0, concat_axis=0, tiled=True)
    came = [lax.ppermute(chip, ("z", "core"), hops(k)) for k in range(1, 4)]
    came.append(lax.ppermute(pool, ("z", "core"), hops(4)))
    swapped = [lax.ppermute(part, "core", swap) for part in came]
    stored = jnp.concatenate([chip, *came, *swapped], axis=0)
    ask = of_column(stored_row, core)
    chosen = jnp.take(stored, ask, axis=0, mode="clip")
    chosen, qg = lax.optimization_barrier((chosen, qg))
    arrived = lax.all_to_all(chosen, "x", split_axis=0, concat_axis=0, tiled=True)
    my_x = lax.dynamic_slice(owner_x, (x, z, core, 0), (1, 1, 1, REQ)).reshape(REQ)
    rows = jnp.take(arrived, my_x * REQ + jnp.arange(REQ), axis=0, mode="clip")
    _, mine = lax.optimization_barrier((rows, mine))
    other = lax.ppermute(mine, "core", swap)
    rows = lax.all_to_all(rows, "mp", split_axis=0, concat_axis=0, tiled=True)
    rows = rows.reshape(2 * STRETCH, WIDTH)

    out, grad_rows = stretch_call(
        core.reshape(1).astype(jnp.int32), rows, stretch_kv, qg, mine, other
    )

    grad_rows = grad_rows.reshape(REQ, SPAN, WIDTH)
    grad_rows = lax.all_to_all(grad_rows, "mp", split_axis=0, concat_axis=0, tiled=True)
    every = lax.all_gather(grad_rows, "x", axis=0, tiled=True)
    every_beside = lax.ppermute(every, "core", swap)

    def places(which):
        here = (of_column(owner_x, which) == x) & (of_column(owner_core, which) == core)
        return jnp.where(here, of_column(row, which), NZ * SLOTS)

    place = jnp.stack([places(core), places(1 - core)]).astype(jnp.int32)
    partial = place_call(place, every, every_beside)
    out = lax.all_to_all(out, "mp", split_axis=0, concat_axis=0, tiled=True)
    grad_pool = lax.psum_scatter(partial, "z", scatter_dimension=0, tiled=True)
    grad_pool = grad_pool.astype(jnp.float32)
    attended = out[:, :STRETCH].reshape(NM * STRETCH, KV)
    grad_queries = out[:, STRETCH:].reshape(NM * STRETCH, KV)
    return attended, grad_queries, grad_pool


def solution(mesh):
    split = Mesh(mesh.devices.reshape(NX, NZ, NC, NM), ("x", "z", "core", "mp"))
    in_specs = (
        P(SEQ, "mp"),
        P(SEQ + ("mp",), None),
        P(SEQ, "mp", None),
        P(),
        P(),
        P("mp", None),
        P(None, None, "mp"),
        P(SEQ, "mp"),
    )
    out_specs = (P(SEQ, "mp"), P(SEQ, "mp"), P(SEQ, "mp", None))
    return jax.shard_map(shards, mesh=split, in_specs=in_specs, out_specs=out_specs, check_vma=False)
```

time: 288 us -> 214 us (0.74)
  the two profiles are of different devices: /device:TPU:1 before, /device:TPU:4 now
where the time goes in v1:
time: 214 us; the launch traced here: 213 us
  blocking collectives  63.5 us (30%)
  starting transfers between devices  48.1 us (22%)
  waiting for transfers between devices  43.1 us (20%)
  Pallas kernels  26.5 us (12%)
  between operations  14.4 us (7%)
  local copies, waits for them, and re-layouts  11.6 us (5%)
  other arithmetic  5.81 us (3%)
    pallas_call x1, Pallas kernels, stretch_call(): pl.pallas_call(stretch_kernel, out_shape=(jax.ShapeDtypeStruct((NM, 2 * S...  23.9 us
    all_to_all x1, blocking collectives, shards(): out = lax.all_to_all(out, 'mp', split_axis=0, concat_axis=0, tiled=True)  20.4 us
    reduce_scatter x1, waiting for transfers between devices, shards(): grad_pool = lax.psum_scatter(partial, 'z', scatter_dimension=0, tiled=True)  18.4 us
    all_to_all x1, blocking collectives, shards(): rows = lax.all_to_all(rows, 'mp', split_axis=0, concat_axis=0, tiled=True)  16.1 us
    all_to_all x1, blocking collectives, shards(): lax.all_to_all(grad_rows, 'mp', split_axis=0, concat_axis=0, tiled=True)  14 us
    all_gather x1, blocking collectives, shards(): every = lax.all_gather(grad_rows, 'x', axis=0, tiled=True)  13 us
    all_to_all x1, waiting for transfers between devices, shards(): lax.all_to_all(chosen, 'x', split_axis=0, concat_axis=0, tiled=True)  11.2 us
    ppermute x1, starting transfers between devices, shards(): came.append(lax.ppermute(pool, ('z', 'core'), hops(4)))  10.9 us
  transfers between devices with their start and end apart: 15, of which 5 were waited for; matrix products, arithmetic and copies ran while one was open for 5% of the time, Pallas kernels for 0%

profile of v1, /device:TPU:4, one launch (start us, length us, event | category | flops | bytes accessed | tf_op | source)
XLA Modules:
  0.0 213.1 jit_solution(5913642881887243917)
XLA Ops:
  9.7 1.9 collective-permute-start
  11.6 10.9 %collective-permute-start.4 = (bf16[8,8,896]{2,1,0:T(8,128)(2,1)S(1)}, bf16[8,8,896]{2,1,0:T(8,128)(2,1)}, u32[]{:S(2)}, u32[]{:S(2)}) collective-permute-start(bf16[8,8,896]{2,1,0:T(8,128)(2,1)S(1)} %copy-done.5), channel_id=1, source_target_pairs={{0,64},{8,72},{16,80},{24,88},{32,96},{40,104},{48,112},{56,120},{... | collective-permute-start | bytes 344072 | tf_op jit(solution)/shard_map/ppermute | solution.py:249
  25.8 5.2 %collective-permute-start.3 = (bf16[16,8,896]{2,1,0:T(8,128)(2,1)S(1)}, bf16[16,8,896]{2,1,0:T(8,128)(2,1)}, u32[]{:S(2)}, u32[]{:S(2)}) collective-permute-start(bf16[16,8,896]{2,1,0:T(8,128)(2,1)S(1)} %pad_maximum_fusion.2), channel_id=1, source_target_pairs={{0,48},{8,88},{16,64},{24,104},{32,80},{40,120},{48,96},{56,8},{64... | collective-permute-start | bytes 688136 | tf_op jit(solution)/shard_map/ppermute | solution.py:248
  31.0 1.9 collective-permute-start.2
  32.9 2.5 %collective-permute-start.1 = (bf16[16,8,896]{2,1,0:T(8,128)(2,1)S(1)}, bf16[16,8,896]{2,1,0:T(8,128)(2,1)}, u32[]{:S(2)}, u32[]{:S(2)}) collective-permute-start(bf16[16,8,896]{2,1,0:T(8,128)(2,1)S(1)} %pad_maximum_fusion.2), channel_id=1, source_target_pairs={{0,16},{8,120},{16,32},{24,8},{32,48},{40,24},{48,64},{56,40},{64,... | collective-permute-start | bytes 688136 | tf_op jit(solution)/shard_map/ppermute | solution.py:248
  35.4 7.1 %all-to-all-start = ((bf16[8,128,256]{2,1,0:T(8,128)(2,1)}), bf16[8,128,256]{2,1,0:T(8,128)(2,1)S(1)}, u32[]{:S(2)}, u32[]{:S(2)}) async-start(bf16[8,128,256]{2,1,0:T(8,128)(2,1)} %pad_maximum_fusion.1), calls=%async_computation | async-start | bytes 1048576 | tf_op jit(solution)/shard_map/all_to_all | solution.py:247
  42.6 3.7 %collective-permute-start.8 = (bf16[8,8,896]{2,1,0:T(8,128)(2,1)}, bf16[8,8,896]{2,1,0:T(8,128)(2,1)S(1)}, u32[]{:S(2)}, u32[]{:S(2)}) collective-permute-start(bf16[8,8,896]{2,1,0:T(8,128)(2,1)} %collective-permute-done.4), channel_id=1, source_target_pairs={{0,8},{8,0},{1,9},{9,1},{2,10},{10,2},{3,11},{11,3},{4,12},{12,4},... | collective-permute-start | bytes 344072 | tf_op jit(solution)/shard_map/ppermute | solution.py:250
  46.3 1.9 collective-permute-start.7
  48.2 2.4 %collective-permute-start.6 = (bf16[16,8,896]{2,1,0:T(8,128)(2,1)}, bf16[16,8,896]{2,1,0:T(8,128)(2,1)S(1)}, u32[]{:S(2)}, u32[]{:S(2)}) collective-permute-start(bf16[16,8,896]{2,1,0:T(8,128)(2,1)} %collective-permute-done.2), channel_id=1, source_target_pairs={{0,8},{8,0},{1,9},{9,1},{2,10},{10,2},{3,11},{11,3},{4,12},{12,4},... | collective-permute-start | bytes 688136 | tf_op jit(solution)/shard_map/ppermute | solution.py:250
  50.6 1.9 collective-permute-start.5
  58.1 8.7 %all-to-all-done.qg_ref = bf16[8,128,256]{2,1,0:T(8,128)(2,1)S(1)} async-done(((bf16[8,128,256]{2,1,0:T(8,128)(2,1)}), bf16[8,128,256]{2,1,0:T(8,128)(2,1)S(1)}, u32[]{:S(2)}, u32[]{:S(2)}) %all-to-all-start) | async-done | bytes 524320 | tf_op jit(solution)/shard_map/all_to_all | solution.py:247
  66.8 4.8 %all-to-all-start.1 = ((bf16[64,8,896]{2,1,0:T(8,128)(2,1)}), bf16[64,8,896]{2,1,0:T(8,128)(2,1)S(1)}, u32[]{:S(2)}, u32[]{:S(2)}) async-start(bf16[64,8,896]{2,1,0:T(8,128)(2,1)} %gather_fusion), calls=%async_computation.1 | async-start | bytes 1835008 | tf_op jit(solution)/shard_map/all_to_all | solution.py:255
  71.7 11.2 %all-to-all-done.1 = bf16[64,8,896]{2,1,0:T(8,128)(2,1)S(1)} async-done(((bf16[64,8,896]{2,1,0:T(8,128)(2,1)}), bf16[64,8,896]{2,1,0:T(8,128)(2,1)S(1)}, u32[]{:S(2)}, u32[]{:S(2)}) %all-to-all-start.1) | async-done | bytes 917536 | tf_op jit(solution)/shard_map/all_to_all | solution.py:255
  83.5 3.3 %all-gather.3.cloned.1.call-done = bf16[8960,256]{1,0:T(8,128)(2,1)} async-done(((bf16[1120,256]{1,0:T(8,128)(2,1)}), bf16[8960,256]{1,0:T(8,128)(2,1)}) %all-gather.3.cloned.1.call-update) | async-done | bytes 4587536 | tf_op jit(solution)/shard_map/all_gather | solution.py:213
  86.8 1.9 collective-permute-start.9
  88.7 16.1 %all_to_all.25 = bf16[16,8,896]{2,1,0:T(8,128)(2,1)S(1)} all-to-all(bf16[16,8,896]{2,1,0:T(8,128)(2,1)S(1)} %gather_fusion.1), channel_id=1, replica_groups=mesh['x'=4,'z'=8,'core'=2,'mp'=8] {'mp'}, dimensions={0} | all-to-all | bytes 458752 | tf_op jit(solution)/shard_map/all_to_all | solution.py:260
  104.8 2.3 %copy-done.1 = bf16[8960,256]{1,0:T(8,128)(2,1)S(1)} copy-done((bf16[8960,256]{1,0:T(8,128)(2,1)S(1)}, bf16[8960,256]{1,0:T(8,128)(2,1)}, u32[]{:S(2)}) %copy-start.1) | copy-done | bytes 4587544
  107.1 23.9 %stretch.1 = (bf16[8,128,256]{2,1,0:T(8,128)(2,1)S(1)}, bf16[128,896]{1,0:T(8,128)(2,1)S(1)}) custom-call(s32[1]{0:T(128)} %bitcast.core_ref, bf16[128,896]{1,0:T(8,128)(2,1)S(1)} %bitcast.20, bf16[64,1792]{1,0:T(8,128)(2,1)S(1)} %copy-done.2, bf16[8,128,256]{2,1,0:T(8,128)(2,1)S(1)} %all-to-all-done.qg_ref, bf16[8,1120,256]{2,1,0:T(8,128)(2,1)S(1)} %bitcast.23, ...), custom_call_target="tpu_custom_call" | custom-call | flops 7000000000 | bytes 11000000 | tf_op jit(solution)/shard_map/stretch/pallas_call | solution.py:142
  131.1 14.0 %all_to_all.26 = bf16[16,8,896]{2,1,0:T(8,128)(2,1)S(1)} all-to-all(bf16[16,8,896]{2,1,0:T(8,128)(2,1)S(1)} %bitcast.21), channel_id=1, replica_groups=mesh['x'=4,'z'=8,'core'=2,'mp'=8] {'mp'}, dimensions={0} | all-to-all | bytes 458752 | tf_op jit(solution)/shard_map/all_to_all | solution.py:268
  145.1 13.0 %all_gather.11.mine_ref = bf16[64,8,896]{2,1,0:T(8,128)(2,1)S(1)} all-gather(bf16[16,8,896]{2,1,0:T(8,128)(2,1)S(1)} %all_to_all.26), channel_id=1, replica_groups=mesh['x'=4,'z'=8,'core'=2,'mp'=8] {'x'}, dimensions={0}, use_global_device_ids=true | all-gather | bytes 1146880 | tf_op jit(solution)/shard_map/all_gather | solution.py:269
  158.1 1.9 collective-permute-start.10
  162.5 2.6 %place.1 = bf16[64,8,896]{2,1,0:T(8,128)(2,1)} custom-call(s32[2,64]{1,0:T(2,128)S(1)} %pad_add_fusion.place_ref, bf16[64,8,896]{2,1,0:T(8,128)(2,1)S(1)} %all_gather.11.mine_ref, bf16[64,8,896]{2,1,0:T(8,128)(2,1)S(1)} %collective-permute-done.10.other_ref), custom_call_target="tpu_custom_call" | custom-call | flops 1000000 | bytes 3000000 | tf_op jit(solution)/shard_map/place/pallas_call | solution.py:184
  165.1 20.4 %all_to_all.27 = bf16[8,128,256]{2,1,0:T(8,128)(2,1)S(1)} all-to-all(bf16[8,128,256]{2,1,0:T(8,128)(2,1)S(1)} %get-tuple-element.15), channel_id=1, replica_groups=mesh['x'=4,'z'=8,'core'=2,'mp'=8] {'mp'}, dimensions={0} | all-to-all | bytes 1048576 | tf_op jit(solution)/shard_map/all_to_all | solution.py:278
  186.3 18.4 %reduce-scatter.2.cloned.1.call-done = bf16[8,8,896]{2,1,0:T(8,128)(2,1)} async-done(((bf16[64,8,896]{2,1,0:T(8,128)(2,1)}), bf16[8,8,896]{2,1,0:T(8,128)(2,1)}) %reduce-scatter.2.cloned.1.call-update) | async-done | bytes 114704 | tf_op jit(solution)/shard_map/reduce_scatter | solution.py:279
  (67 shorter events, 16.7 us)
Async XLA Ops:
  7.2 1.2 copy-start
  7.2 1.6 copy-start.6
  7.2 79.6 %all-gather.3.cloned.1.call-start = ((), (), s32[]{:S(2)}) async-start(), calls=%async_computation.7 | async-start | bytes 5160960 | tf_op jit(solution)/shard_map/all_gather | solution.py:213
  8.4 1.4 copy-start.5
  8.4 14.2 %copy-start.7 = (s32[512,2]{0,1:T(2,128)S(1)}, s32[512,2]{0,1:T(2,128)}, u32[]{:S(2)}) copy-start(s32[512,2]{0,1:T(2,128)} %param.11) | copy-start | bytes 12292
  8.7 14.2 %copy-start.8 = (s32[512,2]{0,1:T(2,128)S(1)}, s32[512,2]{0,1:T(2,128)}, u32[]{:S(2)}) copy-start(s32[512,2]{0,1:T(2,128)} %param.12) | copy-start | bytes 12292
  8.8 16.2 %copy-start.3 = (bf16[512,256]{1,0:T(8,128)(2,1)S(1)}, bf16[512,256]{1,0:T(8,128)(2,1)}, u32[]{:S(2)}) copy-start(bf16[512,256]{1,0:T(8,128)(2,1)} %param.15) | copy-start | bytes 786436
  8.8 16.2 %copy-start.4 = (bf16[512,256]{1,0:T(8,128)(2,1)S(1)}, bf16[512,256]{1,0:T(8,128)(2,1)}, u32[]{:S(2)}) copy-start(bf16[512,256]{1,0:T(8,128)(2,1)} %param.8) | copy-start | bytes 786436
  9.7 16.1 %collective-permute-start = (bf16[8,8,896]{2,1,0:T(8,128)(2,1)S(1)}, bf16[8,8,896]{2,1,0:T(8,128)(2,1)S(1)}, u32[]{:S(2)}, u32[]{:S(2)}) collective-permute-start(bf16[8,8,896]{2,1,0:T(8,128)(2,1)S(1)} %copy-done.5), channel_id=1, source_target_pairs={{0,8},{8,0},{1,9},{9,1},{2,10},{10,2},{3,11},{11,3},{4,12},{12,4},... | collective-permute-start | bytes 344072 | tf_op jit(solution)/shard_map/ppermute | solution.py:244
  11.6 30.9 %collective-permute-start.4 = (bf16[8,8,896]{2,1,0:T(8,128)(2,1)S(1)}, bf16[8,8,896]{2,1,0:T(8,128)(2,1)}, u32[]{:S(2)}, u32[]{:S(2)}) collective-permute-start(bf16[8,8,896]{2,1,0:T(8,128)(2,1)S(1)} %copy-done.5), channel_id=1, source_target_pairs={{0,64},{8,72},{16,80},{24,88},{32,96},{40,104},{48,112},{56,120},{... | collective-permute-start | bytes 344072 | tf_op jit(solution)/shard_map/ppermute | solution.py:249
  25.8 20.4 %collective-permute-start.3 = (bf16[16,8,896]{2,1,0:T(8,128)(2,1)S(1)}, bf16[16,8,896]{2,1,0:T(8,128)(2,1)}, u32[]{:S(2)}, u32[]{:S(2)}) collective-permute-start(bf16[16,8,896]{2,1,0:T(8,128)(2,1)S(1)} %pad_maximum_fusion.2), channel_id=1, source_target_pairs={{0,48},{8,88},{16,64},{24,104},{32,80},{40,120},{48,96},{56,8},{64... | collective-permute-start | bytes 688136 | tf_op jit(solution)/shard_map/ppermute | solution.py:248
  31.0 17.2 %collective-permute-start.2 = (bf16[16,8,896]{2,1,0:T(8,128)(2,1)S(1)}, bf16[16,8,896]{2,1,0:T(8,128)(2,1)}, u32[]{:S(2)}, u32[]{:S(2)}) collective-permute-start(bf16[16,8,896]{2,1,0:T(8,128)(2,1)S(1)} %pad_maximum_fusion.2), channel_id=1, source_target_pairs={{0,32},{8,104},{16,48},{24,120},{32,64},{40,8},{48,80},{56,24},{64... | collective-permute-start | bytes 688136 | tf_op jit(solution)/shard_map/ppermute | solution.py:248
  32.9 17.7 %collective-permute-start.1 = (bf16[16,8,896]{2,1,0:T(8,128)(2,1)S(1)}, bf16[16,8,896]{2,1,0:T(8,128)(2,1)}, u32[]{:S(2)}, u32[]{:S(2)}) collective-permute-start(bf16[16,8,896]{2,1,0:T(8,128)(2,1)S(1)} %pad_maximum_fusion.2), channel_id=1, source_target_pairs={{0,16},{8,120},{16,32},{24,8},{32,48},{40,24},{48,64},{56,40},{64,... | collective-permute-start | bytes 688136 | tf_op jit(solution)/shard_map/ppermute | solution.py:248
  35.4 31.4 %all-to-all-start = ((bf16[8,128,256]{2,1,0:T(8,128)(2,1)}), bf16[8,128,256]{2,1,0:T(8,128)(2,1)S(1)}, u32[]{:S(2)}, u32[]{:S(2)}) async-start(bf16[8,128,256]{2,1,0:T(8,128)(2,1)} %pad_maximum_fusion.1), calls=%async_computation | async-start | bytes 1048576 | tf_op jit(solution)/shard_map/all_to_all | solution.py:247
  42.6 13.9 %collective-permute-start.8 = (bf16[8,8,896]{2,1,0:T(8,128)(2,1)}, bf16[8,8,896]{2,1,0:T(8,128)(2,1)S(1)}, u32[]{:S(2)}, u32[]{:S(2)}) collective-permute-start(bf16[8,8,896]{2,1,0:T(8,128)(2,1)} %collective-permute-done.4), channel_id=1, source_target_pairs={{0,8},{8,0},{1,9},{9,1},{2,10},{10,2},{3,11},{11,3},{4,12},{12,4},... | collective-permute-start | bytes 344072 | tf_op jit(solution)/shard_map/ppermute | solution.py:250
  46.3 10.2 %collective-permute-start.7 = (bf16[16,8,896]{2,1,0:T(8,128)(2,1)}, bf16[16,8,896]{2,1,0:T(8,128)(2,1)S(1)}, u32[]{:S(2)}, u32[]{:S(2)}) collective-permute-start(bf16[16,8,896]{2,1,0:T(8,128)(2,1)} %collective-permute-done.3), channel_id=1, source_target_pairs={{0,8},{8,0},{1,9},{9,1},{2,10},{10,2},{3,11},{11,3},{4,12},{12,4},... | collective-permute-start | bytes 688136 | tf_op jit(solution)/shard_map/ppermute | solution.py:250
  48.2 8.2 %collective-permute-start.6 = (bf16[16,8,896]{2,1,0:T(8,128)(2,1)}, bf16[16,8,896]{2,1,0:T(8,128)(2,1)S(1)}, u32[]{:S(2)}, u32[]{:S(2)}) collective-permute-start(bf16[16,8,896]{2,1,0:T(8,128)(2,1)} %collective-permute-done.2), channel_id=1, source_target_pairs={{0,8},{8,0},{1,9},{9,1},{2,10},{10,2},{3,11},{11,3},{4,12},{12,4},... | collective-permute-start | bytes 688136 | tf_op jit(solution)/shard_map/ppermute | solution.py:250
  50.6 5.7 %collective-permute-start.5 = (bf16[16,8,896]{2,1,0:T(8,128)(2,1)}, bf16[16,8,896]{2,1,0:T(8,128)(2,1)S(1)}, u32[]{:S(2)}, u32[]{:S(2)}) collective-permute-start(bf16[16,8,896]{2,1,0:T(8,128)(2,1)} %collective-permute-done.1), channel_id=1, source_target_pairs={{0,8},{8,0},{1,9},{9,1},{2,10},{10,2},{3,11},{11,3},{4,12},{12,4},... | collective-permute-start | bytes 688136 | tf_op jit(solution)/shard_map/ppermute | solution.py:250
  58.1 46.7 %copy-start.2 = (bf16[64,1792]{1,0:T(8,128)(2,1)S(1)}, bf16[64,1792]{1,0:T(8,128)(2,1)}, u32[]{:S(2)}) copy-start(bf16[64,1792]{1,0:T(8,128)(2,1)} %kv_ref.1) | copy-start | bytes 688132
  66.8 16.1 %all-to-all-start.1 = ((bf16[64,8,896]{2,1,0:T(8,128)(2,1)}), bf16[64,8,896]{2,1,0:T(8,128)(2,1)S(1)}, u32[]{:S(2)}, u32[]{:S(2)}) async-start(bf16[64,8,896]{2,1,0:T(8,128)(2,1)} %gather_fusion), calls=%async_computation.1 | async-start | bytes 1835008 | tf_op jit(solution)/shard_map/all_to_all | solution.py:255
  71.6 133.0 %reduce-scatter.2.cloned.1.call-start = ((), (), s32[]{:S(2)}) async-start(), calls=%async_computation.6 | async-start | bytes 1032192 | tf_op jit(solution)/shard_map/reduce_scatter | solution.py:279
  86.8 18.0 %collective-permute-start.9 = (bf16[8,1120,256]{2,1,0:T(8,128)(2,1)}, bf16[8,1120,256]{2,1,0:T(8,128)(2,1)S(1)}, u32[]{:S(2)}, u32[]{:S(2)}) collective-permute-start(bf16[8,1120,256]{2,1,0:T(8,128)(2,1)} %bitcast.22), channel_id=1, source_target_pairs={{0,8},{8,0},{1,9},{9,1},{2,10},{10,2},{3,11},{11,3},{4,12},{12,4},... | collective-permute-start | bytes 13762568 | tf_op jit(solution)/shard_map/ppermute | solution.py:259
  104.8 2.3 %copy-start.1 = (bf16[8960,256]{1,0:T(8,128)(2,1)S(1)}, bf16[8960,256]{1,0:T(8,128)(2,1)}, u32[]{:S(2)}) copy-start(bf16[8960,256]{1,0:T(8,128)(2,1)} %all-gather.3.cloned.1.call-done) | copy-start | bytes 13762564
  158.1 4.4 %collective-permute-start.10 = (bf16[64,8,896]{2,1,0:T(8,128)(2,1)S(1)}, bf16[64,8,896]{2,1,0:T(8,128)(2,1)S(1)}, u32[]{:S(2)}, u32[]{:S(2)}) collective-permute-start(bf16[64,8,896]{2,1,0:T(8,128)(2,1)S(1)} %all_gather.11.mine_ref), channel_id=1, source_target_pairs={{0,8},{8,0},{1,9},{9,1},{2,10},{10,2},{3,11},{11,3},{4,12},{12,4},... | collective-permute-start | bytes 2752520 | tf_op jit(solution)/shard_map/ppermute | solution.py:270
Sparse Core Ops, SparseCore 0:
  10.1 76.6 all-gather.2
  165.2 39.4 reduce-scatter.1

commit v2 on v1

v2 whole, which is shorter than its diff:
```python
import jax
import jax.numpy as jnp
from jax import lax
from jax.experimental import pallas as pl
from jax.experimental.pallas import tpu as pltpu
from jax.sharding import Mesh
from jax.sharding import PartitionSpec as P

HEAD_DIM = 128
SCALE = HEAD_DIM ** (-0.5)
SEQ = ("x", "z", "core")
NX, NZ, NC, NM = 4, 8, 2, 8
REQ = 16
SLOTS = 8
STRETCH = 64
SPAN = 8
WIDTH = 896
ENC_HEADS = 7
KV = 2 * HEAD_DIM
ENC_ROWS = 112
NONE = NZ * SLOTS


def dot(a, b, dims):
    return lax.dot_general(a, b, ((dims[0], dims[1]), ((), ())), preferred_element_type=jnp.float32)


def softmax(scores):
    top = jnp.max(scores, axis=-1, keepdims=True)
    e = jnp.exp(scores - top)
    return e * (1.0 / jnp.sum(e, axis=-1, keepdims=True))


def softmax_back(weights, grad):
    return weights * (grad - jnp.sum(grad * weights, axis=-1, keepdims=True))


def stretch_kernel(
    rows_ref,
    kv_ref,
    qg_ref,
    packed_ref,
    out_ref,
    grad_ref,
    enc_w,
    dec_w,
    encoded_ref,
    heads_ref,
    probs_ref,
    total_ref,
    enc_sem,
    dec_sem,
):
    enc_copies = []
    for m in range(NM):
        for part, (core, pair, skip, column) in enumerate(
            ((0, 0, 0, 0), (0, 1, 0, 256), (1, 0, 128, 512), (1, 1, 0, 640))
        ):
            enc_copies.append(
                pltpu.make_async_copy(
                    packed_ref.at[
                        core * NM + m,
                        pl.ds(WIDTH + pair * ENC_ROWS, ENC_ROWS),
                        pl.ds(skip, KV - skip),
                    ],
                    enc_w.at[pl.ds(m * ENC_ROWS, ENC_ROWS), pl.ds(column, KV - skip)],
                    enc_sem.at[m, part],
                )
            )
    for copy in enc_copies:
        copy.start()
    dec_copies = []
    for m in range(NM):
        group = []
        for core in range(NC):
            for kind in range(2):
                group.append(
                    pltpu.make_async_copy(
                        packed_ref.at[
                            core * NM + m, pl.ds(0, WIDTH), pl.ds(kind * HEAD_DIM, HEAD_DIM)
                        ],
                        dec_w.at[m, :, pl.ds(kind * KV + core * HEAD_DIM, HEAD_DIM)],
                        dec_sem.at[m, core, kind],
                    )
                )
        dec_copies.append(group)
        for copy in group:
            copy.start()
    for copy in enc_copies:
        copy.wait()

    rows = rows_ref[...]
    query = dot(rows, enc_w[...], ((1,), (0,))).astype(jnp.bfloat16)
    for h in range(ENC_HEADS):
        cols = slice(h * HEAD_DIM, (h + 1) * HEAD_DIM)
        keys = kv_ref[:, cols]
        values = kv_ref[:, WIDTH + h * HEAD_DIM : WIDTH + (h + 1) * HEAD_DIM]
        weights = softmax(dot(query[:, cols], keys, ((1,), (1,))) * SCALE)
        probs_ref[h] = weights
        mixed = dot(weights.astype(jnp.bfloat16), values, ((1,), (0,)))
        encoded_ref[:, cols] = (rows[:, cols].astype(jnp.float32) + mixed).astype(jnp.bfloat16)
    encoded = encoded_ref[...]

    left = lax.broadcasted_iota(jnp.int32, (STRETCH, KV), 1) < HEAD_DIM
    zero = jnp.zeros((STRETCH, KV), jnp.bfloat16)

    def stacked(pair):
        return jnp.concatenate([jnp.where(left, pair, zero), jnp.where(left, zero, pair)], axis=0)

    def beside(blocks):
        return jnp.where(left, blocks[:STRETCH], blocks[STRETCH:]).astype(jnp.bfloat16)

    for m in range(NM):
        for copy in dec_copies[m]:
            copy.wait()
        both = dot(encoded, dec_w[m], ((1,), (0,))).astype(jnp.bfloat16)
        keys, values = both[:, :KV], both[:, KV:]
        q = stacked(qg_ref[m, :STRETCH, :])
        g = stacked(qg_ref[m, STRETCH:, :])
        weights = softmax(dot(q, keys, ((1,), (1,))) * SCALE)
        low_w = weights.astype(jnp.bfloat16)
        out_ref[m, :STRETCH, :] = beside(dot(low_w, values, ((1,), (0,))))
        grad_s = softmax_back(weights, dot(g, values, ((1,), (1,)))).astype(jnp.bfloat16)
        out_ref[m, STRETCH:, :] = beside(dot(grad_s, keys, ((1,), (0,))) * SCALE)
        grad_v = dot(low_w, g, ((0,), (0,))).astype(jnp.bfloat16)
        grad_k = (dot(grad_s, q, ((0,), (0,))) * SCALE).astype(jnp.bfloat16)
        term = dot(jnp.concatenate([grad_k, grad_v], axis=1), dec_w[m], ((1,), (1,)))
        if m == 0:
            total_ref[...] = term
        else:
            total_ref[...] += term

    grad_encoded = total_ref[...].astype(jnp.bfloat16)
    for h in range(ENC_HEADS):
        cols = slice(h * HEAD_DIM, (h + 1) * HEAD_DIM)
        keys = kv_ref[:, cols]
        values = kv_ref[:, WIDTH + h * HEAD_DIM : WIDTH + (h + 1) * HEAD_DIM]
        grad_w = dot(grad_encoded[:, cols], values, ((1,), (1,)))
        grad_s = softmax_back(probs_ref[h], grad_w).astype(jnp.bfloat16)
        heads_ref[:, cols] = (dot(grad_s, keys, ((1,), (0,))) * SCALE).astype(jnp.bfloat16)
    back = dot(heads_ref[...], enc_w[...], ((1,), (1,)))
    grad_ref[...] = (grad_encoded.astype(jnp.float32) + back).astype(jnp.bfloat16)


VMEM = pl.BlockSpec(memory_space=pltpu.VMEM)
SMEM = pl.BlockSpec(memory_space=pltpu.SMEM)


def stretch_call(rows, kv, qg, packed):
    return pl.pallas_call(
        stretch_kernel,
        out_shape=(
            jax.ShapeDtypeStruct((NM, 2 * STRETCH, KV), jnp.bfloat16),
            jax.ShapeDtypeStruct((2 * STRETCH, WIDTH), jnp.bfloat16),
        ),
        in_specs=[VMEM, VMEM, VMEM, pl.BlockSpec(memory_space=pl.ANY)],
        out_specs=(VMEM, VMEM),
        scratch_shapes=[
            pltpu.VMEM((WIDTH, WIDTH), jnp.bfloat16),
            pltpu.VMEM((NM, WIDTH, 2 * KV), jnp.bfloat16),
            pltpu.VMEM((2 * STRETCH, WIDTH), jnp.bfloat16),
            pltpu.VMEM((2 * STRETCH, WIDTH), jnp.bfloat16),
            pltpu.VMEM((ENC_HEADS, 2 * STRETCH, STRETCH), jnp.float32),
            pltpu.VMEM((2 * STRETCH, WIDTH), jnp.float32),
            pltpu.SemaphoreType.DMA((NM, 4)),
            pltpu.SemaphoreType.DMA((NM, NC, 2)),
        ],
        compiler_params=pltpu.CompilerParams(vmem_limit_bytes=28 * 1024 * 1024),
        cost_estimate=pl.CostEstimate(
            flops=7_000_000_000, bytes_accessed=11_000_000, transcendentals=200_000
        ),
        name="stretch",
    )(rows, kv, qg, packed)


def choose_kernel(ask_ref, *refs):
    *parts, out_ref, all_ref = refs
    at = 0
    for part in parts:
        all_ref[at : at + part.shape[0]] = part[...]
        at += part.shape[0]

    def copy(i, carry):
        out_ref[i] = all_ref[ask_ref[i]]
        return carry

    lax.fori_loop(0, out_ref.shape[0], copy, 0, unroll=8)


def choose_call(ask, parts):
    return pl.pallas_call(
        choose_kernel,
        out_shape=jax.ShapeDtypeStruct((NX * REQ, SPAN, WIDTH), jnp.bfloat16),
        in_specs=[SMEM] + [VMEM] * len(parts),
        out_specs=VMEM,
        scratch_shapes=[pltpu.VMEM((NC * NZ * SLOTS, SPAN, WIDTH), jnp.bfloat16)],
        compiler_params=pltpu.CompilerParams(vmem_limit_bytes=12 * 1024 * 1024),
        cost_estimate=pl.CostEstimate(flops=0, bytes_accessed=3_000_000, transcendentals=0),
        name="choose",
    )(ask, *parts)


def place_kernel(place_ref, mine_ref, other_ref, *refs):
    *out_refs, total_ref = refs
    total_ref[...] = jnp.zeros_like(total_ref)
    for source, ref in enumerate((mine_ref, other_ref)):

        def add(i, carry, ref=ref, source=source):
            at = place_ref[source, i]
            total_ref[at] += ref[i].astype(jnp.float32)
            return carry

        lax.fori_loop(0, NX * REQ, add, 0, unroll=4)
    at = 0
    for ref in out_refs:
        ref[...] = total_ref[at : at + ref.shape[0]].astype(jnp.bfloat16)
        at += ref.shape[0]


def place_call(place, mine, other):
    return pl.pallas_call(
        place_kernel,
        out_shape=tuple(
            jax.ShapeDtypeStruct((count * SLOTS, SPAN, WIDTH), jnp.bfloat16)
            for count in (1, 2, 2, 2, 1)
        ),
        in_specs=[SMEM, VMEM, VMEM],
        out_specs=(VMEM,) * 5,
        scratch_shapes=[pltpu.VMEM((NONE + 1, SPAN, WIDTH), jnp.float32)],
        compiler_params=pltpu.CompilerParams(vmem_limit_bytes=12 * 1024 * 1024),
        cost_estimate=pl.CostEstimate(
            flops=1_000_000, bytes_accessed=3_000_000, transcendentals=0
        ),
        name="place",
    )(place, mine, other)


def along_z(values, k):
    index = [(z, core) for z in range(NZ) for core in range(NC)]
    pairs = [
        (z * NC + core, (z + (k if core == 0 else -k)) % NZ * NC + core) for z, core in index
    ]
    return lax.ppermute(values, ("z", "core"), pairs)


def shards(queries, stretch_kv, pool, owner, slot, enc_weight, dec_weight, cotangent):
    x, z, core = lax.axis_index("x"), lax.axis_index("z"), lax.axis_index("core")
    swap = [(0, 1), (1, 0)]

    own = lax.dynamic_slice_in_dim(dec_weight, core * HEAD_DIM, HEAD_DIM, axis=2)
    own = own.reshape(WIDTH, KV)
    enc_own = lax.dynamic_slice_in_dim(enc_weight, core * 384, 2 * KV, axis=1)
    packed = jnp.concatenate([own, enc_own[:, :KV], enc_own[:, KV:]], axis=0)
    packed = lax.all_gather(packed, ("core", "mp"), axis=0, tiled=False)

    qg = jnp.concatenate(
        [queries.reshape(NM, STRETCH, KV), cotangent.reshape(NM, STRETCH, KV)], axis=1
    )
    qg = lax.all_to_all(qg, "mp", split_axis=0, concat_axis=0, tiled=True)

    owner = owner.reshape(NX, NZ, NC, REQ)
    slot = slot.reshape(NX, NZ, NC, REQ)
    owner_core = owner % NC
    owner_z = (owner // NC) % NZ
    owner_x = owner // (NC * NZ)
    ahead = (owner_z - z) % NZ
    far = jnp.minimum(ahead, NZ - ahead)
    own_core = owner_core == core
    ask = (
        jnp.where(far == 0, 0, jnp.where(far == 4, 112, far * 32 - 16))
        + jnp.where((far > 0) & (ahead < 4), NC * SLOTS, 0)
        + owner_core * SLOTS
        + slot
    )
    back = jnp.where(core == 0, ahead < 4, ahead > 4) & (far > 0)
    place = slot + jnp.where(
        back,
        far * 2 * SLOTS - SLOTS + jnp.where(own_core, 0, SLOTS),
        jnp.where(own_core & (far == 0), 0, jnp.where(own_core & (far == 4), 56, NONE)),
    )
    place = jnp.where(owner_x == x, jnp.minimum(place, NONE), NONE)

    def of_column(values, which):
        return lax.dynamic_slice(values, (0, z, which, 0), (NX, 1, 1, REQ)).reshape(NX * REQ)

    chip = lax.all_gather(pool, "core", axis=0, tiled=True)
    came = [along_z(chip, k) for k in range(1, 4)] + [along_z(pool, 4)]
    parts = [chip] + [lax.all_gather(part, "core", axis=0, tiled=True) for part in came]
    chosen = choose_call(of_column(ask, core), parts)
    chosen, qg = lax.optimization_barrier((chosen, qg))
    arrived = lax.all_to_all(chosen, "x", split_axis=0, concat_axis=0, tiled=True)
    my_x = lax.dynamic_slice(owner_x, (x, z, core, 0), (1, 1, 1, REQ)).reshape(REQ)
    rows = jnp.take(arrived, my_x * REQ + jnp.arange(REQ), axis=0, mode="clip")
    rows = lax.all_to_all(rows, "mp", split_axis=0, concat_axis=0, tiled=True)
    rows = rows.reshape(2 * STRETCH, WIDTH)
    _, packed = lax.optimization_barrier((chosen, packed))

    out, grad_rows = stretch_call(rows, stretch_kv, qg, packed)

    grad_rows = grad_rows.reshape(REQ, SPAN, WIDTH)
    grad_rows = lax.all_to_all(grad_rows, "mp", split_axis=0, concat_axis=0, tiled=True)
    every = lax.all_gather(grad_rows, "x", axis=0, tiled=True)
    every_beside = lax.ppermute(every, "core", swap)
    places = jnp.stack([of_column(place, core), of_column(place, 1 - core)])
    mine, *partial = place_call(places, every, every_beside)
    partial = [along_z(part, k).astype(jnp.float32) for k, part in enumerate(partial, 1)]
    ours = mine.astype(jnp.float32) + partial[3] + sum(part[:SLOTS] for part in partial[:3])
    theirs = sum(part[SLOTS:] for part in partial[:3]).astype(jnp.bfloat16)
    grad_pool = ours + lax.ppermute(theirs, "core", swap).astype(jnp.float32)

    out = lax.all_to_all(out, "mp", split_axis=0, concat_axis=0, tiled=True)
    attended = out[:, :STRETCH].reshape(NM * STRETCH, KV)
    grad_queries = out[:, STRETCH:].reshape(NM * STRETCH, KV)
    return attended, grad_queries, grad_pool


def solution(mesh):
    split = Mesh(mesh.devices.reshape(NX, NZ, NC, NM), ("x", "z", "core", "mp"))
    in_specs = (
        P(SEQ, "mp"),
        P(SEQ + ("mp",), None),
        P(SEQ, "mp", None),
        P(),
        P(),
        P("mp", None),
        P(None, None, "mp"),
        P(SEQ, "mp"),
    )
    out_specs = (P(SEQ, "mp"), P(SEQ, "mp"), P(SEQ, "mp", None))
    return jax.shard_map(shards, mesh=split, in_specs=in_specs, out_specs=out_specs, check_vma=False)
```

time: 214 us -> 189 us (0.88)
  the two profiles are of different devices: /device:TPU:4 before, /device:TPU:1 now
where the time goes in v2:
time: 189 us; the launch traced here: 188 us
  starting transfers between devices  61.6 us (33%)
  blocking collectives  41.9 us (22%)
  waiting for transfers between devices  41.2 us (22%)
  Pallas kernels  16.5 us (9%)
  between operations  14.4 us (8%)
  local copies, waits for them, and re-layouts  8.11 us (4%)
  other arithmetic  4.1 us (2%)
    ppermute x8, starting transfers between devices, along_z(): return lax.ppermute(values, ('z', 'core'), pairs)  33.3 us
    pallas_call x1, Pallas kernels, stretch_call(): pl.pallas_call(stretch_kernel, out_shape=(jax.ShapeDtypeStruct((NM, 2 * S...  13.2 us
    all_to_all x1, waiting for transfers between devices, shards(): lax.all_to_all(chosen, 'x', split_axis=0, concat_axis=0, tiled=True)  13.1 us
    all_to_all x1, blocking collectives, shards(): lax.all_to_all(grad_rows, 'mp', split_axis=0, concat_axis=0, tiled=True)  11.7 us
    all_gather x1, blocking collectives, shards(): every = lax.all_gather(grad_rows, 'x', axis=0, tiled=True)  11 us
    all_gather x4, blocking collectives, shards(): lax.all_gather(part, 'core', axis=0, tiled=True)  10.7 us
    all_to_all x1, waiting for transfers between devices, shards(): qg = lax.all_to_all(qg, 'mp', split_axis=0, concat_axis=0, tiled=True)  9.35 us
    ppermute x8, waiting for transfers between devices, along_z(): return lax.ppermute(values, ('z', 'core'), pairs)  9.29 us
  transfers between devices with their start and end apart: 15, of which 7 were waited for; matrix products, arithmetic and copies ran while one was open for 2% of the time, Pallas kernels for 2%

profile of v2, /device:TPU:1, one launch (start us, length us, event | category | flops | bytes accessed | tf_op | source)
XLA Modules:
  0.0 187.8 jit_solution(10279257048146557953)
XLA Ops:
  9.8 8.5 %all_gather.24.refs_0_ = bf16[16,8,896]{2,1,0:T(8,128)(2,1)S(1)} all-gather(bf16[8,8,896]{2,1,0:T(8,128)(2,1)S(1)} %copy-done.5), channel_id=1, replica_groups=mesh['x'=4,'z'=8,'core'=2,'mp'=8] {'core'}, dimensions={0}, use_global_device_ids=true | all-gather | bytes 344064 | tf_op jit(solution)/shard_map/all_gather | solution.py:286
  18.2 5.3 %collective-permute-start = (bf16[16,8,896]{2,1,0:T(8,128)(2,1)S(1)}, bf16[16,8,896]{2,1,0:T(8,128)(2,1)S(1)}, u32[]{:S(2)}, u32[]{:S(2)}) collective-permute-start(bf16[16,8,896]{2,1,0:T(8,128)(2,1)S(1)} %all_gather.24.refs_0_), channel_id=1, source_target_pairs={{0,16},{8,120},{16,32},{24,8},{32,48},{40,24},{48,64},{56,40},{64,... | collective-permute-start | bytes 688136 | tf_op jit(solution)/shard_map/ppermute | solution.py:243
  23.5 2.2 %collective-permute-start.1 = (bf16[16,8,896]{2,1,0:T(8,128)(2,1)S(1)}, bf16[16,8,896]{2,1,0:T(8,128)(2,1)S(1)}, u32[]{:S(2)}, u32[]{:S(2)}) collective-permute-start(bf16[16,8,896]{2,1,0:T(8,128)(2,1)S(1)} %all_gather.24.refs_0_), channel_id=1, source_target_pairs={{0,32},{8,104},{16,48},{24,120},{32,64},{40,8},{48,80},{56,24},{64... | collective-permute-start | bytes 688136 | tf_op jit(solution)/shard_map/ppermute | solution.py:243
  27.6 7.3 %collective-permute-start.3 = (bf16[8,8,896]{2,1,0:T(8,128)(2,1)S(1)}, bf16[8,8,896]{2,1,0:T(8,128)(2,1)S(1)}, u32[]{:S(2)}, u32[]{:S(2)}) collective-permute-start(bf16[8,8,896]{2,1,0:T(8,128)(2,1)S(1)} %copy-done.5), channel_id=1, source_target_pairs={{0,64},{8,72},{16,80},{24,88},{32,96},{40,104},{48,112},{56,120},{... | collective-permute-start | bytes 344072 | tf_op jit(solution)/shard_map/ppermute | solution.py:243
  35.8 6.8 %all-to-all-start = ((bf16[8,128,256]{2,1,0:T(8,128)(2,1)}), bf16[8,128,256]{2,1,0:T(8,128)(2,1)S(1)}, u32[]{:S(2)}, u32[]{:S(2)}) async-start(bf16[8,128,256]{2,1,0:T(8,128)(2,1)} %pad_maximum_fusion.1), calls=%async_computation | async-start | bytes 1048576 | tf_op jit(solution)/shard_map/all_to_all | solution.py:259
  43.9 4.2 %all_gather.28.refs_4_ = bf16[16,8,896]{2,1,0:T(8,128)(2,1)S(1)} all-gather(bf16[8,8,896]{2,1,0:T(8,128)(2,1)S(1)} %collective-permute-done.3), channel_id=1, replica_groups=mesh['x'=4,'z'=8,'core'=2,'mp'=8] {'core'}, dimensions={0}, use_global_device_ids=true | all-gather | bytes 344064 | tf_op jit(solution)/shard_map/all_gather | solution.py:288
  50.3 2.1 %all_gather.26.refs_2_ = bf16[32,8,896]{2,1,0:T(8,128)(2,1)S(1)} all-gather(bf16[16,8,896]{2,1,0:T(8,128)(2,1)S(1)} %collective-permute-done.1), channel_id=1, replica_groups=mesh['x'=4,'z'=8,'core'=2,'mp'=8] {'core'}, dimensions={0}, use_global_device_ids=true | all-gather | bytes 688128 | tf_op jit(solution)/shard_map/all_gather | solution.py:288
  52.4 2.3 %all_gather.27.refs_3_ = bf16[32,8,896]{2,1,0:T(8,128)(2,1)S(1)} all-gather(bf16[16,8,896]{2,1,0:T(8,128)(2,1)S(1)} %collective-permute-done.2), channel_id=1, replica_groups=mesh['x'=4,'z'=8,'core'=2,'mp'=8] {'core'}, dimensions={0}, use_global_device_ids=true | all-gather | bytes 688128 | tf_op jit(solution)/shard_map/all_gather | solution.py:288
  56.4 9.4 %all-to-all-done.qg_ref = bf16[8,128,256]{2,1,0:T(8,128)(2,1)S(1)} async-done(((bf16[8,128,256]{2,1,0:T(8,128)(2,1)}), bf16[8,128,256]{2,1,0:T(8,128)(2,1)S(1)}, u32[]{:S(2)}, u32[]{:S(2)}) %all-to-all-start) | async-done | bytes 524320 | tf_op jit(solution)/shard_map/all_to_all | solution.py:259
  65.7 4.0 %all-to-all-start.1 = ((bf16[64,8,896]{2,1,0:T(8,128)(2,1)}), bf16[64,8,896]{2,1,0:T(8,128)(2,1)S(1)}, u32[]{:S(2)}, u32[]{:S(2)}) async-start(bf16[64,8,896]{2,1,0:T(8,128)(2,1)} %choose.1), calls=%async_computation.1 | async-start | bytes 1835008 | tf_op jit(solution)/shard_map/all_to_all | solution.py:291
  69.8 13.1 %all-to-all-done.1 = bf16[64,8,896]{2,1,0:T(8,128)(2,1)S(1)} async-done(((bf16[64,8,896]{2,1,0:T(8,128)(2,1)}), bf16[64,8,896]{2,1,0:T(8,128)(2,1)S(1)}, u32[]{:S(2)}, u32[]{:S(2)}) %all-to-all-start.1) | async-done | bytes 917536 | tf_op jit(solution)/shard_map/all_to_all | solution.py:291
  84.1 3.4 %all-to-all-start.2 = ((bf16[16,8,896]{2,1,0:T(8,128)(2,1)}), bf16[16,8,896]{2,1,0:T(8,128)(2,1)S(1)}, u32[]{:S(2)}, u32[]{:S(2)}) async-start(bf16[16,8,896]{2,1,0:T(8,128)(2,1)} %gather_fusion), calls=%async_computation.2 | async-start | bytes 458752 | tf_op jit(solution)/shard_map/all_to_all | solution.py:294
  89.2 7.3 %all-to-all-done.2 = bf16[16,8,896]{2,1,0:T(8,128)(2,1)S(1)} async-done(((bf16[16,8,896]{2,1,0:T(8,128)(2,1)}), bf16[16,8,896]{2,1,0:T(8,128)(2,1)S(1)}, u32[]{:S(2)}, u32[]{:S(2)}) %all-to-all-start.2) | async-done | bytes 229408 | tf_op jit(solution)/shard_map/all_to_all | solution.py:294
  96.6 3.6 %copy-done.1 = bf16[17920,256]{1,0:T(8,128)(2,1)S(1)} copy-done((bf16[17920,256]{1,0:T(8,128)(2,1)S(1)}, bf16[17920,256]{1,0:T(8,128)(2,1)}, u32[]{:S(2)}) %copy-start.1) | copy-done | bytes 9175064
  100.2 13.2 %stretch.1 = (bf16[8,128,256]{2,1,0:T(8,128)(2,1)}, bf16[128,896]{1,0:T(8,128)(2,1)S(1)}) custom-call(bf16[128,896]{1,0:T(8,128)(2,1)S(1)} %bitcast.19, bf16[64,1792]{1,0:T(8,128)(2,1)S(1)} %copy-done.2, bf16[8,128,256]{2,1,0:T(8,128)(2,1)S(1)} %all-to-all-done.qg_ref, bf16[16,1120,256]{2,1,0:T(8,128)(2,1)S(1)} %bitcast.21), custom_call_target="tpu_custom_call" | custom-call | flops 7000000000 | bytes 11000000 | tf_op jit(solution)/shard_map/stretch/pallas_call | solution.py:150
  113.4 11.7 %all_to_all.25 = bf16[16,8,896]{2,1,0:T(8,128)(2,1)S(1)} all-to-all(bf16[16,8,896]{2,1,0:T(8,128)(2,1)S(1)} %bitcast.20), channel_id=1, replica_groups=mesh['x'=4,'z'=8,'core'=2,'mp'=8] {'mp'}, dimensions={0} | all-to-all | bytes 458752 | tf_op jit(solution)/shard_map/all_to_all | solution.py:301
  125.1 11.0 %all_gather.31.mine_ref = bf16[64,8,896]{2,1,0:T(8,128)(2,1)S(1)} all-gather(bf16[16,8,896]{2,1,0:T(8,128)(2,1)S(1)} %all_to_all.25), channel_id=1, replica_groups=mesh['x'=4,'z'=8,'core'=2,'mp'=8] {'x'}, dimensions={0}, use_global_device_ids=true | all-gather | bytes 1146880 | tf_op jit(solution)/shard_map/all_gather | solution.py:302
  136.1 8.6 %collective-permute-start.4 = (bf16[64,8,896]{2,1,0:T(8,128)(2,1)S(1)}, bf16[64,8,896]{2,1,0:T(8,128)(2,1)S(1)}, u32[]{:S(2)}, u32[]{:S(2)}) collective-permute-start(bf16[64,8,896]{2,1,0:T(8,128)(2,1)S(1)} %all_gather.31.mine_ref), channel_id=1, source_target_pairs={{0,8},{8,0},{1,9},{9,1},{2,10},{10,2},{3,11},{11,3},{4,12},{12,4},... | collective-permute-start | bytes 2752520 | tf_op jit(solution)/shard_map/ppermute | solution.py:303
  144.8 3.5 %all-to-all-start.3 = ((bf16[8,128,256]{2,1,0:T(8,128)(2,1)}), bf16[8,128,256]{2,1,0:T(8,128)(2,1)S(1)}, u32[]{:S(2)}, u32[]{:S(2)}) async-start(bf16[8,128,256]{2,1,0:T(8,128)(2,1)} %get-tuple-element.16), calls=%async_computation.3 | async-start | bytes 1048576 | tf_op jit(solution)/shard_map/all_to_all | solution.py:311
  150.1 6.0 %collective-permute-start.8 = (bf16[16,8,896]{2,1,0:T(8,128)(2,1)S(1)}, bf16[16,8,896]{2,1,0:T(8,128)(2,1)S(1)}, u32[]{:S(2)}, u32[]{:S(2)}) collective-permute-start(bf16[16,8,896]{2,1,0:T(8,128)(2,1)S(1)} %get-tuple-element.22), channel_id=1, source_target_pairs={{0,48},{8,88},{16,64},{24,104},{32,80},{40,120},{48,96},{56,8},{64... | collective-permute-start | bytes 688136 | tf_op jit(solution)/shard_map/ppermute | solution.py:243
  156.0 2.7 %collective-permute-start.7 = (bf16[16,8,896]{2,1,0:T(8,128)(2,1)S(1)}, bf16[16,8,896]{2,1,0:T(8,128)(2,1)S(1)}, u32[]{:S(2)}, u32[]{:S(2)}) collective-permute-start(bf16[16,8,896]{2,1,0:T(8,128)(2,1)S(1)} %get-tuple-element.21), channel_id=1, source_target_pairs={{0,32},{8,104},{16,48},{24,120},{32,64},{40,8},{48,80},{56,24},{64... | collective-permute-start | bytes 688136 | tf_op jit(solution)/shard_map/ppermute | solution.py:243
  160.9 5.8 %collective-permute-start.5 = (bf16[8,8,896]{2,1,0:T(8,128)(2,1)S(1)}, bf16[8,8,896]{2,1,0:T(8,128)(2,1)}, u32[]{:S(2)}, u32[]{:S(2)}) collective-permute-start(bf16[8,8,896]{2,1,0:T(8,128)(2,1)S(1)} %get-tuple-element.19), channel_id=1, source_target_pairs={{0,64},{8,72},{16,80},{24,88},{32,96},{40,104},{48,112},{56,120},{... | collective-permute-start | bytes 344072 | tf_op jit(solution)/shard_map/ppermute | solution.py:243
  166.7 2.9 %collective-permute-done.7 = bf16[16,8,896]{2,1,0:T(8,128)(2,1)S(1)} collective-permute-done((bf16[16,8,896]{2,1,0:T(8,128)(2,1)S(1)}, bf16[16,8,896]{2,1,0:T(8,128)(2,1)S(1)}, u32[]{:S(2)}, u32[]{:S(2)}) %collective-permute-start.7) | collective-permute-done | bytes 229408 | tf_op jit(solution)/shard_map/ppermute | solution.py:243
  169.6 6.4 %collective-permute-done.6 = bf16[16,8,896]{2,1,0:T(8,128)(2,1)S(1)} collective-permute-done((bf16[16,8,896]{2,1,0:T(8,128)(2,1)S(1)}, bf16[16,8,896]{2,1,0:T(8,128)(2,1)S(1)}, u32[]{:S(2)}, u32[]{:S(2)}) %collective-permute-start.6) | collective-permute-done | bytes 229408 | tf_op jit(solution)/shard_map/ppermute | solution.py:243
  (62 shorter events, 22.2 us)
Async XLA Ops:
  7.2 1.2 copy-start
  7.2 1.6 copy-start.6
  7.2 82.1 %all-gather.3.cloned.1.call-start = ((), (), s32[]{:S(2)}) async-start(), calls=%async_computation.5 | async-start | bytes 9748480 | tf_op jit(solution)/shard_map/all_gather | solution.py:254
  8.8 1.0 copy-start.5
  8.8 26.2 %copy-start.3 = (bf16[512,256]{1,0:T(8,128)(2,1)S(1)}, bf16[512,256]{1,0:T(8,128)(2,1)}, u32[]{:S(2)}) copy-start(bf16[512,256]{1,0:T(8,128)(2,1)} %param.15) | copy-start | bytes 786436
  8.8 26.2 %copy-start.4 = (bf16[512,256]{1,0:T(8,128)(2,1)S(1)}, bf16[512,256]{1,0:T(8,128)(2,1)}, u32[]{:S(2)}) copy-start(bf16[512,256]{1,0:T(8,128)(2,1)} %param.8) | copy-start | bytes 786436
  9.7 32.9 %copy-start.7 = (s32[512,2]{0,1:T(2,128)S(1)}, s32[512,2]{0,1:T(2,128)}, u32[]{:S(2)}) copy-start(s32[512,2]{0,1:T(2,128)} %param.12) | copy-start | bytes 12292
  18.2 29.9 %collective-permute-start = (bf16[16,8,896]{2,1,0:T(8,128)(2,1)S(1)}, bf16[16,8,896]{2,1,0:T(8,128)(2,1)S(1)}, u32[]{:S(2)}, u32[]{:S(2)}) collective-permute-start(bf16[16,8,896]{2,1,0:T(8,128)(2,1)S(1)} %all_gather.24.refs_0_), channel_id=1, source_target_pairs={{0,16},{8,120},{16,32},{24,8},{32,48},{40,24},{48,64},{56,40},{64,... | collective-permute-start | bytes 688136 | tf_op jit(solution)/shard_map/ppermute | solution.py:243
  23.5 26.7 %collective-permute-start.1 = (bf16[16,8,896]{2,1,0:T(8,128)(2,1)S(1)}, bf16[16,8,896]{2,1,0:T(8,128)(2,1)S(1)}, u32[]{:S(2)}, u32[]{:S(2)}) collective-permute-start(bf16[16,8,896]{2,1,0:T(8,128)(2,1)S(1)} %all_gather.24.refs_0_), channel_id=1, source_target_pairs={{0,32},{8,104},{16,48},{24,120},{32,64},{40,8},{48,80},{56,24},{64... | collective-permute-start | bytes 688136 | tf_op jit(solution)/shard_map/ppermute | solution.py:243
  25.7 26.7 %collective-permute-start.2 = (bf16[16,8,896]{2,1,0:T(8,128)(2,1)S(1)}, bf16[16,8,896]{2,1,0:T(8,128)(2,1)S(1)}, u32[]{:S(2)}, u32[]{:S(2)}) collective-permute-start(bf16[16,8,896]{2,1,0:T(8,128)(2,1)S(1)} %all_gather.24.refs_0_), channel_id=1, source_target_pairs={{0,48},{8,88},{16,64},{24,104},{32,80},{40,120},{48,96},{56,8},{64... | collective-permute-start | bytes 688136 | tf_op jit(solution)/shard_map/ppermute | solution.py:243
  27.6 16.3 %collective-permute-start.3 = (bf16[8,8,896]{2,1,0:T(8,128)(2,1)S(1)}, bf16[8,8,896]{2,1,0:T(8,128)(2,1)S(1)}, u32[]{:S(2)}, u32[]{:S(2)}) collective-permute-start(bf16[8,8,896]{2,1,0:T(8,128)(2,1)S(1)} %copy-done.5), channel_id=1, source_target_pairs={{0,64},{8,72},{16,80},{24,88},{32,96},{40,104},{48,112},{56,120},{... | collective-permute-start | bytes 344072 | tf_op jit(solution)/shard_map/ppermute | solution.py:243
  34.9 8.0 %copy-start.8 = (s32[512,2]{0,1:T(2,128)S(1)}, s32[512,2]{0,1:T(2,128)}, u32[]{:S(2)}) copy-start(s32[512,2]{0,1:T(2,128)} %param.11) | copy-start | bytes 12292
  35.8 29.9 %all-to-all-start = ((bf16[8,128,256]{2,1,0:T(8,128)(2,1)}), bf16[8,128,256]{2,1,0:T(8,128)(2,1)S(1)}, u32[]{:S(2)}, u32[]{:S(2)}) async-start(bf16[8,128,256]{2,1,0:T(8,128)(2,1)} %pad_maximum_fusion.1), calls=%async_computation | async-start | bytes 1048576 | tf_op jit(solution)/shard_map/all_to_all | solution.py:259
  56.4 40.2 %copy-start.2 = (bf16[64,1792]{1,0:T(8,128)(2,1)S(1)}, bf16[64,1792]{1,0:T(8,128)(2,1)}, u32[]{:S(2)}) copy-start(bf16[64,1792]{1,0:T(8,128)(2,1)} %kv_ref.1) | copy-start | bytes 688132
  65.7 17.1 %all-to-all-start.1 = ((bf16[64,8,896]{2,1,0:T(8,128)(2,1)}), bf16[64,8,896]{2,1,0:T(8,128)(2,1)S(1)}, u32[]{:S(2)}, u32[]{:S(2)}) async-start(bf16[64,8,896]{2,1,0:T(8,128)(2,1)} %choose.1), calls=%async_computation.1 | async-start | bytes 1835008 | tf_op jit(solution)/shard_map/all_to_all | solution.py:291
  84.1 12.5 %all-to-all-start.2 = ((bf16[16,8,896]{2,1,0:T(8,128)(2,1)}), bf16[16,8,896]{2,1,0:T(8,128)(2,1)S(1)}, u32[]{:S(2)}, u32[]{:S(2)}) async-start(bf16[16,8,896]{2,1,0:T(8,128)(2,1)} %gather_fusion), calls=%async_computation.2 | async-start | bytes 458752 | tf_op jit(solution)/shard_map/all_to_all | solution.py:294
  96.6 3.6 %copy-start.1 = (bf16[17920,256]{1,0:T(8,128)(2,1)S(1)}, bf16[17920,256]{1,0:T(8,128)(2,1)}, u32[]{:S(2)}) copy-start(bf16[17920,256]{1,0:T(8,128)(2,1)} %all-gather.3.cloned.1.call-done) | copy-start | bytes 27525124
  136.1 12.4 %collective-permute-start.4 = (bf16[64,8,896]{2,1,0:T(8,128)(2,1)S(1)}, bf16[64,8,896]{2,1,0:T(8,128)(2,1)S(1)}, u32[]{:S(2)}, u32[]{:S(2)}) collective-permute-start(bf16[64,8,896]{2,1,0:T(8,128)(2,1)S(1)} %all_gather.31.mine_ref), channel_id=1, source_target_pairs={{0,8},{8,0},{1,9},{9,1},{2,10},{10,2},{3,11},{11,3},{4,12},{12,4},... | collective-permute-start | bytes 2752520 | tf_op jit(solution)/shard_map/ppermute | solution.py:303
  144.8 33.3 %all-to-all-start.3 = ((bf16[8,128,256]{2,1,0:T(8,128)(2,1)}), bf16[8,128,256]{2,1,0:T(8,128)(2,1)S(1)}, u32[]{:S(2)}, u32[]{:S(2)}) async-start(bf16[8,128,256]{2,1,0:T(8,128)(2,1)} %get-tuple-element.16), calls=%async_computation.3 | async-start | bytes 1048576 | tf_op jit(solution)/shard_map/all_to_all | solution.py:311
  150.1 16.6 %collective-permute-start.8 = (bf16[16,8,896]{2,1,0:T(8,128)(2,1)S(1)}, bf16[16,8,896]{2,1,0:T(8,128)(2,1)S(1)}, u32[]{:S(2)}, u32[]{:S(2)}) collective-permute-start(bf16[16,8,896]{2,1,0:T(8,128)(2,1)S(1)} %get-tuple-element.22), channel_id=1, source_target_pairs={{0,48},{8,88},{16,64},{24,104},{32,80},{40,120},{48,96},{56,8},{64... | collective-permute-start | bytes 688136 | tf_op jit(solution)/shard_map/ppermute | solution.py:243
  156.0 13.6 %collective-permute-start.7 = (bf16[16,8,896]{2,1,0:T(8,128)(2,1)S(1)}, bf16[16,8,896]{2,1,0:T(8,128)(2,1)S(1)}, u32[]{:S(2)}, u32[]{:S(2)}) collective-permute-start(bf16[16,8,896]{2,1,0:T(8,128)(2,1)S(1)} %get-tuple-element.21), channel_id=1, source_target_pairs={{0,32},{8,104},{16,48},{24,120},{32,64},{40,8},{48,80},{56,24},{64... | collective-permute-start | bytes 688136 | tf_op jit(solution)/shard_map/ppermute | solution.py:243
  158.8 17.3 %collective-permute-start.6 = (bf16[16,8,896]{2,1,0:T(8,128)(2,1)S(1)}, bf16[16,8,896]{2,1,0:T(8,128)(2,1)S(1)}, u32[]{:S(2)}, u32[]{:S(2)}) collective-permute-start(bf16[16,8,896]{2,1,0:T(8,128)(2,1)S(1)} %get-tuple-element.20), channel_id=1, source_target_pairs={{0,16},{8,120},{16,32},{24,8},{32,48},{40,24},{48,64},{56,40},{64,... | collective-permute-start | bytes 688136 | tf_op jit(solution)/shard_map/ppermute | solution.py:243
  160.9 18.0 %collective-permute-start.5 = (bf16[8,8,896]{2,1,0:T(8,128)(2,1)S(1)}, bf16[8,8,896]{2,1,0:T(8,128)(2,1)}, u32[]{:S(2)}, u32[]{:S(2)}) collective-permute-start(bf16[8,8,896]{2,1,0:T(8,128)(2,1)S(1)} %get-tuple-element.19), channel_id=1, source_target_pairs={{0,64},{8,72},{16,80},{24,88},{32,96},{40,104},{48,112},{56,120},{... | collective-permute-start | bytes 344072 | tf_op jit(solution)/shard_map/ppermute | solution.py:243
  176.1 3.2 %collective-permute-start.9 = (bf16[8,8,896]{2,1,0:T(8,128)(2,1)S(1)}, bf16[8,8,896]{2,1,0:T(8,128)(2,1)S(1)}, u32[]{:S(2)}, u32[]{:S(2)}) collective-permute-start(bf16[8,8,896]{2,1,0:T(8,128)(2,1)S(1)} %fusion), channel_id=1, source_target_pairs={{0,8},{8,0},{1,9},{9,1},{2,10},{10,2},{3,11},{11,3},{4,12},{12,4},... | collective-permute-start | bytes 344072 | tf_op jit(solution)/shard_map/ppermute | solution.py:309
Sparse Core Ops, SparseCore 0:
  10.1 79.0 all-gather.2

commit v3 on v2

--- a/solution.py
+++ b/solution.py
@@ -1,3 +1,5 @@
+import functools
+
 import jax
 import jax.numpy as jnp
 from jax import lax
@@ -42,6 +44,7 @@
     packed_ref,
     out_ref,
     grad_ref,
+    enc_parts,
     enc_w,
     dec_w,
     encoded_ref,
@@ -51,43 +54,32 @@
     enc_sem,
     dec_sem,
 ):
-    enc_copies = []
-    for m in range(NM):
-        for part, (core, pair, skip, column) in enumerate(
-            ((0, 0, 0, 0), (0, 1, 0, 256), (1, 0, 128, 512), (1, 1, 0, 640))
-        ):
-            enc_copies.append(
-                pltpu.make_async_copy(
-                    packed_ref.at[
-                        core * NM + m,
-                        pl.ds(WIDTH + pair * ENC_ROWS, ENC_ROWS),
-                        pl.ds(skip, KV - skip),
-                    ],
-                    enc_w.at[pl.ds(m * ENC_ROWS, ENC_ROWS), pl.ds(column, KV - skip)],
-                    enc_sem.at[m, part],
-                )
-            )
-    for copy in enc_copies:
-        copy.start()
+    enc_copy = pltpu.make_async_copy(
+        packed_ref.at[:, pl.ds(WIDTH, 2 * ENC_ROWS), :], enc_parts, enc_sem
+    )
+    enc_copy.start()
     dec_copies = []
     for m in range(NM):
         group = []
         for core in range(NC):
-            for kind in range(2):
-                group.append(
-                    pltpu.make_async_copy(
-                        packed_ref.at[
-                            core * NM + m, pl.ds(0, WIDTH), pl.ds(kind * HEAD_DIM, HEAD_DIM)
-                        ],
-                        dec_w.at[m, :, pl.ds(kind * KV + core * HEAD_DIM, HEAD_DIM)],
-                        dec_sem.at[m, core, kind],
-                    )
+            group.append(
+                pltpu.make_async_copy(
+                    packed_ref.at[core * NM + m, pl.ds(0, WIDTH), :],
+                    dec_w.at[m, core],
+                    dec_sem.at[m, core],
                 )
+            )
         dec_copies.append(group)
+    enc_copy.wait()
+    for group in dec_copies:
         for copy in group:
             copy.start()
-    for copy in enc_copies:
-        copy.wait()
+    for m in range(NM):
+        at = slice(m * ENC_ROWS, (m + 1) * ENC_ROWS)
+        enc_w[at, :256] = enc_parts[m, :ENC_ROWS]
+        enc_w[at, 256:512] = enc_parts[m, ENC_ROWS:]
+        enc_w[at, 512:640] = enc_parts[NM + m, :ENC_ROWS, HEAD_DIM:]
+        enc_w[at, 640:] = enc_parts[NM + m, ENC_ROWS:]
 
     rows = rows_ref[...]
     query = dot(rows, enc_w[...], ((1,), (0,))).astype(jnp.bfloat16)
@@ -113,8 +105,9 @@
     for m in range(NM):
         for copy in dec_copies[m]:
             copy.wait()
-        both = dot(encoded, dec_w[m], ((1,), (0,))).astype(jnp.bfloat16)
-        keys, values = both[:, :KV], both[:, KV:]
+        pair = [dot(encoded, dec_w[m, h], ((1,), (0,))).astype(jnp.bfloat16) for h in range(2)]
+        keys = jnp.concatenate([both[:, :HEAD_DIM] for both in pair], axis=1)
+        values = jnp.concatenate([both[:, HEAD_DIM:] for both in pair], axis=1)
         q = stacked(qg_ref[m, :STRETCH, :])
         g = stacked(qg_ref[m, STRETCH:, :])
         weights = softmax(dot(q, keys, ((1,), (1,))) * SCALE)
@@ -124,11 +117,14 @@
         out_ref[m, STRETCH:, :] = beside(dot(grad_s, keys, ((1,), (0,))) * SCALE)
         grad_v = dot(low_w, g, ((0,), (0,))).astype(jnp.bfloat16)
         grad_k = (dot(grad_s, q, ((0,), (0,))) * SCALE).astype(jnp.bfloat16)
-        term = dot(jnp.concatenate([grad_k, grad_v], axis=1), dec_w[m], ((1,), (1,)))
-        if m == 0:
-            total_ref[...] = term
-        else:
-            total_ref[...] += term
+        for h in range(2):
+            cols = slice(h * HEAD_DIM, (h + 1) * HEAD_DIM)
+            grads = jnp.concatenate([grad_k[:, cols], grad_v[:, cols]], axis=1)
+            term = dot(grads, dec_w[m, h], ((1,), (1,)))
+            if m == 0 and h == 0:
+                total_ref[...] = term
+            else:
+                total_ref[...] += term
 
     grad_encoded = total_ref[...].astype(jnp.bfloat16)
     for h in range(ENC_HEADS):
@@ -153,19 +149,20 @@
             jax.ShapeDtypeStruct((NM, 2 * STRETCH, KV), jnp.bfloat16),
             jax.ShapeDtypeStruct((2 * STRETCH, WIDTH), jnp.bfloat16),
         ),
-        in_specs=[VMEM, VMEM, VMEM, pl.BlockSpec(memory_space=pl.ANY)],
+        in_specs=[VMEM, VMEM, VMEM, pl.BlockSpec(memory_space=pltpu.HBM)],
         out_specs=(VMEM, VMEM),
         scratch_shapes=[
+            pltpu.VMEM((NC * NM, 2 * ENC_ROWS, KV), jnp.bfloat16),
             pltpu.VMEM((WIDTH, WIDTH), jnp.bfloat16),
-            pltpu.VMEM((NM, WIDTH, 2 * KV), jnp.bfloat16),
+            pltpu.VMEM((NM, NC, WIDTH, KV), jnp.bfloat16),
             pltpu.VMEM((2 * STRETCH, WIDTH), jnp.bfloat16),
             pltpu.VMEM((2 * STRETCH, WIDTH), jnp.bfloat16),
             pltpu.VMEM((ENC_HEADS, 2 * STRETCH, STRETCH), jnp.float32),
             pltpu.VMEM((2 * STRETCH, WIDTH), jnp.float32),
-            pltpu.SemaphoreType.DMA((NM, 4)),
-            pltpu.SemaphoreType.DMA((NM, NC, 2)),
+            pltpu.SemaphoreType.DMA,
+            pltpu.SemaphoreType.DMA((NM, NC)),
         ],
-        compiler_params=pltpu.CompilerParams(vmem_limit_bytes=28 * 1024 * 1024),
+        compiler_params=pltpu.CompilerParams(vmem_limit_bytes=52 * 1024 * 1024),
         cost_estimate=pl.CostEstimate(
             flops=7_000_000_000, bytes_accessed=11_000_000, transcendentals=200_000
         ),
@@ -173,27 +170,30 @@
     )(rows, kv, qg, packed)
 
 
-def choose_kernel(ask_ref, *refs):
-    *parts, out_ref, all_ref = refs
+def choose_kernel(count, ask_ref, *refs):
+    parts, out_refs, all_ref = refs[:count], refs[count:-1], refs[-1]
     at = 0
     for part in parts:
         all_ref[at : at + part.shape[0]] = part[...]
         at += part.shape[0]
-
-    def copy(i, carry):
-        out_ref[i] = all_ref[ask_ref[i]]
-        return carry
-
-    lax.fori_loop(0, out_ref.shape[0], copy, 0, unroll=8)
+    for number, out_ref in enumerate(out_refs):
+
+        def copy(i, carry, number=number, out_ref=out_ref):
+            out_ref[i] = all_ref[ask_ref[number * REQ + i]]
+            return carry
+
+        lax.fori_loop(0, REQ, copy, 0, unroll=8)
 
 
 def choose_call(ask, parts):
+    outs = ask.shape[0] // REQ
+    total = sum(part.shape[0] for part in parts)
     return pl.pallas_call(
-        choose_kernel,
-        out_shape=jax.ShapeDtypeStruct((NX * REQ, SPAN, WIDTH), jnp.bfloat16),
+        functools.partial(choose_kernel, len(parts)),
+        out_shape=(jax.ShapeDtypeStruct((REQ, SPAN, WIDTH), jnp.bfloat16),) * outs,
         in_specs=[SMEM] + [VMEM] * len(parts),
-        out_specs=VMEM,
-        scratch_shapes=[pltpu.VMEM((NC * NZ * SLOTS, SPAN, WIDTH), jnp.bfloat16)],
+        out_specs=(VMEM,) * outs,
+        scratch_shapes=[pltpu.VMEM((total, SPAN, WIDTH), jnp.bfloat16)],
         compiler_params=pltpu.CompilerParams(vmem_limit_bytes=12 * 1024 * 1024),
         cost_estimate=pl.CostEstimate(flops=0, bytes_accessed=3_000_000, transcendentals=0),
         name="choose",
@@ -286,14 +286,18 @@
     chip = lax.all_gather(pool, "core", axis=0, tiled=True)
     came = [along_z(chip, k) for k in range(1, 4)] + [along_z(pool, 4)]
     parts = [chip] + [lax.all_gather(part, "core", axis=0, tiled=True) for part in came]
-    chosen = choose_call(of_column(ask, core), parts)
-    chosen, qg = lax.optimization_barrier((chosen, qg))
-    arrived = lax.all_to_all(chosen, "x", split_axis=0, concat_axis=0, tiled=True)
+    ask = of_column(ask, core).reshape(NX, REQ)
+    ask = jnp.take(ask, (x + jnp.arange(NX)) % NX, axis=0, mode="clip").reshape(NX * REQ)
+    chosen = choose_call(ask, parts)
+    arrived = [chosen[0]] + [
+        lax.ppermute(chosen[k], "x", [(i, (i + k) % NX) for i in range(NX)]) for k in range(1, NX)
+    ]
     my_x = lax.dynamic_slice(owner_x, (x, z, core, 0), (1, 1, 1, REQ)).reshape(REQ)
-    rows = jnp.take(arrived, my_x * REQ + jnp.arange(REQ), axis=0, mode="clip")
+    (rows,) = choose_call((x - my_x) % NX * REQ + jnp.arange(REQ), arrived)
+    rows, qg = lax.optimization_barrier((rows, qg))
     rows = lax.all_to_all(rows, "mp", split_axis=0, concat_axis=0, tiled=True)
     rows = rows.reshape(2 * STRETCH, WIDTH)
-    _, packed = lax.optimization_barrier((chosen, packed))
+    _, packed = lax.optimization_barrier((chosen[0], packed))
 
     out, grad_rows = stretch_call(rows, stretch_kv, qg, packed)
 
@@ -303,10 +307,13 @@
     every_beside = lax.ppermute(every, "core", swap)
     places = jnp.stack([of_column(place, core), of_column(place, 1 - core)])
     mine, *partial = place_call(places, every, every_beside)
-    partial = [along_z(part, k).astype(jnp.float32) for k, part in enumerate(partial, 1)]
+    partial = [along_z(part, k) for k, part in enumerate(partial, 1)]
+    partial = [part.astype(jnp.float32) for part in lax.optimization_barrier(partial)]
     ours = mine.astype(jnp.float32) + partial[3] + sum(part[:SLOTS] for part in partial[:3])
     theirs = sum(part[SLOTS:] for part in partial[:3]).astype(jnp.bfloat16)
-    grad_pool = ours + lax.ppermute(theirs, "core", swap).astype(jnp.float32)
+    theirs = lax.all_gather(theirs, "core", axis=0, tiled=False)
+    theirs = lax.dynamic_index_in_dim(theirs, 1 - core, 0, keepdims=False)
+    grad_pool = ours + theirs.astype(jnp.float32)
 
     out = lax.all_to_all(out, "mp", split_axis=0, concat_axis=0, tiled=True)
     attended = out[:, :STRETCH].reshape(NM * STRETCH, KV)

time: 189 us -> 185 us (0.979)
  starting transfers between devices: 61.6 us -> 74.4 us
  waiting for transfers between devices: 41.2 us -> 29.3 us
  local copies, waits for them, and re-layouts: 8.11 us -> 4.82 us
    all_to_all x1 -> x0, waiting for transfers between devices: 13.1 us -> none  [shards(): lax.all_to_all(chosen, 'x', split_axis=0, concat_axis=0, tiled=True)]
    all_gather x1, waiting for transfers between devices: 1.71 us -> 13.9 us  [shards(): packed = lax.all_gather(packed, ('core', 'mp'), axis=0, tiled=False)]
    all_to_all x1, waiting for transfers between devices: 9.35 us -> 0.01 us  [shards(): qg = lax.all_to_all(qg, 'mp', split_axis=0, concat_axis=0, tiled=True)]
    ppermute x1 -> x3, starting transfers between devices: 1.92 us -> 10.7 us  [shards(): lax.ppermute(chosen[k], 'x', [(i, (i + k) % NX) for i in range(NX)])]
    all_to_all x1, waiting for transfers between devices: 7.34 us -> 0.01 us  [shards(): rows = lax.all_to_all(rows, 'mp', split_axis=0, concat_axis=0, tiled=True)]
    ppermute x8, starting transfers between devices: 33.3 us -> 40.5 us  [along_z(): return lax.ppermute(values, ('z', 'core'), pairs)]
    ppermute x1 -> x3, waiting for transfers between devices: 0.45 us -> 6.75 us  [shards(): lax.ppermute(chosen[k], 'x', [(i, (i + k) % NX) for i in range(NX)])]
    all_gather x1, blocking collectives: 8.49 us -> 2.57 us  [shards(): chip = lax.all_gather(pool, 'core', axis=0, tiled=True)]
  transfers between devices with their start and end apart: 15 -> 16, of which waited for: 7 -> 5; matrix products, arithmetic and copies ran while one was open for 2% -> 3% of each run, Pallas kernels for 2% -> 2%
where the time goes in v3:
time: 185 us; the launch traced here: 184 us
  starting transfers between devices  74.4 us (40%)
  blocking collectives  40.8 us (22%)
  waiting for transfers between devices  29.3 us (16%)
  Pallas kernels  17.3 us (9%)
  between operations  14.4 us (8%)
  local copies, waits for them, and re-layouts  4.82 us (3%)
  other arithmetic  3.23 us (2%)
    ppermute x8, starting transfers between devices, along_z(): return lax.ppermute(values, ('z', 'core'), pairs)  40.5 us
    all_to_all x1, blocking collectives, shards(): lax.all_to_all(grad_rows, 'mp', split_axis=0, concat_axis=0, tiled=True)  15.3 us
    all_gather x1, waiting for transfers between devices, shards(): packed = lax.all_gather(packed, ('core', 'mp'), axis=0, tiled=False)  13.9 us
    pallas_call x1, Pallas kernels, stretch_call(): pl.pallas_call(stretch_kernel, out_shape=(jax.ShapeDtypeStruct((NM, 2 * S...  12.9 us
    all_gather x1, blocking collectives, shards(): every = lax.all_gather(grad_rows, 'x', axis=0, tiled=True)  12.6 us
    ppermute x3, starting transfers between devices, shards(): lax.ppermute(chosen[k], 'x', [(i, (i + k) % NX) for i in range(NX)])  10.7 us
    ppermute x8, waiting for transfers between devices, along_z(): return lax.ppermute(values, ('z', 'core'), pairs)  8.62 us
    all_gather x4, blocking collectives, shards(): lax.all_gather(part, 'core', axis=0, tiled=True)  8.33 us
  transfers between devices with their start and end apart: 16, of which 5 were waited for; matrix products, arithmetic and copies ran while one was open for 3% of the time, Pallas kernels for 2%

profile of v3, /device:TPU:1, one launch (start us, length us, event | category | flops | bytes accessed | tf_op | source)
XLA Modules:
  0.0 184.2 jit_solution(9063829373693954817)
XLA Ops:
  9.7 11.5 %collective-permute-start.3 = (bf16[8,8,896]{2,1,0:T(8,128)(2,1)S(1)}, bf16[8,8,896]{2,1,0:T(8,128)(2,1)S(1)}, u32[]{:S(2)}, u32[]{:S(2)}) collective-permute-start(bf16[8,8,896]{2,1,0:T(8,128)(2,1)S(1)} %copy-done.4), channel_id=1, source_target_pairs={{0,64},{8,72},{16,80},{24,88},{32,96},{40,104},{48,112},{56,120},{... | collective-permute-start | bytes 344072 | tf_op jit(solution)/shard_map/ppermute | solution.py:243
  21.2 2.6 %all_gather.30.refs_0_ = bf16[16,8,896]{2,1,0:T(8,128)(2,1)S(1)} all-gather(bf16[8,8,896]{2,1,0:T(8,128)(2,1)S(1)} %copy-done.4), channel_id=1, replica_groups=mesh['x'=4,'z'=8,'core'=2,'mp'=8] {'core'}, dimensions={0}, use_global_device_ids=true | all-gather | bytes 344064 | tf_op jit(solution)/shard_map/all_gather | solution.py:286
  25.7 7.3 %collective-permute-start.1 = (bf16[16,8,896]{2,1,0:T(8,128)(2,1)S(1)}, bf16[16,8,896]{2,1,0:T(8,128)(2,1)S(1)}, u32[]{:S(2)}, u32[]{:S(2)}) collective-permute-start(bf16[16,8,896]{2,1,0:T(8,128)(2,1)S(1)} %all_gather.30.refs_0_), channel_id=1, source_target_pairs={{0,32},{8,104},{16,48},{24,120},{32,64},{40,8},{48,80},{56,24},{64... | collective-permute-start | bytes 688136 | tf_op jit(solution)/shard_map/ppermute | solution.py:243
  33.0 2.2 %collective-permute-start = (bf16[16,8,896]{2,1,0:T(8,128)(2,1)S(1)}, bf16[16,8,896]{2,1,0:T(8,128)(2,1)S(1)}, u32[]{:S(2)}, u32[]{:S(2)}) collective-permute-start(bf16[16,8,896]{2,1,0:T(8,128)(2,1)S(1)} %all_gather.30.refs_0_), channel_id=1, source_target_pairs={{0,16},{8,120},{16,32},{24,8},{32,48},{40,24},{48,64},{56,40},{64,... | collective-permute-start | bytes 688136 | tf_op jit(solution)/shard_map/ppermute | solution.py:243
  36.1 6.8 %all-to-all-start = ((bf16[8,128,256]{2,1,0:T(8,128)(2,1)}), bf16[8,128,256]{2,1,0:T(8,128)(2,1)S(1)}, u32[]{:S(2)}, u32[]{:S(2)}) async-start(bf16[8,128,256]{2,1,0:T(8,128)(2,1)} %pad_maximum_fusion.1), calls=%async_computation | async-start | bytes 1048576 | tf_op jit(solution)/shard_map/all_to_all | solution.py:259
  46.8 2.1 %all_gather.33.refs_3_ = bf16[32,8,896]{2,1,0:T(8,128)(2,1)S(1)} all-gather(bf16[16,8,896]{2,1,0:T(8,128)(2,1)S(1)} %collective-permute-done.2), channel_id=1, replica_groups=mesh['x'=4,'z'=8,'core'=2,'mp'=8] {'core'}, dimensions={0}, use_global_device_ids=true | all-gather | bytes 688128 | tf_op jit(solution)/shard_map/all_gather | solution.py:288
  48.9 2.1 %all_gather.32.refs_2_ = bf16[32,8,896]{2,1,0:T(8,128)(2,1)S(1)} all-gather(bf16[16,8,896]{2,1,0:T(8,128)(2,1)S(1)} %collective-permute-done.1), channel_id=1, replica_groups=mesh['x'=4,'z'=8,'core'=2,'mp'=8] {'core'}, dimensions={0}, use_global_device_ids=true | all-gather | bytes 688128 | tf_op jit(solution)/shard_map/all_gather | solution.py:288
  51.0 2.1 %all_gather.31.refs_1_ = bf16[32,8,896]{2,1,0:T(8,128)(2,1)S(1)} all-gather(bf16[16,8,896]{2,1,0:T(8,128)(2,1)S(1)} %collective-permute-done), channel_id=1, replica_groups=mesh['x'=4,'z'=8,'core'=2,'mp'=8] {'core'}, dimensions={0}, use_global_device_ids=true | all-gather | bytes 688128 | tf_op jit(solution)/shard_map/all_gather | solution.py:288
  54.0 3.3 %collective-permute-start.4 = (bf16[16,8,896]{2,1,0:T(8,128)(2,1)S(1)}, bf16[16,8,896]{2,1,0:T(8,128)(2,1)S(1)}, u32[]{:S(2)}, u32[]{:S(2)}) collective-permute-start(bf16[16,8,896]{2,1,0:T(8,128)(2,1)S(1)} %get-tuple-element.22), channel_id=1, source_target_pairs={{0,128},{128,256},{256,384},{384,0},{1,129},{129,257},{257,385},{3... | collective-permute-start | bytes 688136 | tf_op jit(solution)/shard_map/ppermute | solution.py:293
  57.2 4.4 %collective-permute-start.5 = (bf16[16,8,896]{2,1,0:T(8,128)(2,1)S(1)}, bf16[16,8,896]{2,1,0:T(8,128)(2,1)S(1)}, u32[]{:S(2)}, u32[]{:S(2)}) collective-permute-start(bf16[16,8,896]{2,1,0:T(8,128)(2,1)S(1)} %get-tuple-element.23), channel_id=1, source_target_pairs={{0,256},{128,384},{256,0},{384,128},{1,257},{129,385},{257,1},{385... | collective-permute-start | bytes 688136 | tf_op jit(solution)/shard_map/ppermute | solution.py:293
  61.6 3.1 %collective-permute-start.6 = (bf16[16,8,896]{2,1,0:T(8,128)(2,1)S(1)}, bf16[16,8,896]{2,1,0:T(8,128)(2,1)S(1)}, u32[]{:S(2)}, u32[]{:S(2)}) collective-permute-start(bf16[16,8,896]{2,1,0:T(8,128)(2,1)S(1)} %get-tuple-element.24), channel_id=1, source_target_pairs={{0,384},{128,0},{256,128},{384,256},{1,385},{129,1},{257,129},{385... | collective-permute-start | bytes 688136 | tf_op jit(solution)/shard_map/ppermute | solution.py:293
  64.7 5.5 %collective-permute-done.5.refs_2_ = bf16[16,8,896]{2,1,0:T(8,128)(2,1)S(1)} collective-permute-done((bf16[16,8,896]{2,1,0:T(8,128)(2,1)S(1)}, bf16[16,8,896]{2,1,0:T(8,128)(2,1)S(1)}, u32[]{:S(2)}, u32[]{:S(2)}) %collective-permute-start.5) | collective-permute-done | bytes 229408 | tf_op jit(solution)/shard_map/ppermute | solution.py:293
  72.8 6.6 %all-to-all-start.1 = ((bf16[16,8,896]{2,1,0:T(8,128)(2,1)}), bf16[16,8,896]{2,1,0:T(8,128)(2,1)S(1)}, u32[]{:S(2)}, u32[]{:S(2)}) async-start(bf16[16,8,896]{2,1,0:T(8,128)(2,1)} %choose.3), calls=%async_computation.1 | async-start | bytes 458752 | tf_op jit(solution)/shard_map/all_to_all | solution.py:298
  79.4 13.9 %all-gather.4.cloned.1.call-done = bf16[17920,256]{1,0:T(8,128)(2,1)} async-done(((bf16[1120,256]{1,0:T(8,128)(2,1)}), bf16[17920,256]{1,0:T(8,128)(2,1)}) %all-gather.4.cloned.1.call-update) | async-done | bytes 9175056 | tf_op jit(solution)/shard_map/all_gather | solution.py:254
  93.3 12.9 %stretch.1 = (bf16[8,128,256]{2,1,0:T(8,128)(2,1)}, bf16[128,896]{1,0:T(8,128)(2,1)S(1)}) custom-call(bf16[128,896]{1,0:T(8,128)(2,1)S(1)} %bitcast.22, bf16[64,1792]{1,0:T(8,128)(2,1)S(1)} %copy-done.1, bf16[8,128,256]{2,1,0:T(8,128)(2,1)S(1)} %all-to-all-done.qg_ref, bf16[16,1120,256]{2,1,0:T(8,128)(2,1)} %bitcast.32), custom_call_target="tpu_custom_call" | custom-call | flops 7000000000 | bytes 11000000 | tf_op jit(solution)/shard_map/stretch/pallas_call | solution.py:146
  106.2 15.3 %all_to_all.20 = bf16[16,8,896]{2,1,0:T(8,128)(2,1)S(1)} all-to-all(bf16[16,8,896]{2,1,0:T(8,128)(2,1)S(1)} %bitcast.23), channel_id=1, replica_groups=mesh['x'=4,'z'=8,'core'=2,'mp'=8] {'mp'}, dimensions={0} | all-to-all | bytes 458752 | tf_op jit(solution)/shard_map/all_to_all | solution.py:305
  121.6 12.6 %all_gather.37.mine_ref = bf16[64,8,896]{2,1,0:T(8,128)(2,1)S(1)} all-gather(bf16[16,8,896]{2,1,0:T(8,128)(2,1)S(1)} %all_to_all.20), channel_id=1, replica_groups=mesh['x'=4,'z'=8,'core'=2,'mp'=8] {'x'}, dimensions={0}, use_global_device_ids=true | all-gather | bytes 1146880 | tf_op jit(solution)/shard_map/all_gather | solution.py:306
  134.1 5.6 %collective-permute-start.7 = (bf16[64,8,896]{2,1,0:T(8,128)(2,1)S(1)}, bf16[64,8,896]{2,1,0:T(8,128)(2,1)S(1)}, u32[]{:S(2)}, u32[]{:S(2)}) collective-permute-start(bf16[64,8,896]{2,1,0:T(8,128)(2,1)S(1)} %all_gather.37.mine_ref), channel_id=1, source_target_pairs={{0,8},{8,0},{1,9},{9,1},{2,10},{10,2},{3,11},{11,3},{4,12},{12,4},... | collective-permute-start | bytes 2752520 | tf_op jit(solution)/shard_map/ppermute | solution.py:307
  139.7 4.2 %all-to-all-start.2 = ((bf16[8,128,256]{2,1,0:T(8,128)(2,1)}), bf16[8,128,256]{2,1,0:T(8,128)(2,1)}, u32[]{:S(2)}, u32[]{:S(2)}) async-start(bf16[8,128,256]{2,1,0:T(8,128)(2,1)} %get-tuple-element.28), calls=%async_computation.2 | async-start | bytes 1048576 | tf_op jit(solution)/shard_map/all_to_all | solution.py:318
  144.1 2.2 %place.1 = (bf16[8,8,896]{2,1,0:T(8,128)(2,1)S(1)}, bf16[16,8,896]{2,1,0:T(8,128)(2,1)S(1)}, bf16[16,8,896]{2,1,0:T(8,128)(2,1)S(1)}, bf16[16,8,896]{2,1,0:T(8,128)(2,1)S(1)}, bf16[8,8,896]{2,1,0:T(8,128)(2,1)}) custom-call(s32[2,64]{1,0:T(2,128)S(1)} %pad_add_fusion.place_ref, bf16[64,8,896]{2,1,0:T(8,128)(2,1)S(1)} %all_gather.37.mine_ref, ...), custom_call_target="tpu_custom_call" | custom-call | flops 1000000 | bytes 3000000 | tf_op jit(solution)/shard_map/place/pallas_call | solution.py:221
  146.3 7.7 %collective-permute-start.11 = (bf16[8,8,896]{2,1,0:T(8,128)(2,1)}, bf16[8,8,896]{2,1,0:T(8,128)(2,1)S(1)}, u32[]{:S(2)}, u32[]{:S(2)}) collective-permute-start(bf16[8,8,896]{2,1,0:T(8,128)(2,1)} %get-tuple-element.34), channel_id=1, source_target_pairs={{0,64},{8,72},{16,80},{24,88},{32,96},{40,104},{48,112},{56,120},{... | collective-permute-start | bytes 344072 | tf_op jit(solution)/shard_map/ppermute | solution.py:243
  158.0 6.0 %collective-permute-start.10 = (bf16[16,8,896]{2,1,0:T(8,128)(2,1)S(1)}, bf16[16,8,896]{2,1,0:T(8,128)(2,1)S(1)}, u32[]{:S(2)}, u32[]{:S(2)}) collective-permute-start(bf16[16,8,896]{2,1,0:T(8,128)(2,1)S(1)} %get-tuple-element.33), channel_id=1, source_target_pairs={{0,48},{8,88},{16,64},{24,104},{32,80},{40,120},{48,96},{56,8},{64... | collective-permute-start | bytes 688136 | tf_op jit(solution)/shard_map/ppermute | solution.py:243
  165.9 3.1 %collective-permute-done.9 = bf16[16,8,896]{2,1,0:T(8,128)(2,1)S(1)} collective-permute-done((bf16[16,8,896]{2,1,0:T(8,128)(2,1)S(1)}, bf16[16,8,896]{2,1,0:T(8,128)(2,1)S(1)}, u32[]{:S(2)}, u32[]{:S(2)}) %collective-permute-start.9) | collective-permute-done | bytes 229408 | tf_op jit(solution)/shard_map/ppermute | solution.py:243
  169.0 5.5 %collective-permute-done.10 = bf16[16,8,896]{2,1,0:T(8,128)(2,1)S(1)} collective-permute-done((bf16[16,8,896]{2,1,0:T(8,128)(2,1)S(1)}, bf16[16,8,896]{2,1,0:T(8,128)(2,1)S(1)}, u32[]{:S(2)}, u32[]{:S(2)}) %collective-permute-start.10) | collective-permute-done | bytes 229408 | tf_op jit(solution)/shard_map/ppermute | solution.py:243
  (64 shorter events, 21.3 us)
Async XLA Ops:
  7.2 1.2 copy-start
  7.2 1.6 copy-start.5
  7.2 86.1 %all-gather.4.cloned.1.call-start = ((), (), s32[]{:S(2)}) async-start(), calls=%async_computation.4 | async-start | bytes 9748480 | tf_op jit(solution)/shard_map/all_gather | solution.py:254
  8.8 1.0 copy-start.4
  8.8 26.4 %copy-start.2 = (bf16[512,256]{1,0:T(8,128)(2,1)S(1)}, bf16[512,256]{1,0:T(8,128)(2,1)}, u32[]{:S(2)}) copy-start(bf16[512,256]{1,0:T(8,128)(2,1)} %param.15) | copy-start | bytes 786436
  8.8 26.4 %copy-start.3 = (bf16[512,256]{1,0:T(8,128)(2,1)S(1)}, bf16[512,256]{1,0:T(8,128)(2,1)}, u32[]{:S(2)}) copy-start(bf16[512,256]{1,0:T(8,128)(2,1)} %param.8) | copy-start | bytes 786436
  9.7 33.2 %copy-start.6 = (s32[512,2]{0,1:T(2,128)S(1)}, s32[512,2]{0,1:T(2,128)}, u32[]{:S(2)}) copy-start(s32[512,2]{0,1:T(2,128)} %param.11) | copy-start | bytes 12292
  9.7 35.1 %collective-permute-start.3 = (bf16[8,8,896]{2,1,0:T(8,128)(2,1)S(1)}, bf16[8,8,896]{2,1,0:T(8,128)(2,1)S(1)}, u32[]{:S(2)}, u32[]{:S(2)}) collective-permute-start(bf16[8,8,896]{2,1,0:T(8,128)(2,1)S(1)} %copy-done.4), channel_id=1, source_target_pairs={{0,64},{8,72},{16,80},{24,88},{32,96},{40,104},{48,112},{56,120},{... | collective-permute-start | bytes 344072 | tf_op jit(solution)/shard_map/ppermute | solution.py:243
  23.8 23.0 %collective-permute-start.2 = (bf16[16,8,896]{2,1,0:T(8,128)(2,1)S(1)}, bf16[16,8,896]{2,1,0:T(8,128)(2,1)S(1)}, u32[]{:S(2)}, u32[]{:S(2)}) collective-permute-start(bf16[16,8,896]{2,1,0:T(8,128)(2,1)S(1)} %all_gather.30.refs_0_), channel_id=1, source_target_pairs={{0,48},{8,88},{16,64},{24,104},{32,80},{40,120},{48,96},{56,8},{64... | collective-permute-start | bytes 688136 | tf_op jit(solution)/shard_map/ppermute | solution.py:243
  25.7 23.2 %collective-permute-start.1 = (bf16[16,8,896]{2,1,0:T(8,128)(2,1)S(1)}, bf16[16,8,896]{2,1,0:T(8,128)(2,1)S(1)}, u32[]{:S(2)}, u32[]{:S(2)}) collective-permute-start(bf16[16,8,896]{2,1,0:T(8,128)(2,1)S(1)} %all_gather.30.refs_0_), channel_id=1, source_target_pairs={{0,32},{8,104},{16,48},{24,120},{32,64},{40,8},{48,80},{56,24},{64... | collective-permute-start | bytes 688136 | tf_op jit(solution)/shard_map/ppermute | solution.py:243
  33.0 18.0 %collective-permute-start = (bf16[16,8,896]{2,1,0:T(8,128)(2,1)S(1)}, bf16[16,8,896]{2,1,0:T(8,128)(2,1)S(1)}, u32[]{:S(2)}, u32[]{:S(2)}) collective-permute-start(bf16[16,8,896]{2,1,0:T(8,128)(2,1)S(1)} %all_gather.30.refs_0_), channel_id=1, source_target_pairs={{0,16},{8,120},{16,32},{24,8},{32,48},{40,24},{48,64},{56,40},{64,... | collective-permute-start | bytes 688136 | tf_op jit(solution)/shard_map/ppermute | solution.py:243
  35.2 8.0 %copy-start.7 = (s32[512,2]{0,1:T(2,128)S(1)}, s32[512,2]{0,1:T(2,128)}, u32[]{:S(2)}) copy-start(s32[512,2]{0,1:T(2,128)} %param.12) | copy-start | bytes 12292
  36.1 36.7 %all-to-all-start = ((bf16[8,128,256]{2,1,0:T(8,128)(2,1)}), bf16[8,128,256]{2,1,0:T(8,128)(2,1)S(1)}, u32[]{:S(2)}, u32[]{:S(2)}) async-start(bf16[8,128,256]{2,1,0:T(8,128)(2,1)} %pad_maximum_fusion.1), calls=%async_computation | async-start | bytes 1048576 | tf_op jit(solution)/shard_map/all_to_all | solution.py:259
  54.0 39.4 %copy-start.1 = (bf16[64,1792]{1,0:T(8,128)(2,1)S(1)}, bf16[64,1792]{1,0:T(8,128)(2,1)}, u32[]{:S(2)}) copy-start(bf16[64,1792]{1,0:T(8,128)(2,1)} %kv_ref.1) | copy-start | bytes 688132
  54.0 10.7 %collective-permute-start.4 = (bf16[16,8,896]{2,1,0:T(8,128)(2,1)S(1)}, bf16[16,8,896]{2,1,0:T(8,128)(2,1)S(1)}, u32[]{:S(2)}, u32[]{:S(2)}) collective-permute-start(bf16[16,8,896]{2,1,0:T(8,128)(2,1)S(1)} %get-tuple-element.22), channel_id=1, source_target_pairs={{0,128},{128,256},{256,384},{384,0},{1,129},{129,257},{257,385},{3... | collective-permute-start | bytes 688136 | tf_op jit(solution)/shard_map/ppermute | solution.py:293
  57.2 12.9 %collective-permute-start.5 = (bf16[16,8,896]{2,1,0:T(8,128)(2,1)S(1)}, bf16[16,8,896]{2,1,0:T(8,128)(2,1)S(1)}, u32[]{:S(2)}, u32[]{:S(2)}) collective-permute-start(bf16[16,8,896]{2,1,0:T(8,128)(2,1)S(1)} %get-tuple-element.23), channel_id=1, source_target_pairs={{0,256},{128,384},{256,0},{384,128},{1,257},{129,385},{257,1},{385... | collective-permute-start | bytes 688136 | tf_op jit(solution)/shard_map/ppermute | solution.py:293
  61.6 9.9 %collective-permute-start.6 = (bf16[16,8,896]{2,1,0:T(8,128)(2,1)S(1)}, bf16[16,8,896]{2,1,0:T(8,128)(2,1)S(1)}, u32[]{:S(2)}, u32[]{:S(2)}) collective-permute-start(bf16[16,8,896]{2,1,0:T(8,128)(2,1)S(1)} %get-tuple-element.24), channel_id=1, source_target_pairs={{0,384},{128,0},{256,128},{384,256},{1,385},{129,1},{257,129},{385... | collective-permute-start | bytes 688136 | tf_op jit(solution)/shard_map/ppermute | solution.py:293
  72.8 20.5 %all-to-all-start.1 = ((bf16[16,8,896]{2,1,0:T(8,128)(2,1)}), bf16[16,8,896]{2,1,0:T(8,128)(2,1)S(1)}, u32[]{:S(2)}, u32[]{:S(2)}) async-start(bf16[16,8,896]{2,1,0:T(8,128)(2,1)} %choose.3), calls=%async_computation.1 | async-start | bytes 458752 | tf_op jit(solution)/shard_map/all_to_all | solution.py:298
  134.1 9.9 %collective-permute-start.7 = (bf16[64,8,896]{2,1,0:T(8,128)(2,1)S(1)}, bf16[64,8,896]{2,1,0:T(8,128)(2,1)S(1)}, u32[]{:S(2)}, u32[]{:S(2)}) collective-permute-start(bf16[64,8,896]{2,1,0:T(8,128)(2,1)S(1)} %all_gather.37.mine_ref), channel_id=1, source_target_pairs={{0,8},{8,0},{1,9},{9,1},{2,10},{10,2},{3,11},{11,3},{4,12},{12,4},... | collective-permute-start | bytes 2752520 | tf_op jit(solution)/shard_map/ppermute | solution.py:307
  139.7 24.3 %all-to-all-start.2 = ((bf16[8,128,256]{2,1,0:T(8,128)(2,1)}), bf16[8,128,256]{2,1,0:T(8,128)(2,1)}, u32[]{:S(2)}, u32[]{:S(2)}) async-start(bf16[8,128,256]{2,1,0:T(8,128)(2,1)} %get-tuple-element.28), calls=%async_computation.2 | async-start | bytes 1048576 | tf_op jit(solution)/shard_map/all_to_all | solution.py:318
  146.3 19.6 %collective-permute-start.11 = (bf16[8,8,896]{2,1,0:T(8,128)(2,1)}, bf16[8,8,896]{2,1,0:T(8,128)(2,1)S(1)}, u32[]{:S(2)}, u32[]{:S(2)}) collective-permute-start(bf16[8,8,896]{2,1,0:T(8,128)(2,1)} %get-tuple-element.34), channel_id=1, source_target_pairs={{0,64},{8,72},{16,80},{24,88},{32,96},{40,104},{48,112},{56,120},{... | collective-permute-start | bytes 344072 | tf_op jit(solution)/shard_map/ppermute | solution.py:243
  154.0 11.9 %collective-permute-start.8 = (bf16[16,8,896]{2,1,0:T(8,128)(2,1)S(1)}, bf16[16,8,896]{2,1,0:T(8,128)(2,1)S(1)}, u32[]{:S(2)}, u32[]{:S(2)}) collective-permute-start(bf16[16,8,896]{2,1,0:T(8,128)(2,1)S(1)} %get-tuple-element.31), channel_id=1, source_target_pairs={{0,16},{8,120},{16,32},{24,8},{32,48},{40,24},{48,64},{56,40},{64,... | collective-permute-start | bytes 688136 | tf_op jit(solution)/shard_map/ppermute | solution.py:243
  156.1 13.0 %collective-permute-start.9 = (bf16[16,8,896]{2,1,0:T(8,128)(2,1)S(1)}, bf16[16,8,896]{2,1,0:T(8,128)(2,1)S(1)}, u32[]{:S(2)}, u32[]{:S(2)}) collective-permute-start(bf16[16,8,896]{2,1,0:T(8,128)(2,1)S(1)} %get-tuple-element.32), channel_id=1, source_target_pairs={{0,32},{8,104},{16,48},{24,120},{32,64},{40,8},{48,80},{56,24},{64... | collective-permute-start | bytes 688136 | tf_op jit(solution)/shard_map/ppermute | solution.py:243
  158.0 16.5 %collective-permute-start.10 = (bf16[16,8,896]{2,1,0:T(8,128)(2,1)S(1)}, bf16[16,8,896]{2,1,0:T(8,128)(2,1)S(1)}, u32[]{:S(2)}, u32[]{:S(2)}) collective-permute-start(bf16[16,8,896]{2,1,0:T(8,128)(2,1)S(1)} %get-tuple-element.33), channel_id=1, source_target_pairs={{0,48},{8,88},{16,64},{24,104},{32,80},{40,120},{48,96},{56,8},{64... | collective-permute-start | bytes 688136 | tf_op jit(solution)/shard_map/ppermute | solution.py:243
Sparse Core Ops, SparseCore 0:
  10.1 83.1 all-gather.3

commit v4 on v3

--- a/solution.py
+++ b/solution.py
@@ -235,6 +235,24 @@
     )(place, mine, other)
 
 
+def join_kernel(core_ref, mine_ref, other_ref, out_ref):
+    core = core_ref[0]
+    out_ref[pl.ds(core * SLOTS, SLOTS)] = mine_ref[...]
+    out_ref[pl.ds((1 - core) * SLOTS, SLOTS)] = other_ref[...]
+
+
+def join_call(core, mine, other):
+    return pl.pallas_call(
+        join_kernel,
+        out_shape=jax.ShapeDtypeStruct((NC * SLOTS, SPAN, WIDTH), jnp.bfloat16),
+        in_specs=[SMEM, VMEM, VMEM],
+        out_specs=VMEM,
+        compiler_params=pltpu.CompilerParams(vmem_limit_bytes=4 * 1024 * 1024),
+        cost_estimate=pl.CostEstimate(flops=0, bytes_accessed=460_000, transcendentals=0),
+        name="join",
+    )(core, mine, other)
+
+
 def along_z(values, k):
     index = [(z, core) for z in range(NZ) for core in range(NC)]
     pairs = [
@@ -283,8 +301,10 @@
     def of_column(values, which):
         return lax.dynamic_slice(values, (0, z, which, 0), (NX, 1, 1, REQ)).reshape(NX * REQ)
 
-    chip = lax.all_gather(pool, "core", axis=0, tiled=True)
-    came = [along_z(chip, k) for k in range(1, 4)] + [along_z(pool, 4)]
+    beside = lax.ppermute(pool, "core", swap)
+    chip = join_call(core.reshape(1).astype(jnp.int32), pool, beside)
+    own_pool, _ = lax.optimization_barrier((pool, chip))
+    came = [along_z(chip, k) for k in range(1, 4)] + [along_z(own_pool, 4)]
     parts = [chip] + [lax.all_gather(part, "core", axis=0, tiled=True) for part in came]
     ask = of_column(ask, core).reshape(NX, REQ)
     ask = jnp.take(ask, (x + jnp.arange(NX)) % NX, axis=0, mode="clip").reshape(NX * REQ)

time: 185 us -> 181 us (0.978)
  waiting for transfers between devices: 29.3 us -> 24.6 us
  starting transfers between devices: 74.4 us -> 78.8 us
  blocking collectives: 40.8 us -> 36.9 us
    all_gather x1, waiting for transfers between devices: 13.9 us -> 0.35 us  [shards(): packed = lax.all_gather(packed, ('core', 'mp'), axis=0, tiled=False)]
    ppermute x0 -> x1, starting transfers between devices: none -> 8.79 us  [shards(): beside = lax.ppermute(pool, 'core', swap)]
    all_to_all x1, waiting for transfers between devices: 0.01 us -> 8.52 us  [shards(): rows = lax.all_to_all(rows, 'mp', split_axis=0, concat_axis=0, tiled=True)]
    ppermute x8, starting transfers between devices: 40.5 us -> 36.7 us  [along_z(): return lax.ppermute(values, ('z', 'core'), pairs)]
    all_to_all x1, blocking collectives: 15.3 us -> 11.8 us  [shards(): lax.all_to_all(grad_rows, 'mp', split_axis=0, concat_axis=0, tiled=True)]
    all_to_all x1, starting transfers between devices: 6.82 us -> 3.49 us  [shards(): qg = lax.all_to_all(qg, 'mp', split_axis=0, concat_axis=0, tiled=True)]
    all_gather x1 -> x0, blocking collectives: 2.57 us -> none  [shards(): chip = lax.all_gather(pool, 'core', axis=0, tiled=True)]
    ppermute x1, starting transfers between devices: 5.59 us -> 8.04 us  [shards(): every_beside = lax.ppermute(every, 'core', swap)]
  transfers between devices with their start and end apart: 16 -> 17, of which waited for: 5 -> 10; matrix products, arithmetic and copies ran while one was open for 3% -> 3% of each run, Pallas kernels for 2% -> 2%
where the time goes in v4:
time: 181 us; the launch traced here: 180 us
  starting transfers between devices  78.8 us (44%)
  blocking collectives  36.9 us (20%)
  waiting for transfers between devices  24.6 us (14%)
  Pallas kernels  17.3 us (10%)
  between operations  14.5 us (8%)
  local copies, waits for them, and re-layouts  4.82 us (3%)
  other arithmetic  3.22 us (2%)
    ppermute x8, starting transfers between devices, along_z(): return lax.ppermute(values, ('z', 'core'), pairs)  36.7 us
    all_gather x1, blocking collectives, shards(): every = lax.all_gather(grad_rows, 'x', axis=0, tiled=True)  13 us
    pallas_call x1, Pallas kernels, stretch_call(): pl.pallas_call(stretch_kernel, out_shape=(jax.ShapeDtypeStruct((NM, 2 * S...  12.9 us
    all_to_all x1, blocking collectives, shards(): lax.all_to_all(grad_rows, 'mp', split_axis=0, concat_axis=0, tiled=True)  11.8 us
    ppermute x3, starting transfers between devices, shards(): lax.ppermute(chosen[k], 'x', [(i, (i + k) % NX) for i in range(NX)])  10.7 us
    all_gather x4, blocking collectives, shards(): lax.all_gather(part, 'core', axis=0, tiled=True)  9.73 us
    ppermute x8, waiting for transfers between devices, along_z(): return lax.ppermute(values, ('z', 'core'), pairs)  9.11 us
    ppermute x1, starting transfers between devices, shards(): beside = lax.ppermute(pool, 'core', swap)  8.79 us
  transfers between devices with their start and end apart: 17, of which 10 were waited for; matrix products, arithmetic and copies ran while one was open for 3% of the time, Pallas kernels for 2%

profile of v4, /device:TPU:1, one launch (start us, length us, event | category | flops | bytes accessed | tf_op | source)
XLA Modules:
  0.0 180.1 jit_solution(10861330477796752813)
XLA Ops:
  9.7 8.8 %collective-permute-start = (bf16[8,8,896]{2,1,0:T(8,128)(2,1)S(1)}, bf16[8,8,896]{2,1,0:T(8,128)(2,1)S(1)}, u32[]{:S(2)}, u32[]{:S(2)}) collective-permute-start(bf16[8,8,896]{2,1,0:T(8,128)(2,1)S(1)} %copy-done.1), channel_id=1, source_target_pairs={{0,8},{8,0},{1,9},{9,1},{2,10},{10,2},{3,11},{11,3},{4,12},{12,4},... | collective-permute-start | bytes 344072 | tf_op jit(solution)/shard_map/ppermute | solution.py:304
  19.4 3.5 %all-to-all-start = ((bf16[8,128,256]{2,1,0:T(8,128)(2,1)}), bf16[8,128,256]{2,1,0:T(8,128)(2,1)S(1)}, u32[]{:S(2)}, u32[]{:S(2)}) async-start(bf16[8,128,256]{2,1,0:T(8,128)(2,1)} %pad_maximum_fusion.1), calls=%async_computation | async-start | bytes 1048576 | tf_op jit(solution)/shard_map/all_to_all | solution.py:277
  24.1 8.6 %collective-permute-start.3 = (bf16[16,8,896]{2,1,0:T(8,128)(2,1)S(1)}, bf16[16,8,896]{2,1,0:T(8,128)(2,1)S(1)}, u32[]{:S(2)}, u32[]{:S(2)}) collective-permute-start(bf16[16,8,896]{2,1,0:T(8,128)(2,1)S(1)} %join.1.refs_0_), channel_id=1, source_target_pairs={{0,48},{8,88},{16,64},{24,104},{32,80},{40,120},{48,96},{56,8},{64... | collective-permute-start | bytes 688136 | tf_op jit(solution)/shard_map/ppermute | solution.py:261
  34.7 7.3 %collective-permute-start.2 = (bf16[16,8,896]{2,1,0:T(8,128)(2,1)S(1)}, bf16[16,8,896]{2,1,0:T(8,128)(2,1)S(1)}, u32[]{:S(2)}, u32[]{:S(2)}) collective-permute-start(bf16[16,8,896]{2,1,0:T(8,128)(2,1)S(1)} %join.1.refs_0_), channel_id=1, source_target_pairs={{0,32},{8,104},{16,48},{24,120},{32,64},{40,8},{48,80},{56,24},{64... | collective-permute-start | bytes 688136 | tf_op jit(solution)/shard_map/ppermute | solution.py:261
  42.7 2.2 %collective-permute-start.1 = (bf16[16,8,896]{2,1,0:T(8,128)(2,1)S(1)}, bf16[16,8,896]{2,1,0:T(8,128)(2,1)S(1)}, u32[]{:S(2)}, u32[]{:S(2)}) collective-permute-start(bf16[16,8,896]{2,1,0:T(8,128)(2,1)S(1)} %join.1.refs_0_), channel_id=1, source_target_pairs={{0,16},{8,120},{16,32},{24,8},{32,48},{40,24},{48,64},{56,40},{64,... | collective-permute-start | bytes 688136 | tf_op jit(solution)/shard_map/ppermute | solution.py:261
  52.9 3.4 %all_gather.27.refs_1_ = bf16[32,8,896]{2,1,0:T(8,128)(2,1)S(1)} all-gather(bf16[16,8,896]{2,1,0:T(8,128)(2,1)S(1)} %collective-permute-done.1), channel_id=1, replica_groups=mesh['x'=4,'z'=8,'core'=2,'mp'=8] {'core'}, dimensions={0}, use_global_device_ids=true | all-gather | bytes 688128 | tf_op jit(solution)/shard_map/all_gather | solution.py:308
  57.1 3.3 %collective-permute-start.5 = (bf16[16,8,896]{2,1,0:T(8,128)(2,1)S(1)}, bf16[16,8,896]{2,1,0:T(8,128)(2,1)S(1)}, u32[]{:S(2)}, u32[]{:S(2)}) collective-permute-start(bf16[16,8,896]{2,1,0:T(8,128)(2,1)S(1)} %get-tuple-element.24), channel_id=1, source_target_pairs={{0,128},{128,256},{256,384},{384,0},{1,129},{129,257},{257,385},{3... | collective-permute-start | bytes 688136 | tf_op jit(solution)/shard_map/ppermute | solution.py:313
  60.4 4.4 %collective-permute-start.6 = (bf16[16,8,896]{2,1,0:T(8,128)(2,1)S(1)}, bf16[16,8,896]{2,1,0:T(8,128)(2,1)S(1)}, u32[]{:S(2)}, u32[]{:S(2)}) collective-permute-start(bf16[16,8,896]{2,1,0:T(8,128)(2,1)S(1)} %get-tuple-element.25), channel_id=1, source_target_pairs={{0,256},{128,384},{256,0},{384,128},{1,257},{129,385},{257,1},{385... | collective-permute-start | bytes 688136 | tf_op jit(solution)/shard_map/ppermute | solution.py:313
  64.8 3.1 %collective-permute-start.7 = (bf16[16,8,896]{2,1,0:T(8,128)(2,1)S(1)}, bf16[16,8,896]{2,1,0:T(8,128)(2,1)S(1)}, u32[]{:S(2)}, u32[]{:S(2)}) collective-permute-start(bf16[16,8,896]{2,1,0:T(8,128)(2,1)S(1)} %get-tuple-element.26), channel_id=1, source_target_pairs={{0,384},{128,0},{256,128},{384,256},{1,385},{129,1},{257,129},{385... | collective-permute-start | bytes 688136 | tf_op jit(solution)/shard_map/ppermute | solution.py:313
  67.9 5.2 %collective-permute-done.6.refs_2_ = bf16[16,8,896]{2,1,0:T(8,128)(2,1)S(1)} collective-permute-done((bf16[16,8,896]{2,1,0:T(8,128)(2,1)S(1)}, bf16[16,8,896]{2,1,0:T(8,128)(2,1)S(1)}, u32[]{:S(2)}, u32[]{:S(2)}) %collective-permute-start.6) | collective-permute-done | bytes 229408 | tf_op jit(solution)/shard_map/ppermute | solution.py:313
  75.8 6.9 %all-to-all-start.1 = ((bf16[16,8,896]{2,1,0:T(8,128)(2,1)}), bf16[16,8,896]{2,1,0:T(8,128)(2,1)S(1)}, u32[]{:S(2)}, u32[]{:S(2)}) async-start(bf16[16,8,896]{2,1,0:T(8,128)(2,1)} %choose.3), calls=%async_computation.1 | async-start | bytes 458752 | tf_op jit(solution)/shard_map/all_to_all | solution.py:318
  83.1 8.5 %all-to-all-done.1 = bf16[16,8,896]{2,1,0:T(8,128)(2,1)S(1)} async-done(((bf16[16,8,896]{2,1,0:T(8,128)(2,1)}), bf16[16,8,896]{2,1,0:T(8,128)(2,1)S(1)}, u32[]{:S(2)}, u32[]{:S(2)}) %all-to-all-start.1) | async-done | bytes 229408 | tf_op jit(solution)/shard_map/all_to_all | solution.py:318
  91.6 12.9 %stretch.1 = (bf16[8,128,256]{2,1,0:T(8,128)(2,1)}, bf16[128,896]{1,0:T(8,128)(2,1)S(1)}) custom-call(bf16[128,896]{1,0:T(8,128)(2,1)S(1)} %bitcast.23, bf16[64,1792]{1,0:T(8,128)(2,1)S(1)} %copy-done.2, bf16[8,128,256]{2,1,0:T(8,128)(2,1)S(1)} %all-to-all-done.qg_ref, bf16[16,1120,256]{2,1,0:T(8,128)(2,1)} %bitcast.33), custom_call_target="tpu_custom_call" | custom-call | flops 7000000000 | bytes 11000000 | tf_op jit(solution)/shard_map/stretch/pallas_call | solution.py:146
  104.5 11.8 %all_to_all.20 = bf16[16,8,896]{2,1,0:T(8,128)(2,1)S(1)} all-to-all(bf16[16,8,896]{2,1,0:T(8,128)(2,1)S(1)} %bitcast.24), channel_id=1, replica_groups=mesh['x'=4,'z'=8,'core'=2,'mp'=8] {'mp'}, dimensions={0} | all-to-all | bytes 458752 | tf_op jit(solution)/shard_map/all_to_all | solution.py:325
  116.3 13.0 %all_gather.33.mine_ref = bf16[64,8,896]{2,1,0:T(8,128)(2,1)S(1)} all-gather(bf16[16,8,896]{2,1,0:T(8,128)(2,1)S(1)} %all_to_all.20), channel_id=1, replica_groups=mesh['x'=4,'z'=8,'core'=2,'mp'=8] {'x'}, dimensions={0}, use_global_device_ids=true | all-gather | bytes 1146880 | tf_op jit(solution)/shard_map/all_gather | solution.py:326
  129.3 8.0 %collective-permute-start.8 = (bf16[64,8,896]{2,1,0:T(8,128)(2,1)S(1)}, bf16[64,8,896]{2,1,0:T(8,128)(2,1)S(1)}, u32[]{:S(2)}, u32[]{:S(2)}) collective-permute-start(bf16[64,8,896]{2,1,0:T(8,128)(2,1)S(1)} %all_gather.33.mine_ref), channel_id=1, source_target_pairs={{0,8},{8,0},{1,9},{9,1},{2,10},{10,2},{3,11},{11,3},{4,12},{12,4},... | collective-permute-start | bytes 2752520 | tf_op jit(solution)/shard_map/ppermute | solution.py:327
  137.3 4.2 %all-to-all-start.2 = ((bf16[8,128,256]{2,1,0:T(8,128)(2,1)}), bf16[8,128,256]{2,1,0:T(8,128)(2,1)}, u32[]{:S(2)}, u32[]{:S(2)}) async-start(bf16[8,128,256]{2,1,0:T(8,128)(2,1)} %get-tuple-element.30), calls=%async_computation.2 | async-start | bytes 1048576 | tf_op jit(solution)/shard_map/all_to_all | solution.py:338
  141.7 2.2 %place.1 = (bf16[8,8,896]{2,1,0:T(8,128)(2,1)S(1)}, bf16[16,8,896]{2,1,0:T(8,128)(2,1)S(1)}, bf16[16,8,896]{2,1,0:T(8,128)(2,1)S(1)}, bf16[16,8,896]{2,1,0:T(8,128)(2,1)S(1)}, bf16[8,8,896]{2,1,0:T(8,128)(2,1)}) custom-call(s32[2,64]{1,0:T(2,128)S(1)} %pad_add_fusion.place_ref, bf16[64,8,896]{2,1,0:T(8,128)(2,1)S(1)} %all_gather.33.mine_ref, ...), custom_call_target="tpu_custom_call" | custom-call | flops 1000000 | bytes 3000000 | tf_op jit(solution)/shard_map/place/pallas_call | solution.py:221
  143.9 6.8 %collective-permute-start.12 = (bf16[8,8,896]{2,1,0:T(8,128)(2,1)}, bf16[8,8,896]{2,1,0:T(8,128)(2,1)S(1)}, u32[]{:S(2)}, u32[]{:S(2)}) collective-permute-start(bf16[8,8,896]{2,1,0:T(8,128)(2,1)} %get-tuple-element.36), channel_id=1, source_target_pairs={{0,64},{8,72},{16,80},{24,88},{32,96},{40,104},{48,112},{56,120},{... | collective-permute-start | bytes 344072 | tf_op jit(solution)/shard_map/ppermute | solution.py:261
  152.6 2.6 %collective-permute-start.10 = (bf16[16,8,896]{2,1,0:T(8,128)(2,1)S(1)}, bf16[16,8,896]{2,1,0:T(8,128)(2,1)S(1)}, u32[]{:S(2)}, u32[]{:S(2)}) collective-permute-start(bf16[16,8,896]{2,1,0:T(8,128)(2,1)S(1)} %get-tuple-element.34), channel_id=1, source_target_pairs={{0,32},{8,104},{16,48},{24,120},{32,64},{40,8},{48,80},{56,24},{64... | collective-permute-start | bytes 688136 | tf_op jit(solution)/shard_map/ppermute | solution.py:261
  155.2 5.4 %collective-permute-start.11 = (bf16[16,8,896]{2,1,0:T(8,128)(2,1)S(1)}, bf16[16,8,896]{2,1,0:T(8,128)(2,1)S(1)}, u32[]{:S(2)}, u32[]{:S(2)}) collective-permute-start(bf16[16,8,896]{2,1,0:T(8,128)(2,1)S(1)} %get-tuple-element.35), channel_id=1, source_target_pairs={{0,48},{8,88},{16,64},{24,104},{32,80},{40,120},{48,96},{56,8},{64... | collective-permute-start | bytes 688136 | tf_op jit(solution)/shard_map/ppermute | solution.py:261
  162.5 3.6 %collective-permute-done.10 = bf16[16,8,896]{2,1,0:T(8,128)(2,1)S(1)} collective-permute-done((bf16[16,8,896]{2,1,0:T(8,128)(2,1)S(1)}, bf16[16,8,896]{2,1,0:T(8,128)(2,1)S(1)}, u32[]{:S(2)}, u32[]{:S(2)}) %collective-permute-start.10) | collective-permute-done | bytes 229408 | tf_op jit(solution)/shard_map/ppermute | solution.py:261
  166.1 3.8 %collective-permute-done.11 = bf16[16,8,896]{2,1,0:T(8,128)(2,1)S(1)} collective-permute-done((bf16[16,8,896]{2,1,0:T(8,128)(2,1)S(1)}, bf16[16,8,896]{2,1,0:T(8,128)(2,1)S(1)}, u32[]{:S(2)}, u32[]{:S(2)}) %collective-permute-start.11) | collective-permute-done | bytes 229408 | tf_op jit(solution)/shard_map/ppermute | solution.py:261
  170.1 2.4 %all-gather.1 = bf16[16,8,896]{2,1,0:T(8,128)(2,1)S(1)} all-gather(bf16[8,8,896]{2,1,0:T(8,128)(2,1)S(1)} %fusion), channel_id=3, replica_groups=mesh['x'=4,'z'=8,'core'=2,'mp'=8] {'core'}, dimensions={0}, use_global_device_ids=true | all-gather | bytes 344064 | tf_op jit(solution)/shard_map/all_gather | solution.py:334
  (66 shorter events, 23.8 us)
Async XLA Ops:
  7.2 1.2 copy-start
  7.2 1.6 copy-start.5
  7.2 75.9 %all-gather.4.cloned.1.call-start = ((), (), s32[]{:S(2)}) async-start(), calls=%async_computation.4 | async-start | bytes 9748480 | tf_op jit(solution)/shard_map/all_gather | solution.py:272
  8.8 9.8 %copy-start.3 = (bf16[512,256]{1,0:T(8,128)(2,1)S(1)}, bf16[512,256]{1,0:T(8,128)(2,1)}, u32[]{:S(2)}) copy-start(bf16[512,256]{1,0:T(8,128)(2,1)} %param.15) | copy-start | bytes 786436
  8.8 9.8 %copy-start.4 = (bf16[512,256]{1,0:T(8,128)(2,1)S(1)}, bf16[512,256]{1,0:T(8,128)(2,1)}, u32[]{:S(2)}) copy-start(bf16[512,256]{1,0:T(8,128)(2,1)} %param.8) | copy-start | bytes 786436
  9.7 13.2 %copy-start.6 = (s32[512,2]{0,1:T(2,128)S(1)}, s32[512,2]{0,1:T(2,128)}, u32[]{:S(2)}) copy-start(s32[512,2]{0,1:T(2,128)} %param.11) | copy-start | bytes 12292
  9.7 14.4 %collective-permute-start = (bf16[8,8,896]{2,1,0:T(8,128)(2,1)S(1)}, bf16[8,8,896]{2,1,0:T(8,128)(2,1)S(1)}, u32[]{:S(2)}, u32[]{:S(2)}) collective-permute-start(bf16[8,8,896]{2,1,0:T(8,128)(2,1)S(1)} %copy-done.1), channel_id=1, source_target_pairs={{0,8},{8,0},{1,9},{9,1},{2,10},{10,2},{3,11},{11,3},{4,12},{12,4},... | collective-permute-start | bytes 344072 | tf_op jit(solution)/shard_map/ppermute | solution.py:304
  18.5 4.7 %copy-start.7 = (s32[512,2]{0,1:T(2,128)S(1)}, s32[512,2]{0,1:T(2,128)}, u32[]{:S(2)}) copy-start(s32[512,2]{0,1:T(2,128)} %param.12) | copy-start | bytes 12292
  19.4 56.4 %all-to-all-start = ((bf16[8,128,256]{2,1,0:T(8,128)(2,1)}), bf16[8,128,256]{2,1,0:T(8,128)(2,1)S(1)}, u32[]{:S(2)}, u32[]{:S(2)}) async-start(bf16[8,128,256]{2,1,0:T(8,128)(2,1)} %pad_maximum_fusion.1), calls=%async_computation | async-start | bytes 1048576 | tf_op jit(solution)/shard_map/all_to_all | solution.py:277
  24.1 23.7 %collective-permute-start.3 = (bf16[16,8,896]{2,1,0:T(8,128)(2,1)S(1)}, bf16[16,8,896]{2,1,0:T(8,128)(2,1)S(1)}, u32[]{:S(2)}, u32[]{:S(2)}) collective-permute-start(bf16[16,8,896]{2,1,0:T(8,128)(2,1)S(1)} %join.1.refs_0_), channel_id=1, source_target_pairs={{0,48},{8,88},{16,64},{24,104},{32,80},{40,120},{48,96},{56,8},{64... | collective-permute-start | bytes 688136 | tf_op jit(solution)/shard_map/ppermute | solution.py:261
  32.7 12.9 %collective-permute-start.4 = (bf16[8,8,896]{2,1,0:T(8,128)(2,1)S(1)}, bf16[8,8,896]{2,1,0:T(8,128)(2,1)S(1)}, u32[]{:S(2)}, u32[]{:S(2)}) collective-permute-start(bf16[8,8,896]{2,1,0:T(8,128)(2,1)S(1)} %copy-done.1), channel_id=1, source_target_pairs={{0,64},{8,72},{16,80},{24,88},{32,96},{40,104},{48,112},{56,120},{... | collective-permute-start | bytes 344072 | tf_op jit(solution)/shard_map/ppermute | solution.py:261
  34.7 15.7 %collective-permute-start.2 = (bf16[16,8,896]{2,1,0:T(8,128)(2,1)S(1)}, bf16[16,8,896]{2,1,0:T(8,128)(2,1)S(1)}, u32[]{:S(2)}, u32[]{:S(2)}) collective-permute-start(bf16[16,8,896]{2,1,0:T(8,128)(2,1)S(1)} %join.1.refs_0_), channel_id=1, source_target_pairs={{0,32},{8,104},{16,48},{24,120},{32,64},{40,8},{48,80},{56,24},{64... | collective-permute-start | bytes 688136 | tf_op jit(solution)/shard_map/ppermute | solution.py:261
  42.7 10.2 %collective-permute-start.1 = (bf16[16,8,896]{2,1,0:T(8,128)(2,1)S(1)}, bf16[16,8,896]{2,1,0:T(8,128)(2,1)S(1)}, u32[]{:S(2)}, u32[]{:S(2)}) collective-permute-start(bf16[16,8,896]{2,1,0:T(8,128)(2,1)S(1)} %join.1.refs_0_), channel_id=1, source_target_pairs={{0,16},{8,120},{16,32},{24,8},{32,48},{40,24},{48,64},{56,40},{64,... | collective-permute-start | bytes 688136 | tf_op jit(solution)/shard_map/ppermute | solution.py:261
  57.1 34.5 %copy-start.2 = (bf16[64,1792]{1,0:T(8,128)(2,1)S(1)}, bf16[64,1792]{1,0:T(8,128)(2,1)}, u32[]{:S(2)}) copy-start(bf16[64,1792]{1,0:T(8,128)(2,1)} %kv_ref.1) | copy-start | bytes 688132
  57.1 10.8 %collective-permute-start.5 = (bf16[16,8,896]{2,1,0:T(8,128)(2,1)S(1)}, bf16[16,8,896]{2,1,0:T(8,128)(2,1)S(1)}, u32[]{:S(2)}, u32[]{:S(2)}) collective-permute-start(bf16[16,8,896]{2,1,0:T(8,128)(2,1)S(1)} %get-tuple-element.24), channel_id=1, source_target_pairs={{0,128},{128,256},{256,384},{384,0},{1,129},{129,257},{257,385},{3... | collective-permute-start | bytes 688136 | tf_op jit(solution)/shard_map/ppermute | solution.py:313
  60.4 12.7 %collective-permute-start.6 = (bf16[16,8,896]{2,1,0:T(8,128)(2,1)S(1)}, bf16[16,8,896]{2,1,0:T(8,128)(2,1)S(1)}, u32[]{:S(2)}, u32[]{:S(2)}) collective-permute-start(bf16[16,8,896]{2,1,0:T(8,128)(2,1)S(1)} %get-tuple-element.25), channel_id=1, source_target_pairs={{0,256},{128,384},{256,0},{384,128},{1,257},{129,385},{257,1},{385... | collective-permute-start | bytes 688136 | tf_op jit(solution)/shard_map/ppermute | solution.py:313
  64.8 9.7 %collective-permute-start.7 = (bf16[16,8,896]{2,1,0:T(8,128)(2,1)S(1)}, bf16[16,8,896]{2,1,0:T(8,128)(2,1)S(1)}, u32[]{:S(2)}, u32[]{:S(2)}) collective-permute-start(bf16[16,8,896]{2,1,0:T(8,128)(2,1)S(1)} %get-tuple-element.26), channel_id=1, source_target_pairs={{0,384},{128,0},{256,128},{384,256},{1,385},{129,1},{257,129},{385... | collective-permute-start | bytes 688136 | tf_op jit(solution)/shard_map/ppermute | solution.py:313
  75.8 15.8 %all-to-all-start.1 = ((bf16[16,8,896]{2,1,0:T(8,128)(2,1)}), bf16[16,8,896]{2,1,0:T(8,128)(2,1)S(1)}, u32[]{:S(2)}, u32[]{:S(2)}) async-start(bf16[16,8,896]{2,1,0:T(8,128)(2,1)} %choose.3), calls=%async_computation.1 | async-start | bytes 458752 | tf_op jit(solution)/shard_map/all_to_all | solution.py:318
  129.3 12.4 %collective-permute-start.8 = (bf16[64,8,896]{2,1,0:T(8,128)(2,1)S(1)}, bf16[64,8,896]{2,1,0:T(8,128)(2,1)S(1)}, u32[]{:S(2)}, u32[]{:S(2)}) collective-permute-start(bf16[64,8,896]{2,1,0:T(8,128)(2,1)S(1)} %all_gather.33.mine_ref), channel_id=1, source_target_pairs={{0,8},{8,0},{1,9},{9,1},{2,10},{10,2},{3,11},{11,3},{4,12},{12,4},... | collective-permute-start | bytes 2752520 | tf_op jit(solution)/shard_map/ppermute | solution.py:327
  137.3 23.3 %all-to-all-start.2 = ((bf16[8,128,256]{2,1,0:T(8,128)(2,1)}), bf16[8,128,256]{2,1,0:T(8,128)(2,1)}, u32[]{:S(2)}, u32[]{:S(2)}) async-start(bf16[8,128,256]{2,1,0:T(8,128)(2,1)} %get-tuple-element.30), calls=%async_computation.2 | async-start | bytes 1048576 | tf_op jit(solution)/shard_map/all_to_all | solution.py:338
  143.9 18.6 %collective-permute-start.12 = (bf16[8,8,896]{2,1,0:T(8,128)(2,1)}, bf16[8,8,896]{2,1,0:T(8,128)(2,1)S(1)}, u32[]{:S(2)}, u32[]{:S(2)}) collective-permute-start(bf16[8,8,896]{2,1,0:T(8,128)(2,1)} %get-tuple-element.36), channel_id=1, source_target_pairs={{0,64},{8,72},{16,80},{24,88},{32,96},{40,104},{48,112},{56,120},{... | collective-permute-start | bytes 344072 | tf_op jit(solution)/shard_map/ppermute | solution.py:261
  150.7 11.9 %collective-permute-start.9 = (bf16[16,8,896]{2,1,0:T(8,128)(2,1)S(1)}, bf16[16,8,896]{2,1,0:T(8,128)(2,1)S(1)}, u32[]{:S(2)}, u32[]{:S(2)}) collective-permute-start(bf16[16,8,896]{2,1,0:T(8,128)(2,1)S(1)} %get-tuple-element.33), channel_id=1, source_target_pairs={{0,16},{8,120},{16,32},{24,8},{32,48},{40,24},{48,64},{56,40},{64,... | collective-permute-start | bytes 688136 | tf_op jit(solution)/shard_map/ppermute | solution.py:261
  152.6 13.5 %collective-permute-start.10 = (bf16[16,8,896]{2,1,0:T(8,128)(2,1)S(1)}, bf16[16,8,896]{2,1,0:T(8,128)(2,1)S(1)}, u32[]{:S(2)}, u32[]{:S(2)}) collective-permute-start(bf16[16,8,896]{2,1,0:T(8,128)(2,1)S(1)} %get-tuple-element.34), channel_id=1, source_target_pairs={{0,32},{8,104},{16,48},{24,120},{32,64},{40,8},{48,80},{56,24},{64... | collective-permute-start | bytes 688136 | tf_op jit(solution)/shard_map/ppermute | solution.py:261
  155.2 14.7 %collective-permute-start.11 = (bf16[16,8,896]{2,1,0:T(8,128)(2,1)S(1)}, bf16[16,8,896]{2,1,0:T(8,128)(2,1)S(1)}, u32[]{:S(2)}, u32[]{:S(2)}) collective-permute-start(bf16[16,8,896]{2,1,0:T(8,128)(2,1)S(1)} %get-tuple-element.35), channel_id=1, source_target_pairs={{0,48},{8,88},{16,64},{24,104},{32,80},{40,120},{48,96},{56,8},{64... | collective-permute-start | bytes 688136 | tf_op jit(solution)/shard_map/ppermute | solution.py:261
  (1 other events, 1.0 us)
Sparse Core Ops, SparseCore 0:
  10.1 72.8 all-gather.3

commit v5 on v4

--- a/solution.py
+++ b/solution.py
@@ -328,16 +328,18 @@
     places = jnp.stack([of_column(place, core), of_column(place, 1 - core)])
     mine, *partial = place_call(places, every, every_beside)
     partial = [along_z(part, k) for k, part in enumerate(partial, 1)]
-    partial = [part.astype(jnp.float32) for part in lax.optimization_barrier(partial)]
+    out = lax.all_gather(out, "mp", axis=0, tiled=False)
+    out = lax.dynamic_index_in_dim(out, lax.axis_index("mp"), 1, keepdims=False)
+    attended = out[:, :STRETCH].reshape(NM * STRETCH, KV)
+    grad_queries = out[:, STRETCH:].reshape(NM * STRETCH, KV)
+    partial, attended, grad_queries = lax.optimization_barrier((partial, attended, grad_queries))
+    partial = [part.astype(jnp.float32) for part in partial]
     ours = mine.astype(jnp.float32) + partial[3] + sum(part[:SLOTS] for part in partial[:3])
     theirs = sum(part[SLOTS:] for part in partial[:3]).astype(jnp.bfloat16)
     theirs = lax.all_gather(theirs, "core", axis=0, tiled=False)
     theirs = lax.dynamic_index_in_dim(theirs, 1 - core, 0, keepdims=False)
     grad_pool = ours + theirs.astype(jnp.float32)
 
-    out = lax.all_to_all(out, "mp", split_axis=0, concat_axis=0, tiled=True)
-    attended = out[:, :STRETCH].reshape(NM * STRETCH, KV)
-    grad_queries = out[:, STRETCH:].reshape(NM * STRETCH, KV)
     return attended, grad_queries, grad_pool
 
 

time: 181 us -> 179 us (0.989)
  starting transfers between devices: 78.8 us -> 74.2 us
  waiting for transfers between devices: 24.6 us -> 26.5 us
    all_to_all x1 -> x0, starting transfers between devices: 4.17 us -> none  [shards(): out = lax.all_to_all(out, 'mp', split_axis=0, concat_axis=0, tiled=True)]
    ppermute x1, waiting for transfers between devices: 0.01 us -> 1.9 us  [shards(): every_beside = lax.ppermute(every, 'core', swap)]
    ppermute x8, waiting for transfers between devices: 9.11 us -> 7.22 us  [along_z(): return lax.ppermute(values, ('z', 'core'), pairs)]
  transfers between devices with their start and end apart: 17 -> 17, of which waited for: 10 -> 12; matrix products, arithmetic and copies ran while one was open for 3% -> 3% of each run, Pallas kernels for 2% -> 2%
where the time goes in v5:
time: 179 us; the launch traced here: 177 us
  starting transfers between devices  74.2 us (41%)
  blocking collectives  36.8 us (21%)
  waiting for transfers between devices  26.5 us (15%)
  Pallas kernels  17.3 us (10%)
  between operations  14.5 us (8%)
  local copies, waits for them, and re-layouts  4.85 us (3%)
  other arithmetic  3.24 us (2%)
    ppermute x8, starting transfers between devices, along_z(): return lax.ppermute(values, ('z', 'core'), pairs)  36.4 us
    all_gather x1, blocking collectives, shards(): every = lax.all_gather(grad_rows, 'x', axis=0, tiled=True)  13.4 us
    pallas_call x1, Pallas kernels, stretch_call(): pl.pallas_call(stretch_kernel, out_shape=(jax.ShapeDtypeStruct((NM, 2 * S...  12.9 us
    all_to_all x1, blocking collectives, shards(): lax.all_to_all(grad_rows, 'mp', split_axis=0, concat_axis=0, tiled=True)  11.6 us
    ppermute x3, starting transfers between devices, shards(): lax.ppermute(chosen[k], 'x', [(i, (i + k) % NX) for i in range(NX)])  10.7 us
    all_gather x4, blocking collectives, shards(): lax.all_gather(part, 'core', axis=0, tiled=True)  9.75 us
    all_to_all x1, waiting for transfers between devices, shards(): rows = lax.all_to_all(rows, 'mp', split_axis=0, concat_axis=0, tiled=True)  8.82 us
    ppermute x1, starting transfers between devices, shards(): beside = lax.ppermute(pool, 'core', swap)  8.79 us
  transfers between devices with their start and end apart: 17, of which 12 were waited for; matrix products, arithmetic and copies ran while one was open for 3% of the time, Pallas kernels for 2%

profile of v5, /device:TPU:1, one launch (start us, length us, event | category | flops | bytes accessed | tf_op | source)
XLA Modules:
  0.0 177.4 jit_solution(7020985409234063223)
XLA Ops:
  9.7 8.8 %collective-permute-start = (bf16[8,8,896]{2,1,0:T(8,128)(2,1)S(1)}, bf16[8,8,896]{2,1,0:T(8,128)(2,1)S(1)}, u32[]{:S(2)}, u32[]{:S(2)}) collective-permute-start(bf16[8,8,896]{2,1,0:T(8,128)(2,1)S(1)} %copy-done.1), channel_id=1, source_target_pairs={{0,8},{8,0},{1,9},{9,1},{2,10},{10,2},{3,11},{11,3},{4,12},{12,4},... | collective-permute-start | bytes 344072 | tf_op jit(solution)/shard_map/ppermute | solution.py:304
  19.4 3.5 %all-to-all-start = ((bf16[8,128,256]{2,1,0:T(8,128)(2,1)}), bf16[8,128,256]{2,1,0:T(8,128)(2,1)S(1)}, u32[]{:S(2)}, u32[]{:S(2)}) async-start(bf16[8,128,256]{2,1,0:T(8,128)(2,1)} %pad_maximum_fusion.1), calls=%async_computation | async-start | bytes 1048576 | tf_op jit(solution)/shard_map/all_to_all | solution.py:277
  24.2 8.6 %collective-permute-start.3 = (bf16[16,8,896]{2,1,0:T(8,128)(2,1)S(1)}, bf16[16,8,896]{2,1,0:T(8,128)(2,1)S(1)}, u32[]{:S(2)}, u32[]{:S(2)}) collective-permute-start(bf16[16,8,896]{2,1,0:T(8,128)(2,1)S(1)} %join.1.refs_0_), channel_id=1, source_target_pairs={{0,48},{8,88},{16,64},{24,104},{32,80},{40,120},{48,96},{56,8},{64... | collective-permute-start | bytes 688136 | tf_op jit(solution)/shard_map/ppermute | solution.py:261
  34.7 7.3 %collective-permute-start.2 = (bf16[16,8,896]{2,1,0:T(8,128)(2,1)S(1)}, bf16[16,8,896]{2,1,0:T(8,128)(2,1)S(1)}, u32[]{:S(2)}, u32[]{:S(2)}) collective-permute-start(bf16[16,8,896]{2,1,0:T(8,128)(2,1)S(1)} %join.1.refs_0_), channel_id=1, source_target_pairs={{0,32},{8,104},{16,48},{24,120},{32,64},{40,8},{48,80},{56,24},{64... | collective-permute-start | bytes 688136 | tf_op jit(solution)/shard_map/ppermute | solution.py:261
  42.7 2.2 %collective-permute-start.1 = (bf16[16,8,896]{2,1,0:T(8,128)(2,1)S(1)}, bf16[16,8,896]{2,1,0:T(8,128)(2,1)S(1)}, u32[]{:S(2)}, u32[]{:S(2)}) collective-permute-start(bf16[16,8,896]{2,1,0:T(8,128)(2,1)S(1)} %join.1.refs_0_), channel_id=1, source_target_pairs={{0,16},{8,120},{16,32},{24,8},{32,48},{40,24},{48,64},{56,40},{64,... | collective-permute-start | bytes 688136 | tf_op jit(solution)/shard_map/ppermute | solution.py:261
  47.9 2.1 %all_gather.35.refs_3_ = bf16[32,8,896]{2,1,0:T(8,128)(2,1)S(1)} all-gather(bf16[16,8,896]{2,1,0:T(8,128)(2,1)S(1)} %collective-permute-done.3), channel_id=1, replica_groups=mesh['x'=4,'z'=8,'core'=2,'mp'=8] {'core'}, dimensions={0}, use_global_device_ids=true | all-gather | bytes 688128 | tf_op jit(solution)/shard_map/all_gather | solution.py:308
  50.4 2.1 %all_gather.34.refs_2_ = bf16[32,8,896]{2,1,0:T(8,128)(2,1)S(1)} all-gather(bf16[16,8,896]{2,1,0:T(8,128)(2,1)S(1)} %collective-permute-done.2), channel_id=1, replica_groups=mesh['x'=4,'z'=8,'core'=2,'mp'=8] {'core'}, dimensions={0}, use_global_device_ids=true | all-gather | bytes 688128 | tf_op jit(solution)/shard_map/all_gather | solution.py:308
  52.9 3.5 %all_gather.33.refs_1_ = bf16[32,8,896]{2,1,0:T(8,128)(2,1)S(1)} all-gather(bf16[16,8,896]{2,1,0:T(8,128)(2,1)S(1)} %collective-permute-done.1), channel_id=1, replica_groups=mesh['x'=4,'z'=8,'core'=2,'mp'=8] {'core'}, dimensions={0}, use_global_device_ids=true | all-gather | bytes 688128 | tf_op jit(solution)/shard_map/all_gather | solution.py:308
  57.2 3.2 %collective-permute-start.5 = (bf16[16,8,896]{2,1,0:T(8,128)(2,1)S(1)}, bf16[16,8,896]{2,1,0:T(8,128)(2,1)S(1)}, u32[]{:S(2)}, u32[]{:S(2)}) collective-permute-start(bf16[16,8,896]{2,1,0:T(8,128)(2,1)S(1)} %get-tuple-element.26), channel_id=1, source_target_pairs={{0,128},{128,256},{256,384},{384,0},{1,129},{129,257},{257,385},{3... | collective-permute-start | bytes 688136 | tf_op jit(solution)/shard_map/ppermute | solution.py:313
  60.4 4.4 %collective-permute-start.6 = (bf16[16,8,896]{2,1,0:T(8,128)(2,1)S(1)}, bf16[16,8,896]{2,1,0:T(8,128)(2,1)S(1)}, u32[]{:S(2)}, u32[]{:S(2)}) collective-permute-start(bf16[16,8,896]{2,1,0:T(8,128)(2,1)S(1)} %get-tuple-element.27), channel_id=1, source_target_pairs={{0,256},{128,384},{256,0},{384,128},{1,257},{129,385},{257,1},{385... | collective-permute-start | bytes 688136 | tf_op jit(solution)/shard_map/ppermute | solution.py:313
  64.8 3.1 %collective-permute-start.7 = (bf16[16,8,896]{2,1,0:T(8,128)(2,1)S(1)}, bf16[16,8,896]{2,1,0:T(8,128)(2,1)S(1)}, u32[]{:S(2)}, u32[]{:S(2)}) collective-permute-start(bf16[16,8,896]{2,1,0:T(8,128)(2,1)S(1)} %get-tuple-element.28), channel_id=1, source_target_pairs={{0,384},{128,0},{256,128},{384,256},{1,385},{129,1},{257,129},{385... | collective-permute-start | bytes 688136 | tf_op jit(solution)/shard_map/ppermute | solution.py:313
  67.9 5.2 %collective-permute-done.6.refs_2_ = bf16[16,8,896]{2,1,0:T(8,128)(2,1)S(1)} collective-permute-done((bf16[16,8,896]{2,1,0:T(8,128)(2,1)S(1)}, bf16[16,8,896]{2,1,0:T(8,128)(2,1)S(1)}, u32[]{:S(2)}, u32[]{:S(2)}) %collective-permute-start.6) | collective-permute-done | bytes 229408 | tf_op jit(solution)/shard_map/ppermute | solution.py:313
  75.8 7.0 %all-to-all-start.1 = ((bf16[16,8,896]{2,1,0:T(8,128)(2,1)}), bf16[16,8,896]{2,1,0:T(8,128)(2,1)S(1)}, u32[]{:S(2)}, u32[]{:S(2)}) async-start(bf16[16,8,896]{2,1,0:T(8,128)(2,1)} %choose.3), calls=%async_computation.1 | async-start | bytes 458752 | tf_op jit(solution)/shard_map/all_to_all | solution.py:318
  83.1 8.8 %all-to-all-done.1 = bf16[16,8,896]{2,1,0:T(8,128)(2,1)S(1)} async-done(((bf16[16,8,896]{2,1,0:T(8,128)(2,1)}), bf16[16,8,896]{2,1,0:T(8,128)(2,1)S(1)}, u32[]{:S(2)}, u32[]{:S(2)}) %all-to-all-start.1) | async-done | bytes 229408 | tf_op jit(solution)/shard_map/all_to_all | solution.py:318
  91.9 12.9 %stretch.1 = (bf16[8,128,256]{2,1,0:T(8,128)(2,1)}, bf16[128,896]{1,0:T(8,128)(2,1)S(1)}) custom-call(bf16[128,896]{1,0:T(8,128)(2,1)S(1)} %bitcast.26, bf16[64,1792]{1,0:T(8,128)(2,1)S(1)} %copy-done.2, bf16[8,128,256]{2,1,0:T(8,128)(2,1)S(1)} %all-to-all-done.qg_ref, bf16[16,1120,256]{2,1,0:T(8,128)(2,1)} %bitcast.37), custom_call_target="tpu_custom_call" | custom-call | flops 7000000000 | bytes 11000000 | tf_op jit(solution)/shard_map/stretch/pallas_call | solution.py:146
  104.9 11.6 %all_to_all.15 = bf16[16,8,896]{2,1,0:T(8,128)(2,1)S(1)} all-to-all(bf16[16,8,896]{2,1,0:T(8,128)(2,1)S(1)} %bitcast.27), channel_id=1, replica_groups=mesh['x'=4,'z'=8,'core'=2,'mp'=8] {'mp'}, dimensions={0} | all-to-all | bytes 458752 | tf_op jit(solution)/shard_map/all_to_all | solution.py:325
  116.4 13.4 %all_gather.39.mine_ref = bf16[64,8,896]{2,1,0:T(8,128)(2,1)S(1)} all-gather(bf16[16,8,896]{2,1,0:T(8,128)(2,1)S(1)} %all_to_all.15), channel_id=1, replica_groups=mesh['x'=4,'z'=8,'core'=2,'mp'=8] {'x'}, dimensions={0}, use_global_device_ids=true | all-gather | bytes 1146880 | tf_op jit(solution)/shard_map/all_gather | solution.py:326
  129.9 7.8 %collective-permute-start.8 = (bf16[64,8,896]{2,1,0:T(8,128)(2,1)S(1)}, bf16[64,8,896]{2,1,0:T(8,128)(2,1)S(1)}, u32[]{:S(2)}, u32[]{:S(2)}) collective-permute-start(bf16[64,8,896]{2,1,0:T(8,128)(2,1)S(1)} %all_gather.39.mine_ref), channel_id=1, source_target_pairs={{0,8},{8,0},{1,9},{9,1},{2,10},{10,2},{3,11},{11,3},{4,12},{12,4},... | collective-permute-start | bytes 2752520 | tf_op jit(solution)/shard_map/ppermute | solution.py:327
  139.8 2.2 %place.1 = (bf16[8,8,896]{2,1,0:T(8,128)(2,1)S(1)}, bf16[16,8,896]{2,1,0:T(8,128)(2,1)S(1)}, bf16[16,8,896]{2,1,0:T(8,128)(2,1)S(1)}, bf16[16,8,896]{2,1,0:T(8,128)(2,1)S(1)}, bf16[8,8,896]{2,1,0:T(8,128)(2,1)}) custom-call(s32[2,64]{1,0:T(2,128)S(1)} %pad_add_fusion.place_ref, bf16[64,8,896]{2,1,0:T(8,128)(2,1)S(1)} %all_gather.39.mine_ref, ...), custom_call_target="tpu_custom_call" | custom-call | flops 1000000 | bytes 3000000 | tf_op jit(solution)/shard_map/place/pallas_call | solution.py:221
  142.1 6.5 %collective-permute-start.12 = (bf16[8,8,896]{2,1,0:T(8,128)(2,1)}, bf16[8,8,896]{2,1,0:T(8,128)(2,1)S(1)}, u32[]{:S(2)}, u32[]{:S(2)}) collective-permute-start(bf16[8,8,896]{2,1,0:T(8,128)(2,1)} %get-tuple-element.36), channel_id=1, source_target_pairs={{0,64},{8,72},{16,80},{24,88},{32,96},{40,104},{48,112},{56,120},{... | collective-permute-start | bytes 344072 | tf_op jit(solution)/shard_map/ppermute | solution.py:261
  150.5 2.8 %collective-permute-start.10 = (bf16[16,8,896]{2,1,0:T(8,128)(2,1)S(1)}, bf16[16,8,896]{2,1,0:T(8,128)(2,1)S(1)}, u32[]{:S(2)}, u32[]{:S(2)}) collective-permute-start(bf16[16,8,896]{2,1,0:T(8,128)(2,1)S(1)} %get-tuple-element.34), channel_id=1, source_target_pairs={{0,32},{8,104},{16,48},{24,120},{32,64},{40,8},{48,80},{56,24},{64... | collective-permute-start | bytes 688136 | tf_op jit(solution)/shard_map/ppermute | solution.py:261
  153.3 5.2 %collective-permute-start.11 = (bf16[16,8,896]{2,1,0:T(8,128)(2,1)S(1)}, bf16[16,8,896]{2,1,0:T(8,128)(2,1)S(1)}, u32[]{:S(2)}, u32[]{:S(2)}) collective-permute-start(bf16[16,8,896]{2,1,0:T(8,128)(2,1)S(1)} %get-tuple-element.35), channel_id=1, source_target_pairs={{0,48},{8,88},{16,64},{24,104},{32,80},{40,120},{48,96},{56,8},{64... | collective-permute-start | bytes 688136 | tf_op jit(solution)/shard_map/ppermute | solution.py:261
  162.1 2.2 %collective-permute-done.10 = bf16[16,8,896]{2,1,0:T(8,128)(2,1)S(1)} collective-permute-done((bf16[16,8,896]{2,1,0:T(8,128)(2,1)S(1)}, bf16[16,8,896]{2,1,0:T(8,128)(2,1)S(1)}, u32[]{:S(2)}, u32[]{:S(2)}) %collective-permute-start.10) | collective-permute-done | bytes 229408 | tf_op jit(solution)/shard_map/ppermute | solution.py:261
  164.3 3.3 %collective-permute-done.11 = bf16[16,8,896]{2,1,0:T(8,128)(2,1)S(1)} collective-permute-done((bf16[16,8,896]{2,1,0:T(8,128)(2,1)S(1)}, bf16[16,8,896]{2,1,0:T(8,128)(2,1)S(1)}, u32[]{:S(2)}, u32[]{:S(2)}) %collective-permute-start.11) | collective-permute-done | bytes 229408 | tf_op jit(solution)/shard_map/ppermute | solution.py:261
  (68 shorter events, 25.2 us)
Async XLA Ops:
  7.2 1.2 copy-start
  7.2 1.6 copy-start.5
  7.2 75.9 %all-gather.6.cloned.1.call-start = ((), (), s32[]{:S(2)}) async-start(), calls=%async_computation.3 | async-start | bytes 9748480 | tf_op jit(solution)/shard_map/all_gather | solution.py:272
  8.8 9.8 %copy-start.3 = (bf16[512,256]{1,0:T(8,128)(2,1)S(1)}, bf16[512,256]{1,0:T(8,128)(2,1)}, u32[]{:S(2)}) copy-start(bf16[512,256]{1,0:T(8,128)(2,1)} %param.15) | copy-start | bytes 786436
  8.8 9.7 %copy-start.4 = (bf16[512,256]{1,0:T(8,128)(2,1)S(1)}, bf16[512,256]{1,0:T(8,128)(2,1)}, u32[]{:S(2)}) copy-start(bf16[512,256]{1,0:T(8,128)(2,1)} %param.8) | copy-start | bytes 786436
  9.7 13.2 %copy-start.6 = (s32[512,2]{0,1:T(2,128)S(1)}, s32[512,2]{0,1:T(2,128)}, u32[]{:S(2)}) copy-start(s32[512,2]{0,1:T(2,128)} %param.11) | copy-start | bytes 12292
  9.7 14.4 %collective-permute-start = (bf16[8,8,896]{2,1,0:T(8,128)(2,1)S(1)}, bf16[8,8,896]{2,1,0:T(8,128)(2,1)S(1)}, u32[]{:S(2)}, u32[]{:S(2)}) collective-permute-start(bf16[8,8,896]{2,1,0:T(8,128)(2,1)S(1)} %copy-done.1), channel_id=1, source_target_pairs={{0,8},{8,0},{1,9},{9,1},{2,10},{10,2},{3,11},{11,3},{4,12},{12,4},... | collective-permute-start | bytes 344072 | tf_op jit(solution)/shard_map/ppermute | solution.py:304
  18.5 4.7 %copy-start.7 = (s32[512,2]{0,1:T(2,128)S(1)}, s32[512,2]{0,1:T(2,128)}, u32[]{:S(2)}) copy-start(s32[512,2]{0,1:T(2,128)} %param.12) | copy-start | bytes 12292
  19.4 56.4 %all-to-all-start = ((bf16[8,128,256]{2,1,0:T(8,128)(2,1)}), bf16[8,128,256]{2,1,0:T(8,128)(2,1)S(1)}, u32[]{:S(2)}, u32[]{:S(2)}) async-start(bf16[8,128,256]{2,1,0:T(8,128)(2,1)} %pad_maximum_fusion.1), calls=%async_computation | async-start | bytes 1048576 | tf_op jit(solution)/shard_map/all_to_all | solution.py:277
  24.2 23.7 %collective-permute-start.3 = (bf16[16,8,896]{2,1,0:T(8,128)(2,1)S(1)}, bf16[16,8,896]{2,1,0:T(8,128)(2,1)S(1)}, u32[]{:S(2)}, u32[]{:S(2)}) collective-permute-start(bf16[16,8,896]{2,1,0:T(8,128)(2,1)S(1)} %join.1.refs_0_), channel_id=1, source_target_pairs={{0,48},{8,88},{16,64},{24,104},{32,80},{40,120},{48,96},{56,8},{64... | collective-permute-start | bytes 688136 | tf_op jit(solution)/shard_map/ppermute | solution.py:261
  32.7 12.9 %collective-permute-start.4 = (bf16[8,8,896]{2,1,0:T(8,128)(2,1)S(1)}, bf16[8,8,896]{2,1,0:T(8,128)(2,1)S(1)}, u32[]{:S(2)}, u32[]{:S(2)}) collective-permute-start(bf16[8,8,896]{2,1,0:T(8,128)(2,1)S(1)} %copy-done.1), channel_id=1, source_target_pairs={{0,64},{8,72},{16,80},{24,88},{32,96},{40,104},{48,112},{56,120},{... | collective-permute-start | bytes 344072 | tf_op jit(solution)/shard_map/ppermute | solution.py:261
  34.7 15.7 %collective-permute-start.2 = (bf16[16,8,896]{2,1,0:T(8,128)(2,1)S(1)}, bf16[16,8,896]{2,1,0:T(8,128)(2,1)S(1)}, u32[]{:S(2)}, u32[]{:S(2)}) collective-permute-start(bf16[16,8,896]{2,1,0:T(8,128)(2,1)S(1)} %join.1.refs_0_), channel_id=1, source_target_pairs={{0,32},{8,104},{16,48},{24,120},{32,64},{40,8},{48,80},{56,24},{64... | collective-permute-start | bytes 688136 | tf_op jit(solution)/shard_map/ppermute | solution.py:261
  42.7 10.2 %collective-permute-start.1 = (bf16[16,8,896]{2,1,0:T(8,128)(2,1)S(1)}, bf16[16,8,896]{2,1,0:T(8,128)(2,1)S(1)}, u32[]{:S(2)}, u32[]{:S(2)}) collective-permute-start(bf16[16,8,896]{2,1,0:T(8,128)(2,1)S(1)} %join.1.refs_0_), channel_id=1, source_target_pairs={{0,16},{8,120},{16,32},{24,8},{32,48},{40,24},{48,64},{56,40},{64,... | collective-permute-start | bytes 688136 | tf_op jit(solution)/shard_map/ppermute | solution.py:261
  57.2 34.7 %copy-start.2 = (bf16[64,1792]{1,0:T(8,128)(2,1)S(1)}, bf16[64,1792]{1,0:T(8,128)(2,1)}, u32[]{:S(2)}) copy-start(bf16[64,1792]{1,0:T(8,128)(2,1)} %kv_ref.1) | copy-start | bytes 688132
  57.2 10.7 %collective-permute-start.5 = (bf16[16,8,896]{2,1,0:T(8,128)(2,1)S(1)}, bf16[16,8,896]{2,1,0:T(8,128)(2,1)S(1)}, u32[]{:S(2)}, u32[]{:S(2)}) collective-permute-start(bf16[16,8,896]{2,1,0:T(8,128)(2,1)S(1)} %get-tuple-element.26), channel_id=1, source_target_pairs={{0,128},{128,256},{256,384},{384,0},{1,129},{129,257},{257,385},{3... | collective-permute-start | bytes 688136 | tf_op jit(solution)/shard_map/ppermute | solution.py:313
  60.4 12.7 %collective-permute-start.6 = (bf16[16,8,896]{2,1,0:T(8,128)(2,1)S(1)}, bf16[16,8,896]{2,1,0:T(8,128)(2,1)S(1)}, u32[]{:S(2)}, u32[]{:S(2)}) collective-permute-start(bf16[16,8,896]{2,1,0:T(8,128)(2,1)S(1)} %get-tuple-element.27), channel_id=1, source_target_pairs={{0,256},{128,384},{256,0},{384,128},{1,257},{129,385},{257,1},{385... | collective-permute-start | bytes 688136 | tf_op jit(solution)/shard_map/ppermute | solution.py:313
  64.8 9.7 %collective-permute-start.7 = (bf16[16,8,896]{2,1,0:T(8,128)(2,1)S(1)}, bf16[16,8,896]{2,1,0:T(8,128)(2,1)S(1)}, u32[]{:S(2)}, u32[]{:S(2)}) collective-permute-start(bf16[16,8,896]{2,1,0:T(8,128)(2,1)S(1)} %get-tuple-element.28), channel_id=1, source_target_pairs={{0,384},{128,0},{256,128},{384,256},{1,385},{129,1},{257,129},{385... | collective-permute-start | bytes 688136 | tf_op jit(solution)/shard_map/ppermute | solution.py:313
  75.8 16.1 %all-to-all-start.1 = ((bf16[16,8,896]{2,1,0:T(8,128)(2,1)}), bf16[16,8,896]{2,1,0:T(8,128)(2,1)S(1)}, u32[]{:S(2)}, u32[]{:S(2)}) async-start(bf16[16,8,896]{2,1,0:T(8,128)(2,1)} %choose.3), calls=%async_computation.1 | async-start | bytes 458752 | tf_op jit(solution)/shard_map/all_to_all | solution.py:318
  82.8 77.4 %all-gather.8.cloned.1.call-start = ((), (), s32[]{:S(2)}) async-start(), calls=%async_computation.4 | async-start | bytes 4718592 | tf_op jit(solution)/shard_map/all_gather | solution.py:331
  129.9 9.9 %collective-permute-start.8 = (bf16[64,8,896]{2,1,0:T(8,128)(2,1)S(1)}, bf16[64,8,896]{2,1,0:T(8,128)(2,1)S(1)}, u32[]{:S(2)}, u32[]{:S(2)}) collective-permute-start(bf16[64,8,896]{2,1,0:T(8,128)(2,1)S(1)} %all_gather.39.mine_ref), channel_id=1, source_target_pairs={{0,8},{8,0},{1,9},{9,1},{2,10},{10,2},{3,11},{11,3},{4,12},{12,4},... | collective-permute-start | bytes 2752520 | tf_op jit(solution)/shard_map/ppermute | solution.py:327
  142.1 20.0 %collective-permute-start.12 = (bf16[8,8,896]{2,1,0:T(8,128)(2,1)}, bf16[8,8,896]{2,1,0:T(8,128)(2,1)S(1)}, u32[]{:S(2)}, u32[]{:S(2)}) collective-permute-start(bf16[8,8,896]{2,1,0:T(8,128)(2,1)} %get-tuple-element.36), channel_id=1, source_target_pairs={{0,64},{8,72},{16,80},{24,88},{32,96},{40,104},{48,112},{56,120},{... | collective-permute-start | bytes 344072 | tf_op jit(solution)/shard_map/ppermute | solution.py:261
  148.6 13.5 %collective-permute-start.9 = (bf16[16,8,896]{2,1,0:T(8,128)(2,1)S(1)}, bf16[16,8,896]{2,1,0:T(8,128)(2,1)S(1)}, u32[]{:S(2)}, u32[]{:S(2)}) collective-permute-start(bf16[16,8,896]{2,1,0:T(8,128)(2,1)S(1)} %get-tuple-element.33), channel_id=1, source_target_pairs={{0,16},{8,120},{16,32},{24,8},{32,48},{40,24},{48,64},{56,40},{64,... | collective-permute-start | bytes 688136 | tf_op jit(solution)/shard_map/ppermute | solution.py:261
  150.5 13.8 %collective-permute-start.10 = (bf16[16,8,896]{2,1,0:T(8,128)(2,1)S(1)}, bf16[16,8,896]{2,1,0:T(8,128)(2,1)S(1)}, u32[]{:S(2)}, u32[]{:S(2)}) collective-permute-start(bf16[16,8,896]{2,1,0:T(8,128)(2,1)S(1)} %get-tuple-element.34), channel_id=1, source_target_pairs={{0,32},{8,104},{16,48},{24,120},{32,64},{40,8},{48,80},{56,24},{64... | collective-permute-start | bytes 688136 | tf_op jit(solution)/shard_map/ppermute | solution.py:261
  153.3 14.3 %collective-permute-start.11 = (bf16[16,8,896]{2,1,0:T(8,128)(2,1)S(1)}, bf16[16,8,896]{2,1,0:T(8,128)(2,1)S(1)}, u32[]{:S(2)}, u32[]{:S(2)}) collective-permute-start(bf16[16,8,896]{2,1,0:T(8,128)(2,1)S(1)} %get-tuple-element.35), channel_id=1, source_target_pairs={{0,48},{8,88},{16,64},{24,104},{32,80},{40,120},{48,96},{56,8},{64... | collective-permute-start | bytes 688136 | tf_op jit(solution)/shard_map/ppermute | solution.py:261
  (1 other events, 0.9 us)
Sparse Core Ops, SparseCore 0:
  10.1 72.8 all-gather.5
  105.0 55.1 all-gather.7

commit v6 on v5

--- a/solution.py
+++ b/solution.py
@@ -210,7 +210,7 @@
             total_ref[at] += ref[i].astype(jnp.float32)
             return carry
 
-        lax.fori_loop(0, NX * REQ, add, 0, unroll=4)
+        lax.fori_loop(0, NX * REQ, add, 0, unroll=8)
     at = 0
     for ref in out_refs:
         ref[...] = total_ref[at : at + ref.shape[0]].astype(jnp.bfloat16)
@@ -313,7 +313,12 @@
         lax.ppermute(chosen[k], "x", [(i, (i + k) % NX) for i in range(NX)]) for k in range(1, NX)
     ]
     my_x = lax.dynamic_slice(owner_x, (x, z, core, 0), (1, 1, 1, REQ)).reshape(REQ)
-    (rows,) = choose_call((x - my_x) % NX * REQ + jnp.arange(REQ), arrived)
+    step = ((x - my_x) % NX)[:, None, None]
+    rows = jnp.where(
+        step < 2,
+        jnp.where(step == 0, arrived[0], arrived[1]),
+        jnp.where(step == 2, arrived[2], arrived[3]),
+    )
     rows, qg = lax.optimization_barrier((rows, qg))
     rows = lax.all_to_all(rows, "mp", split_axis=0, concat_axis=0, tiled=True)
     rows = rows.reshape(2 * STRETCH, WIDTH)

time: 179 us -> 178 us (level)
  transfers between devices with their start and end apart: 17 -> 17, of which waited for: 12 -> 11; matrix products, arithmetic and copies ran while one was open for 3% -> 3% of each run, Pallas kernels for 2% -> 2%
where the time goes in v6:
time: 178 us; the launch traced here: 177 us
  starting transfers between devices  74.4 us (42%)
  blocking collectives  36.8 us (21%)
  waiting for transfers between devices  26.4 us (15%)
  Pallas kernels  15.9 us (9%)
  between operations  14.5 us (8%)
  local copies, waits for them, and re-layouts  4.85 us (3%)
  other arithmetic  4.12 us (2%)
    ppermute x8, starting transfers between devices, along_z(): return lax.ppermute(values, ('z', 'core'), pairs)  36.5 us
    all_gather x1, blocking collectives, shards(): every = lax.all_gather(grad_rows, 'x', axis=0, tiled=True)  13.5 us
    pallas_call x1, Pallas kernels, stretch_call(): pl.pallas_call(stretch_kernel, out_shape=(jax.ShapeDtypeStruct((NM, 2 * S...  12.9 us
    all_to_all x1, blocking collectives, shards(): lax.all_to_all(grad_rows, 'mp', split_axis=0, concat_axis=0, tiled=True)  11.6 us
    ppermute x3, starting transfers between devices, shards(): lax.ppermute(chosen[k], 'x', [(i, (i + k) % NX) for i in range(NX)])  10.7 us
    all_gather x4, blocking collectives, shards(): lax.all_gather(part, 'core', axis=0, tiled=True)  9.75 us
    ppermute x1, starting transfers between devices, shards(): beside = lax.ppermute(pool, 'core', swap)  8.79 us
    all_to_all x1, waiting for transfers between devices, shards(): rows = lax.all_to_all(rows, 'mp', split_axis=0, concat_axis=0, tiled=True)  8.35 us
  transfers between devices with their start and end apart: 17, of which 11 were waited for; matrix products, arithmetic and copies ran while one was open for 3% of the time, Pallas kernels for 2%

profile of v6, /device:TPU:1, one launch (start us, length us, event | category | flops | bytes accessed | tf_op | source)
XLA Modules:
  0.0 176.9 jit_solution(16653315689120570121)
XLA Ops:
  9.7 8.8 %collective-permute-start = (bf16[8,8,896]{2,1,0:T(8,128)(2,1)S(1)}, bf16[8,8,896]{2,1,0:T(8,128)(2,1)S(1)}, u32[]{:S(2)}, u32[]{:S(2)}) collective-permute-start(bf16[8,8,896]{2,1,0:T(8,128)(2,1)S(1)} %copy-done.1), channel_id=1, source_target_pairs={{0,8},{8,0},{1,9},{9,1},{2,10},{10,2},{3,11},{11,3},{4,12},{12,4},... | collective-permute-start | bytes 344072 | tf_op jit(solution)/shard_map/ppermute | solution.py:304
  19.4 3.5 %all-to-all-start = ((bf16[8,128,256]{2,1,0:T(8,128)(2,1)}), bf16[8,128,256]{2,1,0:T(8,128)(2,1)S(1)}, u32[]{:S(2)}, u32[]{:S(2)}) async-start(bf16[8,128,256]{2,1,0:T(8,128)(2,1)} %pad_maximum_fusion.1), calls=%async_computation | async-start | bytes 1048576 | tf_op jit(solution)/shard_map/all_to_all | solution.py:277
  24.2 8.6 %collective-permute-start.3 = (bf16[16,8,896]{2,1,0:T(8,128)(2,1)S(1)}, bf16[16,8,896]{2,1,0:T(8,128)(2,1)S(1)}, u32[]{:S(2)}, u32[]{:S(2)}) collective-permute-start(bf16[16,8,896]{2,1,0:T(8,128)(2,1)S(1)} %join.1.refs_0_), channel_id=1, source_target_pairs={{0,48},{8,88},{16,64},{24,104},{32,80},{40,120},{48,96},{56,8},{64... | collective-permute-start | bytes 688136 | tf_op jit(solution)/shard_map/ppermute | solution.py:261
  34.7 7.3 %collective-permute-start.2 = (bf16[16,8,896]{2,1,0:T(8,128)(2,1)S(1)}, bf16[16,8,896]{2,1,0:T(8,128)(2,1)S(1)}, u32[]{:S(2)}, u32[]{:S(2)}) collective-permute-start(bf16[16,8,896]{2,1,0:T(8,128)(2,1)S(1)} %join.1.refs_0_), channel_id=1, source_target_pairs={{0,32},{8,104},{16,48},{24,120},{32,64},{40,8},{48,80},{56,24},{64... | collective-permute-start | bytes 688136 | tf_op jit(solution)/shard_map/ppermute | solution.py:261
  42.7 2.2 %collective-permute-start.1 = (bf16[16,8,896]{2,1,0:T(8,128)(2,1)S(1)}, bf16[16,8,896]{2,1,0:T(8,128)(2,1)S(1)}, u32[]{:S(2)}, u32[]{:S(2)}) collective-permute-start(bf16[16,8,896]{2,1,0:T(8,128)(2,1)S(1)} %join.1.refs_0_), channel_id=1, source_target_pairs={{0,16},{8,120},{16,32},{24,8},{32,48},{40,24},{48,64},{56,40},{64,... | collective-permute-start | bytes 688136 | tf_op jit(solution)/shard_map/ppermute | solution.py:261
  45.7 2.1 %all_gather.36.refs_4_ = bf16[16,8,896]{2,1,0:T(8,128)(2,1)S(1)} all-gather(bf16[8,8,896]{2,1,0:T(8,128)(2,1)S(1)} %collective-permute-done.4), channel_id=1, replica_groups=mesh['x'=4,'z'=8,'core'=2,'mp'=8] {'core'}, dimensions={0}, use_global_device_ids=true | all-gather | bytes 344064 | tf_op jit(solution)/shard_map/all_gather | solution.py:308
  47.9 2.1 %all_gather.35.refs_3_ = bf16[32,8,896]{2,1,0:T(8,128)(2,1)S(1)} all-gather(bf16[16,8,896]{2,1,0:T(8,128)(2,1)S(1)} %collective-permute-done.3), channel_id=1, replica_groups=mesh['x'=4,'z'=8,'core'=2,'mp'=8] {'core'}, dimensions={0}, use_global_device_ids=true | all-gather | bytes 688128 | tf_op jit(solution)/shard_map/all_gather | solution.py:308
  50.5 2.1 %all_gather.34.refs_2_ = bf16[32,8,896]{2,1,0:T(8,128)(2,1)S(1)} all-gather(bf16[16,8,896]{2,1,0:T(8,128)(2,1)S(1)} %collective-permute-done.2), channel_id=1, replica_groups=mesh['x'=4,'z'=8,'core'=2,'mp'=8] {'core'}, dimensions={0}, use_global_device_ids=true | all-gather | bytes 688128 | tf_op jit(solution)/shard_map/all_gather | solution.py:308
  52.9 3.5 %all_gather.33.refs_1_ = bf16[32,8,896]{2,1,0:T(8,128)(2,1)S(1)} all-gather(bf16[16,8,896]{2,1,0:T(8,128)(2,1)S(1)} %collective-permute-done.1), channel_id=1, replica_groups=mesh['x'=4,'z'=8,'core'=2,'mp'=8] {'core'}, dimensions={0}, use_global_device_ids=true | all-gather | bytes 688128 | tf_op jit(solution)/shard_map/all_gather | solution.py:308
  57.2 3.2 %collective-permute-start.5 = (bf16[16,8,896]{2,1,0:T(8,128)(2,1)S(1)}, bf16[16,8,896]{2,1,0:T(8,128)(2,1)S(1)}, u32[]{:S(2)}, u32[]{:S(2)}) collective-permute-start(bf16[16,8,896]{2,1,0:T(8,128)(2,1)S(1)} %get-tuple-element.26), channel_id=1, source_target_pairs={{0,128},{128,256},{256,384},{384,0},{1,129},{129,257},{257,385},{3... | collective-permute-start | bytes 688136 | tf_op jit(solution)/shard_map/ppermute | solution.py:313
  60.4 4.4 %collective-permute-start.6 = (bf16[16,8,896]{2,1,0:T(8,128)(2,1)S(1)}, bf16[16,8,896]{2,1,0:T(8,128)(2,1)S(1)}, u32[]{:S(2)}, u32[]{:S(2)}) collective-permute-start(bf16[16,8,896]{2,1,0:T(8,128)(2,1)S(1)} %get-tuple-element.27), channel_id=1, source_target_pairs={{0,256},{128,384},{256,0},{384,128},{1,257},{129,385},{257,1},{385... | collective-permute-start | bytes 688136 | tf_op jit(solution)/shard_map/ppermute | solution.py:313
  64.8 3.1 %collective-permute-start.7 = (bf16[16,8,896]{2,1,0:T(8,128)(2,1)S(1)}, bf16[16,8,896]{2,1,0:T(8,128)(2,1)S(1)}, u32[]{:S(2)}, u32[]{:S(2)}) collective-permute-start(bf16[16,8,896]{2,1,0:T(8,128)(2,1)S(1)} %get-tuple-element.28), channel_id=1, source_target_pairs={{0,384},{128,0},{256,128},{384,256},{1,385},{129,1},{257,129},{385... | collective-permute-start | bytes 688136 | tf_op jit(solution)/shard_map/ppermute | solution.py:313
  67.9 5.2 %collective-permute-done.6 = bf16[16,8,896]{2,1,0:T(8,128)(2,1)S(1)} collective-permute-done((bf16[16,8,896]{2,1,0:T(8,128)(2,1)S(1)}, bf16[16,8,896]{2,1,0:T(8,128)(2,1)S(1)}, u32[]{:S(2)}, u32[]{:S(2)}) %collective-permute-start.6) | collective-permute-done | bytes 229408 | tf_op jit(solution)/shard_map/ppermute | solution.py:313
  75.3 7.0 %all-to-all-start.1 = ((bf16[16,8,896]{2,1,0:T(8,128)(2,1)}), bf16[16,8,896]{2,1,0:T(8,128)(2,1)S(1)}, u32[]{:S(2)}, u32[]{:S(2)}) async-start(bf16[16,8,896]{2,1,0:T(8,128)(2,1)} %select_select_fusion), calls=%async_computation.1 | async-start | bytes 458752 | tf_op jit(solution)/shard_map/all_to_all | solution.py:323
  83.1 8.4 %all-to-all-done.1 = bf16[16,8,896]{2,1,0:T(8,128)(2,1)S(1)} async-done(((bf16[16,8,896]{2,1,0:T(8,128)(2,1)}), bf16[16,8,896]{2,1,0:T(8,128)(2,1)S(1)}, u32[]{:S(2)}, u32[]{:S(2)}) %all-to-all-start.1) | async-done | bytes 229408 | tf_op jit(solution)/shard_map/all_to_all | solution.py:323
  91.5 12.9 %stretch.1 = (bf16[8,128,256]{2,1,0:T(8,128)(2,1)}, bf16[128,896]{1,0:T(8,128)(2,1)S(1)}) custom-call(bf16[128,896]{1,0:T(8,128)(2,1)S(1)} %bitcast.27, bf16[64,1792]{1,0:T(8,128)(2,1)S(1)} %copy-done.2, bf16[8,128,256]{2,1,0:T(8,128)(2,1)S(1)} %all-to-all-done.qg_ref, bf16[16,1120,256]{2,1,0:T(8,128)(2,1)} %bitcast.38), custom_call_target="tpu_custom_call" | custom-call | flops 7000000000 | bytes 11000000 | tf_op jit(solution)/shard_map/stretch/pallas_call | solution.py:146
  104.4 11.6 %all_to_all.15 = bf16[16,8,896]{2,1,0:T(8,128)(2,1)S(1)} all-to-all(bf16[16,8,896]{2,1,0:T(8,128)(2,1)S(1)} %bitcast.28), channel_id=1, replica_groups=mesh['x'=4,'z'=8,'core'=2,'mp'=8] {'mp'}, dimensions={0} | all-to-all | bytes 458752 | tf_op jit(solution)/shard_map/all_to_all | solution.py:330
  116.0 13.5 %all_gather.39.mine_ref = bf16[64,8,896]{2,1,0:T(8,128)(2,1)S(1)} all-gather(bf16[16,8,896]{2,1,0:T(8,128)(2,1)S(1)} %all_to_all.15), channel_id=1, replica_groups=mesh['x'=4,'z'=8,'core'=2,'mp'=8] {'x'}, dimensions={0}, use_global_device_ids=true | all-gather | bytes 1146880 | tf_op jit(solution)/shard_map/all_gather | solution.py:331
  129.5 7.8 %collective-permute-start.8 = (bf16[64,8,896]{2,1,0:T(8,128)(2,1)S(1)}, bf16[64,8,896]{2,1,0:T(8,128)(2,1)S(1)}, u32[]{:S(2)}, u32[]{:S(2)}) collective-permute-start(bf16[64,8,896]{2,1,0:T(8,128)(2,1)S(1)} %all_gather.39.mine_ref), channel_id=1, source_target_pairs={{0,8},{8,0},{1,9},{9,1},{2,10},{10,2},{3,11},{11,3},{4,12},{12,4},... | collective-permute-start | bytes 2752520 | tf_op jit(solution)/shard_map/ppermute | solution.py:332
  139.4 2.2 %place.1 = (bf16[8,8,896]{2,1,0:T(8,128)(2,1)S(1)}, bf16[16,8,896]{2,1,0:T(8,128)(2,1)S(1)}, bf16[16,8,896]{2,1,0:T(8,128)(2,1)S(1)}, bf16[16,8,896]{2,1,0:T(8,128)(2,1)S(1)}, bf16[8,8,896]{2,1,0:T(8,128)(2,1)}) custom-call(s32[2,64]{1,0:T(2,128)S(1)} %pad_add_fusion.place_ref, bf16[64,8,896]{2,1,0:T(8,128)(2,1)S(1)} %all_gather.39.mine_ref, ...), custom_call_target="tpu_custom_call" | custom-call | flops 1000000 | bytes 3000000 | tf_op jit(solution)/shard_map/place/pallas_call | solution.py:221
  141.5 6.7 %collective-permute-start.12 = (bf16[8,8,896]{2,1,0:T(8,128)(2,1)}, bf16[8,8,896]{2,1,0:T(8,128)(2,1)S(1)}, u32[]{:S(2)}, u32[]{:S(2)}) collective-permute-start(bf16[8,8,896]{2,1,0:T(8,128)(2,1)} %get-tuple-element.36), channel_id=1, source_target_pairs={{0,64},{8,72},{16,80},{24,88},{32,96},{40,104},{48,112},{56,120},{... | collective-permute-start | bytes 344072 | tf_op jit(solution)/shard_map/ppermute | solution.py:261
  150.1 2.6 %collective-permute-start.10 = (bf16[16,8,896]{2,1,0:T(8,128)(2,1)S(1)}, bf16[16,8,896]{2,1,0:T(8,128)(2,1)S(1)}, u32[]{:S(2)}, u32[]{:S(2)}) collective-permute-start(bf16[16,8,896]{2,1,0:T(8,128)(2,1)S(1)} %get-tuple-element.34), channel_id=1, source_target_pairs={{0,32},{8,104},{16,48},{24,120},{32,64},{40,8},{48,80},{56,24},{64... | collective-permute-start | bytes 688136 | tf_op jit(solution)/shard_map/ppermute | solution.py:261
  152.8 5.3 %collective-permute-start.11 = (bf16[16,8,896]{2,1,0:T(8,128)(2,1)S(1)}, bf16[16,8,896]{2,1,0:T(8,128)(2,1)S(1)}, u32[]{:S(2)}, u32[]{:S(2)}) collective-permute-start(bf16[16,8,896]{2,1,0:T(8,128)(2,1)S(1)} %get-tuple-element.35), channel_id=1, source_target_pairs={{0,48},{8,88},{16,64},{24,104},{32,80},{40,120},{48,96},{56,8},{64... | collective-permute-start | bytes 688136 | tf_op jit(solution)/shard_map/ppermute | solution.py:261
  161.7 5.5 %collective-permute-done.10 = bf16[16,8,896]{2,1,0:T(8,128)(2,1)S(1)} collective-permute-done((bf16[16,8,896]{2,1,0:T(8,128)(2,1)S(1)}, bf16[16,8,896]{2,1,0:T(8,128)(2,1)S(1)}, u32[]{:S(2)}, u32[]{:S(2)}) %collective-permute-start.10) | collective-permute-done | bytes 229408 | tf_op jit(solution)/shard_map/ppermute | solution.py:261
  (69 shorter events, 23.1 us)
Async XLA Ops:
  7.2 1.2 copy-start
  7.2 1.6 copy-start.5
  7.2 75.9 %all-gather.6.cloned.1.call-start = ((), (), s32[]{:S(2)}) async-start(), calls=%async_computation.3 | async-start | bytes 9748480 | tf_op jit(solution)/shard_map/all_gather | solution.py:272
  8.8 9.8 %copy-start.3 = (bf16[512,256]{1,0:T(8,128)(2,1)S(1)}, bf16[512,256]{1,0:T(8,128)(2,1)}, u32[]{:S(2)}) copy-start(bf16[512,256]{1,0:T(8,128)(2,1)} %param.15) | copy-start | bytes 786436
  8.8 9.8 %copy-start.4 = (bf16[512,256]{1,0:T(8,128)(2,1)S(1)}, bf16[512,256]{1,0:T(8,128)(2,1)}, u32[]{:S(2)}) copy-start(bf16[512,256]{1,0:T(8,128)(2,1)} %param.8) | copy-start | bytes 786436
  9.7 13.2 %copy-start.6 = (s32[512,2]{0,1:T(2,128)S(1)}, s32[512,2]{0,1:T(2,128)}, u32[]{:S(2)}) copy-start(s32[512,2]{0,1:T(2,128)} %param.11) | copy-start | bytes 12292
  9.7 14.4 %collective-permute-start = (bf16[8,8,896]{2,1,0:T(8,128)(2,1)S(1)}, bf16[8,8,896]{2,1,0:T(8,128)(2,1)S(1)}, u32[]{:S(2)}, u32[]{:S(2)}) collective-permute-start(bf16[8,8,896]{2,1,0:T(8,128)(2,1)S(1)} %copy-done.1), channel_id=1, source_target_pairs={{0,8},{8,0},{1,9},{9,1},{2,10},{10,2},{3,11},{11,3},{4,12},{12,4},... | collective-permute-start | bytes 344072 | tf_op jit(solution)/shard_map/ppermute | solution.py:304
  18.5 4.7 %copy-start.7 = (s32[512,2]{0,1:T(2,128)S(1)}, s32[512,2]{0,1:T(2,128)}, u32[]{:S(2)}) copy-start(s32[512,2]{0,1:T(2,128)} %param.12) | copy-start | bytes 12292
  19.4 55.9 %all-to-all-start = ((bf16[8,128,256]{2,1,0:T(8,128)(2,1)}), bf16[8,128,256]{2,1,0:T(8,128)(2,1)S(1)}, u32[]{:S(2)}, u32[]{:S(2)}) async-start(bf16[8,128,256]{2,1,0:T(8,128)(2,1)} %pad_maximum_fusion.1), calls=%async_computation | async-start | bytes 1048576 | tf_op jit(solution)/shard_map/all_to_all | solution.py:277
  24.2 23.7 %collective-permute-start.3 = (bf16[16,8,896]{2,1,0:T(8,128)(2,1)S(1)}, bf16[16,8,896]{2,1,0:T(8,128)(2,1)S(1)}, u32[]{:S(2)}, u32[]{:S(2)}) collective-permute-start(bf16[16,8,896]{2,1,0:T(8,128)(2,1)S(1)} %join.1.refs_0_), channel_id=1, source_target_pairs={{0,48},{8,88},{16,64},{24,104},{32,80},{40,120},{48,96},{56,8},{64... | collective-permute-start | bytes 688136 | tf_op jit(solution)/shard_map/ppermute | solution.py:261
  32.8 12.9 %collective-permute-start.4 = (bf16[8,8,896]{2,1,0:T(8,128)(2,1)S(1)}, bf16[8,8,896]{2,1,0:T(8,128)(2,1)S(1)}, u32[]{:S(2)}, u32[]{:S(2)}) collective-permute-start(bf16[8,8,896]{2,1,0:T(8,128)(2,1)S(1)} %copy-done.1), channel_id=1, source_target_pairs={{0,64},{8,72},{16,80},{24,88},{32,96},{40,104},{48,112},{56,120},{... | collective-permute-start | bytes 344072 | tf_op jit(solution)/shard_map/ppermute | solution.py:261
  34.7 15.7 %collective-permute-start.2 = (bf16[16,8,896]{2,1,0:T(8,128)(2,1)S(1)}, bf16[16,8,896]{2,1,0:T(8,128)(2,1)S(1)}, u32[]{:S(2)}, u32[]{:S(2)}) collective-permute-start(bf16[16,8,896]{2,1,0:T(8,128)(2,1)S(1)} %join.1.refs_0_), channel_id=1, source_target_pairs={{0,32},{8,104},{16,48},{24,120},{32,64},{40,8},{48,80},{56,24},{64... | collective-permute-start | bytes 688136 | tf_op jit(solution)/shard_map/ppermute | solution.py:261
  42.7 10.2 %collective-permute-start.1 = (bf16[16,8,896]{2,1,0:T(8,128)(2,1)S(1)}, bf16[16,8,896]{2,1,0:T(8,128)(2,1)S(1)}, u32[]{:S(2)}, u32[]{:S(2)}) collective-permute-start(bf16[16,8,896]{2,1,0:T(8,128)(2,1)S(1)} %join.1.refs_0_), channel_id=1, source_target_pairs={{0,16},{8,120},{16,32},{24,8},{32,48},{40,24},{48,64},{56,40},{64,... | collective-permute-start | bytes 688136 | tf_op jit(solution)/shard_map/ppermute | solution.py:261
  57.2 34.3 %copy-start.2 = (bf16[64,1792]{1,0:T(8,128)(2,1)S(1)}, bf16[64,1792]{1,0:T(8,128)(2,1)}, u32[]{:S(2)}) copy-start(bf16[64,1792]{1,0:T(8,128)(2,1)} %kv_ref.1) | copy-start | bytes 688132
  57.2 10.7 %collective-permute-start.5 = (bf16[16,8,896]{2,1,0:T(8,128)(2,1)S(1)}, bf16[16,8,896]{2,1,0:T(8,128)(2,1)S(1)}, u32[]{:S(2)}, u32[]{:S(2)}) collective-permute-start(bf16[16,8,896]{2,1,0:T(8,128)(2,1)S(1)} %get-tuple-element.26), channel_id=1, source_target_pairs={{0,128},{128,256},{256,384},{384,0},{1,129},{129,257},{257,385},{3... | collective-permute-start | bytes 688136 | tf_op jit(solution)/shard_map/ppermute | solution.py:313
  60.4 12.7 %collective-permute-start.6 = (bf16[16,8,896]{2,1,0:T(8,128)(2,1)S(1)}, bf16[16,8,896]{2,1,0:T(8,128)(2,1)S(1)}, u32[]{:S(2)}, u32[]{:S(2)}) collective-permute-start(bf16[16,8,896]{2,1,0:T(8,128)(2,1)S(1)} %get-tuple-element.27), channel_id=1, source_target_pairs={{0,256},{128,384},{256,0},{384,128},{1,257},{129,385},{257,1},{385... | collective-permute-start | bytes 688136 | tf_op jit(solution)/shard_map/ppermute | solution.py:313
  64.8 9.6 %collective-permute-start.7 = (bf16[16,8,896]{2,1,0:T(8,128)(2,1)S(1)}, bf16[16,8,896]{2,1,0:T(8,128)(2,1)S(1)}, u32[]{:S(2)}, u32[]{:S(2)}) collective-permute-start(bf16[16,8,896]{2,1,0:T(8,128)(2,1)S(1)} %get-tuple-element.28), channel_id=1, source_target_pairs={{0,384},{128,0},{256,128},{384,256},{1,385},{129,1},{257,129},{385... | collective-permute-start | bytes 688136 | tf_op jit(solution)/shard_map/ppermute | solution.py:313
  75.3 16.1 %all-to-all-start.1 = ((bf16[16,8,896]{2,1,0:T(8,128)(2,1)}), bf16[16,8,896]{2,1,0:T(8,128)(2,1)S(1)}, u32[]{:S(2)}, u32[]{:S(2)}) async-start(bf16[16,8,896]{2,1,0:T(8,128)(2,1)} %select_select_fusion), calls=%async_computation.1 | async-start | bytes 458752 | tf_op jit(solution)/shard_map/all_to_all | solution.py:323
  82.3 77.4 %all-gather.8.cloned.1.call-start = ((), (), s32[]{:S(2)}) async-start(), calls=%async_computation.4 | async-start | bytes 4718592 | tf_op jit(solution)/shard_map/all_gather | solution.py:336
  129.5 9.9 %collective-permute-start.8 = (bf16[64,8,896]{2,1,0:T(8,128)(2,1)S(1)}, bf16[64,8,896]{2,1,0:T(8,128)(2,1)S(1)}, u32[]{:S(2)}, u32[]{:S(2)}) collective-permute-start(bf16[64,8,896]{2,1,0:T(8,128)(2,1)S(1)} %all_gather.39.mine_ref), channel_id=1, source_target_pairs={{0,8},{8,0},{1,9},{9,1},{2,10},{10,2},{3,11},{11,3},{4,12},{12,4},... | collective-permute-start | bytes 2752520 | tf_op jit(solution)/shard_map/ppermute | solution.py:332
  141.5 20.1 %collective-permute-start.12 = (bf16[8,8,896]{2,1,0:T(8,128)(2,1)}, bf16[8,8,896]{2,1,0:T(8,128)(2,1)S(1)}, u32[]{:S(2)}, u32[]{:S(2)}) collective-permute-start(bf16[8,8,896]{2,1,0:T(8,128)(2,1)} %get-tuple-element.36), channel_id=1, source_target_pairs={{0,64},{8,72},{16,80},{24,88},{32,96},{40,104},{48,112},{56,120},{... | collective-permute-start | bytes 344072 | tf_op jit(solution)/shard_map/ppermute | solution.py:261
  148.2 13.4 %collective-permute-start.9 = (bf16[16,8,896]{2,1,0:T(8,128)(2,1)S(1)}, bf16[16,8,896]{2,1,0:T(8,128)(2,1)S(1)}, u32[]{:S(2)}, u32[]{:S(2)}) collective-permute-start(bf16[16,8,896]{2,1,0:T(8,128)(2,1)S(1)} %get-tuple-element.33), channel_id=1, source_target_pairs={{0,16},{8,120},{16,32},{24,8},{32,48},{40,24},{48,64},{56,40},{64,... | collective-permute-start | bytes 688136 | tf_op jit(solution)/shard_map/ppermute | solution.py:261
  150.1 17.0 %collective-permute-start.10 = (bf16[16,8,896]{2,1,0:T(8,128)(2,1)S(1)}, bf16[16,8,896]{2,1,0:T(8,128)(2,1)S(1)}, u32[]{:S(2)}, u32[]{:S(2)}) collective-permute-start(bf16[16,8,896]{2,1,0:T(8,128)(2,1)S(1)} %get-tuple-element.34), channel_id=1, source_target_pairs={{0,32},{8,104},{16,48},{24,120},{32,64},{40,8},{48,80},{56,24},{64... | collective-permute-start | bytes 688136 | tf_op jit(solution)/shard_map/ppermute | solution.py:261
  152.8 14.4 %collective-permute-start.11 = (bf16[16,8,896]{2,1,0:T(8,128)(2,1)S(1)}, bf16[16,8,896]{2,1,0:T(8,128)(2,1)S(1)}, u32[]{:S(2)}, u32[]{:S(2)}) collective-permute-start(bf16[16,8,896]{2,1,0:T(8,128)(2,1)S(1)} %get-tuple-element.35), channel_id=1, source_target_pairs={{0,48},{8,88},{16,64},{24,104},{32,80},{40,120},{48,96},{56,8},{64... | collective-permute-start | bytes 688136 | tf_op jit(solution)/shard_map/ppermute | solution.py:261
  (1 other events, 1.0 us)
Sparse Core Ops, SparseCore 0:
  10.1 72.9 all-gather.5
  104.5 55.1 all-gather.7
